TPU v7x, 32 devices: a whole 2x2x4 slice. The times are simulated.
32 devices in a mesh: groups: 2 (over x), dom: 16 (over z, y, core).
Axes of the slice: x: 2, y: 2, z: 4, core: 2. Of those that a mesh axis runs over, the one named last changes fastest.
Arguments:
- blocks: float32 [1280, 4, 128, 128], P(('groups', 'dom')), parts along dimension 0, may hold values from -0.25 to 0.25
- offsets: int32 [1280, 4], P(('groups', 'dom')), parts along dimension 0, may hold values from -2 to 2, as said below
- diag_shift: float32 [163840], P(('groups', 'dom')), parts along dimension 0, may hold values from 1.2 to 2
- right_side: float32 [4, 163840], P(None, ('groups', 'dom')), parts along dimension 1, may hold values from -6 to 6
Outputs:
- solution: float32 [4, 163840], P(None, ('groups', 'dom')), parts along dimension 1
- residual: float32 [4, 163840], P(None, ('groups', 'dom')), parts along dimension 1
There are 2 independent parts, one for each index of `groups`. A program takes and returns all parts, laid end to end along the dimension named above; each array names one. Nothing has to cross between parts.
Inputs may be any that keep to these rules, and one draw needn't show every extreme that they name: The first entry of each block row is 0, the diagonal block; the other 3 entries of a row are distinct nonzero offsets between -2 and 2.
All inputs are finite; a program needn't handle non-finite values.
Results may differ from a plain program's by a relative error of at most 0.0003.
Values sent between devices are 32-bit elements; how exact they have to be, the bound alone decides.
No kernel may reach another device: no remote copies, remote signals or barrier semaphores. Data moves between devices by JAX's collectives and lax.ppermute only.
A program may use at most 128 MiB of HBM per device.

v0:
```python
import math

import jax
import jax.numpy as jnp
from jax import lax
from jax.sharding import PartitionSpec as P

W = 2
S = 6
CYCLES = 2


center_value = 1.6
half_range = 0.8


def with_halo(block, sides, width):
    for axis, dim in sides:
        count = lax.axis_size(axis)
        forward = [(i, i + 1) for i in range(count - 1)]
        backward = [(target, source) for source, target in forward]
        low = lax.ppermute(
            lax.slice_in_dim(block, block.shape[dim] - width, None, axis=dim), axis, forward
        )
        high = lax.ppermute(lax.slice_in_dim(block, 0, width, axis=dim), axis, backward)
        block = jnp.concatenate([low, block, high], axis=dim)
    return block


def newton_shifts():
    places = jnp.arange(S, dtype=jnp.float32)
    return center_value + half_range * jnp.cos(math.pi * (2.0 * places + 1.0) / (2.0 * S))


def with_diagonal(blocks, diag_shift):
    block_count = blocks.shape[0]
    block_size = blocks.shape[2]
    ident_block = jnp.eye(block_size, dtype=jnp.float32)
    diag_blocks = diag_shift.reshape(block_count, block_size)
    first = blocks[:, 0] + diag_blocks[:, :, None] * ident_block[None]
    return jnp.concatenate([first[:, None], blocks[:, 1:]], axis=1)


def apply_rows(matrix, pattern, region, count_rows, shift_value):
    column_index = jnp.arange(count_rows, dtype=jnp.int32)[:, None] + W + pattern
    gathered = region[:, column_index, :]
    product = jnp.einsum("ikab,rikb->ria", matrix, gathered, precision=lax.Precision.HIGHEST)
    return product - shift_value * region[:, W : W + count_rows, :]


def basis_matrix(shift_values):
    steps_count = shift_values.shape[0]
    places = jnp.arange(steps_count)
    bmat = jnp.zeros((steps_count + 1, steps_count), jnp.float32)
    bmat = bmat.at[places, places].set(shift_values)
    return bmat.at[places + 1, places].set(1.0)


def small_solve(gram, bmat):
    normal = jnp.einsum("ia,rij,jb->rab", bmat, gram, bmat, precision=lax.Precision.HIGHEST)
    target = jnp.einsum("ia,ri->ra", bmat, gram[:, :, 0], precision=lax.Precision.HIGHEST)
    lower = jnp.linalg.cholesky(normal)
    middle = lax.linalg.triangular_solve(lower, target[:, :, None], left_side=True, lower=True)
    coeffs = lax.linalg.triangular_solve(
        lower, middle, left_side=True, lower=True, transpose_a=True
    )[:, :, 0]
    unit = jnp.zeros((bmat.shape[0],), jnp.float32).at[0].set(1.0)
    combine = unit[None, :] - jnp.einsum("ja,ra->rj", bmat, coeffs, precision=lax.Precision.HIGHEST)
    return (coeffs, combine)


def local(blocks, offsets, diag_shift, right_side):
    rhs_count = right_side.shape[0]
    row_blocks = blocks.shape[0]
    block_size = blocks.shape[2]
    effective = with_diagonal(blocks, diag_shift)
    shift_values = newton_shifts()
    bmat = basis_matrix(shift_values)
    margin = (S - 1) * W
    ext_matrix = with_halo(effective, (("dom", 0),), margin)
    ext_pattern = with_halo(offsets, (("dom", 0),), margin)
    solution = jnp.zeros_like(right_side)
    residual = right_side
    for cycle in range(CYCLES):
        start_blocks = residual.reshape(rhs_count, row_blocks, block_size)
        vectors = [start_blocks]
        region = with_halo(start_blocks, (("dom", 1),), S * W)
        for step in range(S):
            keep = (S - 1 - step) * W
            count_rows = row_blocks + 2 * keep
            start_row = margin - keep
            region = apply_rows(
                ext_matrix[start_row : start_row + count_rows],
                ext_pattern[start_row : start_row + count_rows],
                region,
                count_rows,
                shift_values[step],
            )
            vectors.append(region[:, keep : keep + row_blocks])
        basis = jnp.stack(vectors, 1).reshape(rhs_count, S + 1, row_blocks * block_size)
        local_gram = jnp.einsum("rin,rjn->rij", basis, basis, precision=lax.Precision.HIGHEST)
        gram = lax.psum(local_gram, "dom")
        coeffs, combine = small_solve(gram, bmat)
        solution = solution + jnp.einsum(
            "rj,rjn->rn", coeffs, basis[:, :S], precision=lax.Precision.HIGHEST
        )
        residual = jnp.einsum("rj,rjn->rn", combine, basis, precision=lax.Precision.HIGHEST)
    return (solution, residual)


def solution(mesh):
    in_specs = (
        P(("groups", "dom"), None, None, None),
        P(("groups", "dom"), None),
        P(("groups", "dom")),
        P(None, ("groups", "dom")),
    )
    out_specs = (P(None, ("groups", "dom")), P(None, ("groups", "dom")))
    return jax.shard_map(local, mesh=mesh, in_specs=in_specs, out_specs=out_specs, check_vma=False)
```

profile of v0, /device:TPU:0, one launch (start us, length us, event | category | flops | bytes accessed | tf_op | source)
XLA Modules:
  0.0 426.0 jit_solution(9099849331423662296)
XLA Ops:
  0.7 3.8 slice.185
  4.5 4.3 %multiply_add_fusion = f32[40,1,128,128]{3,2,1,0:T(8,128)S(1)} fusion(f32[40,4,128,128]{3,2,1,0:T(8,128)} %param.13, f32[128,128]{1,0:T(8,128)S(1)} %fusion.70, f32[40,128]{1,0:T(8,128)S(1)} %bitcast.318), kind=kLoop, calls=%fused_computation.36 | loop fusion | flops 1310720 | bytes 5328896 | tf_op jit(solution)/shard_map/add | solution.py:40
  8.8 2.8 pad_maximum_fusion.5
  11.6 3.8 collective-permute-start.4
  15.4 1.3 collective-permute-start.5
  16.7 3.7 collective-permute-start
  20.6 3.6 collective-permute-start.2
  24.2 1.3 collective-permute-start.3
  25.9 0.8 scatter_fusion
  27.4 0.8 scatter_fusion.1
  28.2 1.3 collective-permute-start.1
  31.1 45.5 %collective-permute-done.1 = f32[4,12,128]{2,0,1:T(4,128)S(1)} collective-permute-done((f32[4,12,128]{2,0,1:T(4,128)S(1)}, f32[4,12,128]{2,0,1:T(4,128)S(1)}, u32[]{:S(2)}, u32[]{:S(2)}) %collective-permute-start.1) | collective-permute-done | bytes 24608 | tf_op jit(solution)/shard_map/ppermute | solution.py:25
  76.7 1.7 gather_fusion
  78.4 15.9 %fusion.19 = f32[4,60,128]{2,0,1:T(4,128)S(1)} fusion(f32[4,60,4,128]{3,0,2,1:T(4,128)} %bitcast.314, f32[4,64,128]{2,0,1:T(4,128)S(1)} %pad_maximum_fusion.10, f32[]{:T(128)} %bitcast.10, f32[10,4,128,128]{3,2,1,0:T(8,128)} %collective-permute-done.5, f32[40,3,128,128]{3,2,1,0:T(8,128)} %copy-done.1, f32[40,1,128,128]{3,2,1,0:T(8,128)S(1)} %multiply_add_fusion, ...), kind=kOutput, calls=%fused_computation.40 | convolution fusion | flops 200601600 | bytes 16465924 | tf_op jit(solution)/shard_map/ikab,rikb->ria/dot_general | solution.py:47
  95.0 0.9 gather_fusion.1
  95.9 6.0 %pad_maximum_fusion = f32[60,4,128,128]{3,2,1,0:T(8,128)S(1)} fusion(f32[10,4,128,128]{3,2,1,0:T(8,128)} %collective-permute-done.5, f32[40,3,128,128]{3,2,1,0:T(8,128)} %copy-done.1, f32[40,1,128,128]{3,2,1,0:T(8,128)S(1)} %multiply_add_fusion, f32[10,4,128,128]{3,2,1,0:T(8,128)} %collective-permute-done.4), kind=kLoop, calls=%fused_computation.14 | loop fusion | flops 11796480 | bytes 31457280 | tf_op jit(solution)/shard_map/concatenate | solution.py:26
  101.9 5.5 %copy-done = f32[60,4,128,128]{3,2,1,0:T(8,128)} copy-done((f32[60,4,128,128]{3,2,1,0:T(8,128)}, f32[60,4,128,128]{3,2,1,0:T(8,128)S(1)}, u32[]{:S(2)}) %copy-start) | copy-done | bytes 15728664
  107.4 12.8 %fusion.49 = f32[4,56,128]{2,0,1:T(4,128)S(1)} fusion(f32[4,56,4,128]{3,0,2,1:T(4,128)S(1)} %bitcast.299, f32[60,4,128,128]{3,2,1,0:T(8,128)S(1)} %pad_maximum_fusion, f32[4,60,128]{2,0,1:T(4,128)S(1)} %fusion.19, f32[]{:T(128)} %bitcast.17), kind=kOutput, calls=%fused_computation.52 | convolution fusion | flops 176218112 | bytes 15368196 | tf_op jit(solution)/shard_map/ikab,rikb->ria/dot_general | solution.py:47
  120.1 0.7 slice_bitcast_fusion.6
  120.8 0.9 gather_fusion.2
  121.7 15.0 %fusion.55 = f32[4,52,128]{2,0,1:T(4,128)S(1)} fusion(f32[4,52,4,128]{3,0,2,1:T(4,128)S(1)} %bitcast.302, f32[60,4,128,128]{3,2,1,0:T(8,128)} %copy-done, f32[4,56,128]{2,0,1:T(4,128)S(1)} %fusion.49, f32[]{:T(128)} %bitcast.24), kind=kOutput, calls=%fused_computation.54 | convolution fusion | flops 163631104 | bytes 14270976 | tf_op jit(solution)/shard_map/ikab,rikb->ria/dot_general | solution.py:47
  137.3 0.9 gather_fusion.3
  138.2 13.3 %fusion.61 = f32[4,48,128]{2,0,1:T(4,128)S(1)} fusion(f32[4,48,4,128]{3,0,2,1:T(4,128)S(1)} %bitcast.304, f32[60,4,128,128]{3,2,1,0:T(8,128)} %copy-done, f32[4,52,128]{2,0,1:T(4,128)S(1)} %fusion.55, f32[]{:T(128)} %bitcast.31), kind=kOutput, calls=%fused_computation.56 | convolution fusion | flops 151044096 | bytes 13173248 | tf_op jit(solution)/shard_map/ikab,rikb->ria/dot_general | solution.py:47
  152.2 0.8 gather_fusion.4
  153.1 13.2 %fusion.67 = f32[4,44,128]{2,0,1:T(4,128)S(1)} fusion(f32[4,44,4,128]{3,0,2,1:T(4,128)S(1)} %bitcast.306, f32[60,4,128,128]{3,2,1,0:T(8,128)} %copy-done, f32[4,48,128]{2,0,1:T(4,128)S(1)} %fusion.61, f32[]{:T(128)} %bitcast.38), kind=kOutput, calls=%fused_computation.58 | convolution fusion | flops 138457088 | bytes 12075520 | tf_op jit(solution)/shard_map/ikab,rikb->ria/dot_general | solution.py:47
  167.0 0.8 gather_fusion.5
  167.8 11.5 %subtract_bitcast_fusion.1 = f32[4,1,5120]{2,0,1:T(4,128)S(1)} fusion(f32[4,44,128]{2,0,1:T(4,128)S(1)} %fusion.67, f32[]{:T(128)} %bitcast.45, f32[4,40,4,128]{3,0,2,1:T(4,128)S(1)} %bitcast.308, f32[40,3,128,128]{3,2,1,0:T(8,128)} %copy-done.1, f32[40,1,128,128]{3,2,1,0:T(8,128)S(1)} %multiply_add_fusion), kind=kOutput, calls=%fused_computation.86 | convolution fusion | flops 128491520 | bytes 10977284 | tf_op jit(solution)/shard_map/ikab,rikb->ria/dot_general | solution.py:47
  179.3 0.7 copy.53
  180.1 1.0 copy.51
  181.1 1.0 copy.50
  182.2 1.0 copy.49
  184.4 1.9 stack.58
  186.3 2.3 stack.57
  188.6 1.4 fusion.103
  190.0 60.8 %psum.14 = f32[4,7,7]{2,1,0:T(8,128)S(1)} all-reduce(f32[4,7,7]{2,1,0:T(8,128)S(1)} %fusion.103), channel_id=1, replica_groups=mesh['groups'=2,'dom'=16] {'dom'}, use_global_device_ids=true, to_apply=%region_0.0 | all-reduce | flops 196 | bytes 1568 | tf_op jit(solution)/shard_map/psum | solution.py:102
  251.4 2.2 custom-call.16
  253.9 1.9 custom-call.18
  256.4 0.7 fusion.105
  257.1 1.3 collective-permute-start.6
  258.4 1.5 collective-permute-start.7
  259.9 2.4 fusion.89
  262.3 0.7 stack.59
  263.0 1.7 gather_fusion.6
  264.8 15.9 %fusion.18 = f32[4,60,128]{2,0,1:T(4,128)S(1)} fusion(f32[4,60,4,128]{3,0,2,1:T(4,128)} %bitcast.315, f32[4,64,128]{2,0,1:T(4,128)S(1)} %pad_maximum_fusion.11, f32[]{:T(128)} %bitcast.10, f32[10,4,128,128]{3,2,1,0:T(8,128)} %collective-permute-done.5, f32[40,3,128,128]{3,2,1,0:T(8,128)} %copy-done.1, f32[40,1,128,128]{3,2,1,0:T(8,128)S(1)} %multiply_add_fusion, ...), kind=kOutput, calls=%fused_computation.38 | convolution fusion | flops 200601600 | bytes 16465924 | tf_op jit(solution)/shard_map/ikab,rikb->ria/dot_general | solution.py:47
  280.7 0.9 gather_fusion.7
  281.6 15.7 %fusion.46 = f32[4,56,128]{2,0,1:T(4,128)S(1)} fusion(f32[4,56,4,128]{3,0,2,1:T(4,128)S(1)} %bitcast.300, f32[60,4,128,128]{3,2,1,0:T(8,128)} %copy-done, f32[4,60,128]{2,0,1:T(4,128)S(1)} %fusion.18, f32[]{:T(128)} %bitcast.17), kind=kOutput, calls=%fused_computation.51 | convolution fusion | flops 176218112 | bytes 15368704 | tf_op jit(solution)/shard_map/ikab,rikb->ria/dot_general | solution.py:47
  297.4 0.9 gather_fusion.8
  298.3 15.0 %fusion.52 = f32[4,52,128]{2,0,1:T(4,128)S(1)} fusion(f32[4,52,4,128]{3,0,2,1:T(4,128)S(1)} %bitcast.301, f32[60,4,128,128]{3,2,1,0:T(8,128)} %copy-done, f32[4,56,128]{2,0,1:T(4,128)S(1)} %fusion.46, f32[]{:T(128)} %bitcast.24), kind=kOutput, calls=%fused_computation.53 | convolution fusion | flops 163631104 | bytes 14270976 | tf_op jit(solution)/shard_map/ikab,rikb->ria/dot_general | solution.py:47
  313.3 1.0 gather_fusion.9
  314.3 13.3 %fusion.58 = f32[4,48,128]{2,0,1:T(4,128)S(1)} fusion(f32[4,48,4,128]{3,0,2,1:T(4,128)S(1)} %bitcast.303, f32[60,4,128,128]{3,2,1,0:T(8,128)} %copy-done, f32[4,52,128]{2,0,1:T(4,128)S(1)} %fusion.52, f32[]{:T(128)} %bitcast.31), kind=kOutput, calls=%fused_computation.55 | convolution fusion | flops 151044096 | bytes 13173248 | tf_op jit(solution)/shard_map/ikab,rikb->ria/dot_general | solution.py:47
  327.6 0.9 gather_fusion.10
  328.5 13.1 %fusion.64 = f32[4,44,128]{2,0,1:T(4,128)S(1)} fusion(f32[4,44,4,128]{3,0,2,1:T(4,128)S(1)} %bitcast.305, f32[60,4,128,128]{3,2,1,0:T(8,128)} %copy-done, f32[4,48,128]{2,0,1:T(4,128)S(1)} %fusion.58, f32[]{:T(128)} %bitcast.38), kind=kOutput, calls=%fused_computation.57 | convolution fusion | flops 138457088 | bytes 12075520 | tf_op jit(solution)/shard_map/ikab,rikb->ria/dot_general | solution.py:47
  341.6 0.8 gather_fusion.11
  342.5 11.5 %subtract_bitcast_fusion = f32[4,1,5120]{2,0,1:T(4,128)S(1)} fusion(f32[4,44,128]{2,0,1:T(4,128)S(1)} %fusion.64, f32[]{:T(128)} %bitcast.45, f32[4,40,4,128]{3,0,2,1:T(4,128)S(1)} %bitcast.307, f32[40,3,128,128]{3,2,1,0:T(8,128)} %copy-done.1, f32[40,1,128,128]{3,2,1,0:T(8,128)S(1)} %multiply_add_fusion), kind=kOutput, calls=%fused_computation.85 | convolution fusion | flops 128491520 | bytes 10977284 | tf_op jit(solution)/shard_map/ikab,rikb->ria/dot_general | solution.py:47
  354.6 0.9 stack.66
  355.5 1.4 fusion.106
  356.9 58.7 %psum.15 = f32[4,7,7]{2,1,0:T(8,128)S(1)} all-reduce(f32[4,7,7]{2,1,0:T(8,128)S(1)} %fusion.106), channel_id=1, replica_groups=mesh['groups'=2,'dom'=16] {'dom'}, use_global_device_ids=true, to_apply=%region_5.9 | all-reduce | flops 196 | bytes 1568 | tf_op jit(solution)/shard_map/psum | solution.py:102
  415.9 0.8 stack.67
  417.0 2.2 custom-call.19
  419.5 1.9 custom-call.21
  422.0 0.7 fusion.108
  422.6 0.7 copy.115
  423.3 0.7 fusion.87
  424.0 1.6 bitcast_add_fusion
  (138 shorter events, 10.1 us)
Async XLA Ops:
  0.6 3.8 copy-start.15
  4.4 7.2 %copy-start.1 = (f32[40,3,128,128]{3,2,1,0:T(8,128)}, f32[40,3,128,128]{3,2,1,0:T(8,128)S(1)}, u32[]{:S(2)}) copy-start(f32[40,3,128,128]{3,2,1,0:T(8,128)S(1)} %slice.185) | copy-start | bytes 23592964
  4.5 12.3 %copy-start.9 = (f32[4,5120]{1,0:T(4,128)S(1)}, f32[4,5120]{1,0:T(4,128)}, u32[]{:S(2)}) copy-start(f32[4,5120]{1,0:T(4,128)} %param.16) | copy-start | bytes 245764
  4.5 16.0 %copy-start.14 = (s32[40,4]{0,1:T(4,128)S(1)}, s32[40,4]{0,1:T(4,128)}, u32[]{:S(2)}) copy-start(s32[40,4]{0,1:T(4,128)} %param.14) | copy-start | bytes 1924
  11.6 66.8 %collective-permute-start.4 = (f32[10,4,128,128]{3,2,1,0:T(8,128)}, f32[10,4,128,128]{3,2,1,0:T(8,128)}, u32[]{:S(2)}, u32[]{:S(2)}) collective-permute-start(f32[10,4,128,128]{3,2,1,0:T(8,128)} %get-tuple-element.25), channel_id=1, source_target_pairs={{0,1},{1,2},{2,3},{3,4},{4,5},{5,6},{6,7},{7,8},{8,9},{9,10},{10,1... | collective-permute-start | bytes 7864328 | tf_op jit(solution)/shard_map/ppermute | solution.py:22
  15.4 63.0 %collective-permute-start.5 = (f32[10,4,128,128]{3,2,1,0:T(8,128)}, f32[10,4,128,128]{3,2,1,0:T(8,128)}, u32[]{:S(2)}, u32[]{:S(2)}) collective-permute-start(f32[10,4,128,128]{3,2,1,0:T(8,128)} %get-tuple-element.26), channel_id=1, source_target_pairs={{1,0},{2,1},{3,2},{4,3},{5,4},{6,5},{7,6},{8,7},{9,8},{10,9},{11,1... | collective-permute-start | bytes 7864328 | tf_op jit(solution)/shard_map/ppermute | solution.py:25
  16.7 14.4 %collective-permute-start = (f32[4,12,128]{2,0,1:T(4,128)S(1)}, f32[4,12,128]{2,0,1:T(4,128)S(1)}, u32[]{:S(2)}, u32[]{:S(2)}) collective-permute-start(f32[4,12,128]{2,0,1:T(4,128)S(1)} %get-tuple-element.31), channel_id=1, source_target_pairs={{0,1},{1,2},{2,3},{3,4},{4,5},{5,6},{6,7},{7,8},{8,9},{9,10},{10,1... | collective-permute-start | bytes 73736 | tf_op jit(solution)/shard_map/ppermute | solution.py:22
  20.6 7.6 %collective-permute-start.2 = (s32[10,4]{0,1:T(4,128)S(1)}, s32[10,4]{0,1:T(4,128)S(1)}, u32[]{:S(2)}, u32[]{:S(2)}) collective-permute-start(s32[10,4]{0,1:T(4,128)S(1)} %get-tuple-element.33), channel_id=1, source_target_pairs={{0,1},{1,2},{2,3},{3,4},{4,5},{5,6},{6,7},{7,8},{8,9},{9,10},{10,1... | collective-permute-start | bytes 488 | tf_op jit(solution)/shard_map/ppermute | solution.py:22
  24.2 5.3 %collective-permute-start.3 = (s32[10,4]{0,1:T(4,128)S(1)}, s32[10,4]{0,1:T(4,128)S(1)}, u32[]{:S(2)}, u32[]{:S(2)}) collective-permute-start(s32[10,4]{0,1:T(4,128)S(1)} %get-tuple-element.34), channel_id=1, source_target_pairs={{1,0},{2,1},{3,2},{4,3},{5,4},{6,5},{7,6},{8,7},{9,8},{10,9},{11,1... | collective-permute-start | bytes 488 | tf_op jit(solution)/shard_map/ppermute | solution.py:25
  26.7 226.9 %copy-start.18 = (pred[6,6]{1,0:T(8,128)(4,1)}, pred[6,6]{1,0:T(8,128)(4,1)S(1)}, u32[]{:S(2)}) copy-start(pred[6,6]{1,0:T(8,128)(4,1)S(1)} %iota_compare_fusion.2) | copy-start | bytes 112
  26.7 227.1 %copy-start.16 = (pred[6,6]{1,0:T(8,128)(4,1)}, pred[6,6]{1,0:T(8,128)(4,1)S(1)}, u32[]{:S(2)}) copy-start(pred[6,6]{1,0:T(8,128)(4,1)S(1)} %iota_compare_fusion.1) | copy-start | bytes 112
  26.8 140.2 %copy-start.10 = (s32[1024]{0:T(1024)}, s32[1024]{0:T(1024)S(1)}, u32[]{:S(2)}) copy-start(s32[1024]{0:T(1024)S(1)} %pad_clamp_fusion) | copy-start | bytes 12292
  28.2 48.4 %collective-permute-start.1 = (f32[4,12,128]{2,0,1:T(4,128)S(1)}, f32[4,12,128]{2,0,1:T(4,128)S(1)}, u32[]{:S(2)}, u32[]{:S(2)}) collective-permute-start(f32[4,12,128]{2,0,1:T(4,128)S(1)} %get-tuple-element.32), channel_id=1, source_target_pairs={{1,0},{2,1},{3,2},{4,3},{5,4},{6,5},{7,6},{8,7},{9,8},{10,9},{11,1... | collective-permute-start | bytes 73736 | tf_op jit(solution)/shard_map/ppermute | solution.py:25
  31.1 106.3 %copy-start.8 = (s32[1024]{0:T(1024)}, s32[1024]{0:T(1024)S(1)}, u32[]{:S(2)}) copy-start(s32[1024]{0:T(1024)S(1)} %pad_clamp_fusion.2) | copy-start | bytes 12292
  101.9 5.5 %copy-start = (f32[60,4,128,128]{3,2,1,0:T(8,128)}, f32[60,4,128,128]{3,2,1,0:T(8,128)S(1)}, u32[]{:S(2)}) copy-start(f32[60,4,128,128]{3,2,1,0:T(8,128)S(1)} %pad_maximum_fusion) | copy-start | bytes 47185924
  153.1 30.1 %copy-start.12 = (f32[4,1,5120]{2,0,1:T(4,128)S(1)}, f32[4,1,5120]{2,0,1:T(4,128)}, u32[]{:S(2)}) copy-start(f32[4,1,5120]{2,0,1:T(4,128)} %slice_bitcast_fusion.7) | copy-start | bytes 245764
  166.3 89.9 %copy-start.20 = (f32[7]{0:T(128)S(1)}, f32[7]{0:T(128)}, u32[]{:S(2)}) copy-start(f32[7]{0:T(128)} %constant.125.clone.1) | copy-start | bytes 88
  167.8 12.2 %copy-start.13 = (f32[4,1,5120]{2,0,1:T(4,128)S(1)}, f32[4,1,5120]{2,0,1:T(4,128)}, u32[]{:S(2)}) copy-start(f32[4,1,5120]{2,0,1:T(4,128)} %slice_bitcast_fusion.9) | copy-start | bytes 245764
  180.1 3.2 copy-start.3
  181.1 2.2 copy-start.4
  182.1 1.2 copy-start.5
  183.2 0.6 copy-start.6
  183.8 0.6 copy-start.7
  257.1 5.9 %collective-permute-start.6 = (f32[4,12,128]{2,0,1:T(4,128)S(1)}, f32[4,12,128]{2,0,1:T(4,128)S(1)}, u32[]{:S(2)}, u32[]{:S(2)}) collective-permute-start(f32[4,12,128]{2,0,1:T(4,128)S(1)} %get-tuple-element.27), channel_id=1, source_target_pairs={{0,1},{1,2},{2,3},{3,4},{4,5},{5,6},{6,7},{7,8},{8,9},{9,10},{10,1... | collective-permute-start | bytes 73736 | tf_op jit(solution)/shard_map/ppermute | solution.py:22
  258.4 4.6 %collective-permute-start.7 = (f32[4,12,128]{2,0,1:T(4,128)S(1)}, f32[4,12,128]{2,0,1:T(4,128)S(1)}, u32[]{:S(2)}, u32[]{:S(2)}) collective-permute-start(f32[4,12,128]{2,0,1:T(4,128)S(1)} %get-tuple-element.28), channel_id=1, source_target_pairs={{1,0},{2,1},{3,2},{4,3},{5,4},{6,5},{7,6},{8,7},{9,8},{10,9},{11,1... | collective-permute-start | bytes 73736 | tf_op jit(solution)/shard_map/ppermute | solution.py:25
  327.6 13.9 %copy-start.11 = (s32[1024]{0:T(1024)S(1)}, s32[1024]{0:T(1024)}, u32[]{:S(2)}) copy-start(s32[1024]{0:T(1024)} %copy-done.10) | copy-start | bytes 12292
  341.6 77.6 %copy-start.19 = (pred[6,6]{1,0:T(8,128)(4,1)S(1)}, pred[6,6]{1,0:T(8,128)(4,1)}, u32[]{:S(2)}) copy-start(pred[6,6]{1,0:T(8,128)(4,1)} %copy-done.18) | copy-start | bytes 112
  341.6 77.8 %copy-start.17 = (pred[6,6]{1,0:T(8,128)(4,1)S(1)}, pred[6,6]{1,0:T(8,128)(4,1)}, u32[]{:S(2)}) copy-start(pred[6,6]{1,0:T(8,128)(4,1)} %copy-done.16) | copy-start | bytes 112
  341.6 80.2 %copy-start.21 = (f32[7]{0:T(128)S(1)}, f32[7]{0:T(128)}, u32[]{:S(2)}) copy-start(f32[7]{0:T(128)} %constant.125.clone.1) | copy-start | bytes 88
  342.5 12.1 %copy-start.2 = (f32[4,1,5120]{2,1,0:T(1,128)S(1)}, f32[4,1,5120]{2,1,0:T(1,128)}, u32[]{:S(2)}) copy-start(f32[4,1,5120]{2,1,0:T(1,128)} %stack.59) | copy-start | bytes 245764
where the time goes:
time: 434 us; the launch traced here: 426 us
  matrix products  175 us (40%)
  blocking collectives  120 us (28%)
  waiting for transfers between devices  45.5 us (10%)
  local copies, waits for them, and re-layouts  41.9 us (10%)
  other arithmetic  24 us (6%)
  starting transfers between devices  17.8 us (4%)
    dot_general x12, matrix products, apply_rows(): jnp.einsum('ikab,rikb->ria', matrix, gathered, precision=lax.Precision.HI...  166 us
    psum x2, blocking collectives, local(): gram = lax.psum(local_gram, 'dom')  120 us
    ppermute x4, waiting for transfers between devices, with_halo(): lax.ppermute(lax.slice_in_dim(block, 0, width, axis=dim), axis, backward)  45.5 us
    another operation x28, local copies, waits for them, and re-layouts, local(): jnp.stack(vectors, 1).reshape(rhs_count, S + 1, row_blocks * block_size)  14.4 us
    ppermute x4, starting transfers between devices, with_halo(): lax.ppermute(lax.slice_in_dim(block, block.shape[dim] - width, None, axis...  12.5 us
    gather x12, local copies, waits for them, and re-layouts, apply_rows(): gathered = region[:, column_index, :]  12.4 us
  transfers between devices with their start and end apart: 8, of which 1 were waited for; matrix products, arithmetic and copies ran while one was open for 2% of the time, Pallas kernels for 0%

commit v1 on v0

v1 whole, which is shorter than its diff:
```python
import functools
import math

import jax
import jax.numpy as jnp
import numpy as np
from jax import lax
from jax.experimental import pallas as pl
from jax.experimental.pallas import tpu as pltpu
from jax.sharding import PartitionSpec as P

W = 2
S = 6
CYCLES = 2
CHAIN = S * CYCLES
GROUPS = (2, 2, 2, 2, 2, 2)
SCALE = 0.125
GROW = 1.0 / SCALE
SHIFTS = [
    float(np.float32(1.6) + np.float32(0.8) * np.float32(math.cos(math.pi * (2 * j + 1) / (2 * S))))
    for j in range(S)
]
F32 = jnp.float32
BF16 = jnp.bfloat16
VM = pl.BlockSpec(memory_space=pltpu.VMEM)
SM = pl.BlockSpec(memory_space=pltpu.SMEM)
HB = pl.BlockSpec(memory_space=pltpu.HBM)


def params(mib):
    return pltpu.CompilerParams(vmem_limit_bytes=mib << 20)


def halves():
    return lax.broadcasted_iota(jnp.int32, (8, 128), 0) < 4


def split(tile, mask):
    high = tile.astype(BF16).astype(F32)
    return jnp.where(mask, high, tile - high)


def store_pair(block, high_ref, low_ref, pair, half, k):
    turned = block.T * SCALE
    high = turned.astype(BF16)
    low = (turned - high.astype(F32)).astype(BF16)
    rows, cols = slice(k * 128, (k + 1) * 128), slice(half * 128, (half + 1) * 128)
    high_ref[pair, rows, cols] = high
    low_ref[pair, rows, cols] = low


def prep_kernel(depth, margin, info, blocks, rhs, diag, offs, start, even, odd, sems):
    rows = diag.shape[0]
    parity = info[0]
    copies = []
    for place, (ref, at) in enumerate(((even, 1 - parity), (odd, parity))):
        first = pl.multiple_of(at * (rows - margin) * 512, 512)
        copies.append(
            pltpu.make_async_copy(
                blocks.at[pl.ds(first, margin * 512)],
                ref.at[pl.ds(0, margin * 512)],
                sems.at[place],
            )
        )
        copies[-1].start()
    for i in range(rows):
        part = rhs[:, i * 128 : (i + 1) * 128]
        start[i] = jnp.concatenate([part, part], 0)
    fill = jnp.zeros((margin, 124), F32)
    for ref, at in ((even, 1 - parity), (odd, parity)):
        base = margin * 512
        for i in range(depth):
            ref[base + 8 * i : base + 8 * i + 8, :] = start[at * (rows - depth) + i]
        base += 8 * depth
        is_high = at == 1
        diag_part = jnp.where(is_high, diag[rows - margin :, :], diag[:margin, :])
        offs_part = jnp.where(is_high, offs[rows - margin :, :], offs[:margin, :]).astype(F32)
        ref[base : base + margin, :] = diag_part
        ref[base + margin : base + 2 * margin, :] = jnp.concatenate([offs_part, fill], 1)
        if margin % 4:
            ref[base + 2 * margin : base + 8, :] = jnp.zeros((8 - 2 * margin, 128), F32)
    for copy in copies:
        copy.wait()


def convert_kernel(slots, blocks, high, low, buf, sems):
    rows = blocks.shape[0] // 512

    def fetch(i, slot):
        first = pl.multiple_of(i * 512, 512)
        return pltpu.make_async_copy(blocks.at[pl.ds(first, 512)], buf.at[slot], sems.at[slot])

    for slot in range(slots):
        fetch(slot, slot).start()

    def body(q, carry):
        for slot in range(slots):
            i = q * slots + slot
            fetch(i, slot).wait()
            for k in range(4):
                store_pair(
                    buf[slot, k * 128 : (k + 1) * 128, :],
                    high,
                    low,
                    q * (slots // 2) + slot // 2,
                    slot % 2,
                    k,
                )

            @pl.when(i + slots < rows)
            def _():
                fetch(i + slots, slot).start()

        return carry

    lax.fori_loop(0, rows // slots, body, 0)


def halo_kernel(depth, margin, info, even, odd, diag, high, low, scaled, halo):
    rows = diag.shape[0]
    parity = info[0]
    for i in range(rows):
        scaled[margin + i] = diag[i : i + 1, :] * SCALE
    for ref, side in ((even, 1 - parity), (odd, parity)):
        for m in range(margin):
            for k in range(4):
                first = (m * 4 + k) * 128
                store_pair(
                    ref[first : first + 128, :], high, low, side * (margin // 2) + m // 2, m % 2, k
                )
        base = margin * 512
        for i in range(depth):
            halo[side, i] = ref[base + 8 * i : base + 8 * i + 8, :]
        base += 8 * depth
        for m in range(margin):
            scaled[side * (rows + margin) + m] = ref[base + m : base + m + 1, :] * SCALE


def steps_kernel(first, steps, shifts, margin, next_depth, *refs):
    refs = list(refs)
    info, offs, high, low, halo_high, halo_low, scaled, own = refs[:8]
    del refs[:8]
    depth = W * steps
    if first:
        halo = refs.pop(0)
    else:
        from_even, from_odd = refs[:2]
        del refs[:2]
    outs = refs[:steps]
    del refs[:steps]
    if next_depth:
        to_even, to_odd = refs[:2]
        del refs[:2]
    splits = refs[:steps]
    del refs[:steps]
    if not first:
        halo = refs.pop(0)
    inner = refs
    rows = own.shape[0]
    parity = info[0]
    mask = halves()
    if not first:
        there = info[1] == 1
        for i in range(depth):
            halo[1 - parity, i] = from_even[i]
            tile = from_odd[parity, i]
            halo[parity, i] = jnp.where(there, tile, jnp.zeros_like(tile))
    for i in range(depth):
        splits[0][i] = split(halo[0, i], mask)
        splits[0][depth + rows + i] = split(halo[1, i], mask)
    for i in range(rows):
        splits[0][depth + i] = split(own[i], mask)

    def value(step, row):
        if 0 <= row < rows:
            return own[row] if step == 0 else outs[step - 1][row]
        if step == 0:
            return halo[0, row + depth] if row < 0 else halo[1, row - rows]
        keep = W * (steps - step)
        ref = inner[step - 1]
        return ref[row + keep] if row < 0 else ref[keep + row - rows]

    for step in range(steps):
        keep = W * (steps - 1 - step)
        reach = keep + W
        source = splits[step]
        pairs = list(range(-keep, rows + keep, 2))
        streamed = []
        for row in pairs:
            parts = []
            for k in range(4):
                tiles = [
                    source[offs[(row + h + margin) * 4 + k] + (row + h + reach)] for h in range(2)
                ]
                parts.append(jnp.concatenate(tiles, 0).astype(BF16))
            streamed.append(jnp.concatenate(parts, 1))
        sums = []
        for row, left in zip(pairs, streamed):
            if row < 0:
                mats = halo_high[(row + margin) // 2], halo_low[(row + margin) // 2]
            elif row >= rows:
                at = margin // 2 + (row - rows) // 2
                mats = halo_high[at], halo_low[at]
            else:
                mats = high[row // 2], low[row // 2]
            sums.append(
                jnp.dot(left, mats[0], preferred_element_type=F32)
                + jnp.dot(left, mats[1], preferred_element_type=F32)
            )
        for row, total in zip(pairs, sums):
            for h in range(2):
                at = row + h
                part = total[8 * h : 8 * h + 8, 128 * h : 128 * h + 128]
                part = part + pltpu.roll(part, 4, 0)
                tile = part + (scaled[at + margin] - SCALE * shifts[step]) * value(step, at)
                if 0 <= at < rows:
                    outs[step][at] = tile
                elif at < 0:
                    inner[step][at + keep] = tile
                else:
                    inner[step][keep + at - rows] = tile
                if step < steps - 1:
                    splits[step + 1][at + keep] = split(tile, mask)
    if next_depth:
        last = outs[-1]
        for i in range(next_depth):
            to_even[i] = last[(1 - parity) * (rows - next_depth) + i]
            to_odd[i] = last[parity * (rows - next_depth) + i]


def pair_list():
    half = CHAIN // 2 + 1
    low, top = range(half), range(half, CHAIN + 1)
    return (
        [(i, j) for i in low for j in low if i <= j],
        [(i, j) for i in low for j in top],
        [(i, j) for i in top for j in top if i <= j],
    )


PLACES = {pair: at for at, pair in enumerate(sum(pair_list(), []))}


def dense(ref, p, mask):
    return jnp.where(mask, ref[2 * p], ref[2 * p + 1])


def gram_kernel(*refs):
    vectors, out = refs[:-1], refs[-1]
    count = vectors[0].shape[0] // 2
    mask = halves()
    lane = lax.broadcasted_iota(jnp.int32, (8, 128), 1)
    tile = jnp.zeros((8, 128), F32)
    for pairs in pair_list():
        used = sorted({i for pair in pairs for i in pair})
        total = None
        for p in range(count):
            here = {i: dense(vectors[i], p, mask) for i in used}
            products = [here[i] * here[j] for i, j in pairs]
            total = products if total is None else [a + b for a, b in zip(total, products)]
        for pair, one in zip(pairs, total):
            tile = jnp.where(lane == PLACES[pair], jnp.sum(one, axis=1, keepdims=True), tile)
    for d in range(out.shape[0]):
        out[d] = tile


def small_solve(gram):
    def g(i, j):
        return gram[(i, j) if i <= j else (j, i)]

    right = [[SHIFTS[b] * g(a, b) + GROW * g(a, b + 1) for b in range(S)] for a in range(S + 1)]
    normal = [
        [SHIFTS[a] * right[a][b] + GROW * right[a + 1][b] for b in range(a + 1)] for a in range(S)
    ]
    target = [SHIFTS[a] * g(a, 0) + GROW * g(a + 1, 0) for a in range(S)]
    lower = [[None] * S for _ in range(S)]
    scaled = [[None] * S for _ in range(S)]
    inverse = []
    for j in range(S):
        pivot = normal[j][j]
        for k in range(j):
            pivot = pivot - scaled[j][k] * lower[j][k]
        inverse.append(1.0 / pivot)
        for i in range(j + 1, S):
            entry = normal[i][j]
            for k in range(j):
                entry = entry - scaled[i][k] * lower[j][k]
            scaled[i][j] = entry
            lower[i][j] = entry * inverse[j]
    coeffs = list(target)
    for i in range(S):
        for k in range(i):
            coeffs[i] = coeffs[i] - lower[i][k] * coeffs[k]
    coeffs = [c * d for c, d in zip(coeffs, inverse)]
    for i in reversed(range(S)):
        for k in range(i + 1, S):
            coeffs[i] = coeffs[i] - lower[k][i] * coeffs[k]
    combine = []
    for m in range(S + 1):
        entry = jnp.ones_like(coeffs[0]) if m == 0 else -GROW * coeffs[m - 1]
        if m < S:
            entry = entry - SHIFTS[m] * coeffs[m]
        combine.append(entry)
    return coeffs, combine


def final_kernel(grams, *refs):
    vectors, solution_ref, residual_ref = refs[:-2], refs[-2], refs[-1]
    count = vectors[0].shape[0] // 2
    mask = halves()
    parts = [grams[d] for d in range(grams.shape[0])]
    while len(parts) > 1:
        parts = [a + b for a, b in zip(parts[::2], parts[1::2])] + (
            parts[-1:] if len(parts) % 2 else []
        )
    tile = parts[0] + pltpu.roll(parts[0], 4, 0)
    gram = {
        pair: jnp.broadcast_to(tile[:, at : at + 1], (8, 128)) for pair, at in PLACES.items()
    }

    def g(i, j):
        return gram[(i, j) if i <= j else (j, i)]

    coeffs, combine = small_solve(gram)
    columns = [combine]
    for k in range(S):
        last = columns[-1]
        column = []
        for m in range(len(last) + 1):
            entry = None
            if m < len(last):
                gap = SCALE * (SHIFTS[m % S] - SHIFTS[k])
                entry = gap * last[m] if m % S != k else None
            if m > 0:
                entry = last[m - 1] if entry is None else entry + last[m - 1]
            column.append(jnp.zeros_like(last[0]) if entry is None else entry)
        columns.append(column)
    second = {}
    for b in range(S + 1):
        image = []
        for m in range(len(columns[b])):
            total = None
            for i, c in enumerate(columns[b]):
                term = g(m, i) * c
                total = term if total is None else total + term
            image.append(total)
        for a in range(b + 1):
            total = None
            for m, c in enumerate(columns[a]):
                term = c * image[m]
                total = term if total is None else total + term
            second[(a, b)] = total
    more, ending = small_solve(second)
    to_solution, to_residual = [], []
    for m in range(CHAIN + 1):
        total = coeffs[m] if m < S else None
        for a in range(S):
            if m < len(columns[a]):
                term = more[a] * columns[a][m]
                total = term if total is None else total + term
        to_solution.append(total)
        total = None
        for a in range(S + 1):
            if m < len(columns[a]):
                term = ending[a] * columns[a][m]
                total = term if total is None else total + term
        to_residual.append(total)
    for p in range(count):
        here = [dense(ref, p, mask) for ref in vectors]
        for ref, weights in ((solution_ref, to_solution), (residual_ref, to_residual)):
            total = None
            for weight, one in zip(weights, here):
                if weight is not None:
                    total = weight * one if total is None else total + weight * one
            ref[:, (2 * p) * 128 : (2 * p + 1) * 128] = total[0:4]
            ref[:, (2 * p + 1) * 128 : (2 * p + 2) * 128] = total[4:8]


def shape(*dims, kind=F32):
    return jax.ShapeDtypeStruct(dims, kind)


def local(blocks, offsets, diag_shift, right_side):
    rhs_count = right_side.shape[0]
    rows, per_row, size = blocks.shape[0], blocks.shape[1], blocks.shape[2]
    count, copies = lax.axis_size("dom"), lax.axis_size("groups")
    me = lax.axis_index("dom")
    parity = me % 2
    linked = jnp.logical_and(me > 0, me < count - 1)
    info = jnp.stack([parity, linked.astype(jnp.int32)])
    margin = W * (max(GROUPS) - 1)
    depth = W * GROUPS[0]
    flat = blocks.reshape(rows * per_row * size, size)
    diag = diag_shift.reshape(rows, size)
    message = shape(margin * 512 + 8 * depth + -(-2 * margin // 8) * 8, size)
    start, even, odd = pl.pallas_call(
        functools.partial(prep_kernel, depth, margin),
        out_shape=[shape(rows, 8, size), message, message],
        in_specs=[SM, HB, VM, VM, VM],
        out_specs=[VM] * 3,
        scratch_shapes=[pltpu.SemaphoreType.DMA((2,))],
        compiler_params=params(8),
        name="prepare",
    )(info, flat, right_side, diag, offsets)

    swap_even = [(i, i ^ 1) for i in range(count)]
    swap_odd = [(i, i + 1) for i in range(1, count - 1, 2)]
    swap_odd = swap_odd + [(b, a) for a, b in swap_odd]
    if copies % 2:
        axes, pairs = "dom", [[i, (i + 1) % count] for i in range(1, count, 2)]
    else:
        axes = ("groups", "dom")
        pairs = [[g * count + i, g * count + i + 1] for g in range(copies) for i in range(1, count - 1, 2)]
        for g in range(0, copies, 2):
            pairs += [[g * count + e, (g + 1) * count + e] for e in (0, count - 1)]

    odd = lax.ppermute(odd, "dom", swap_odd)
    even = lax.ppermute(even, "dom", swap_even)

    pair_shape = shape(rows // 2, per_row * size, 2 * size, kind=BF16)
    high, low = pl.pallas_call(
        functools.partial(convert_kernel, 4),
        out_shape=[pair_shape] * 2,
        in_specs=[HB],
        out_specs=[VM] * 2,
        scratch_shapes=[pltpu.VMEM((4, per_row * size, size), F32), pltpu.SemaphoreType.DMA((4,))],
        compiler_params=params(16),
        name="convert",
    )(flat)

    halo_shape = shape(margin, per_row * size, 2 * size, kind=BF16)
    halo_high, halo_low, scaled, halo = pl.pallas_call(
        functools.partial(halo_kernel, depth, margin),
        out_shape=[halo_shape, halo_shape, shape(rows + 2 * margin, 1, size), shape(2, depth, 8, size)],
        in_specs=[SM] + [VM] * 3,
        out_specs=[VM] * 4,
        compiler_params=params(8),
        name="halo",
    )(info, even, odd, diag)

    at = margin * 512 + 8 * depth + margin
    even_offs, odd_offs = even[at : at + margin, :per_row], odd[at : at + margin, :per_row]
    left = jnp.where(parity == 0, odd_offs, even_offs).astype(jnp.int32)
    right = jnp.where(parity == 0, even_offs, odd_offs).astype(jnp.int32)
    all_offs = jnp.concatenate([left, offsets, right], 0).reshape(-1)

    vectors = [start]
    done = 0
    for number, steps in enumerate(GROUPS):
        first = number == 0
        next_depth = W * GROUPS[number + 1] if number + 1 < len(GROUPS) else 0
        depth = W * steps
        outs = [shape(rows, 8, size)] * steps + [shape(next_depth, 8, size)] * (2 if next_depth else 0)
        scratch = [pltpu.VMEM((rows + 2 * W * (steps - j), 8, size), F32) for j in range(steps)]
        if not first:
            scratch.append(pltpu.VMEM((2, depth, 8, size), F32))
        scratch += [pltpu.VMEM((2 * W * (steps - 1 - j), 8, size), F32) for j in range(steps - 1)]
        received = [halo] if first else [even, odd]
        results = pl.pallas_call(
            functools.partial(
                steps_kernel, first, steps, [SHIFTS[(done + j) % S] for j in range(steps)], margin, next_depth
            ),
            out_shape=outs,
            in_specs=[SM, SM] + [VM] * (6 + len(received)),
            out_specs=[VM] * len(outs),
            scratch_shapes=scratch,
            compiler_params=params(16),
            name="steps",
        )(info, all_offs, high, low, halo_high, halo_low, scaled, vectors[-1], *received)
        vectors += results[:steps]
        done += steps
        if next_depth:
            even, odd = results[steps:]
            even = lax.ppermute(even, "dom", swap_even)
            odd = lax.all_gather(odd, axes, axis_index_groups=pairs)

    gram = pl.pallas_call(
        gram_kernel,
        out_shape=shape(count, 8, size),
        in_specs=[VM] * len(vectors),
        out_specs=VM,
        compiler_params=params(16),
        name="gram",
    )(*vectors)
    gram = lax.all_to_all(gram, "dom", 0, 0)
    return tuple(
        pl.pallas_call(
            final_kernel,
            out_shape=[shape(rhs_count, rows * size)] * 2,
            in_specs=[VM] * (1 + len(vectors)),
            out_specs=[VM] * 2,
            compiler_params=params(16),
            name="finish",
        )(gram, *vectors)
    )


def solution(mesh):
    in_specs = (
        P(("groups", "dom"), None, None, None),
        P(("groups", "dom"), None),
        P(("groups", "dom")),
        P(None, ("groups", "dom")),
    )
    out_specs = (P(None, ("groups", "dom")), P(None, ("groups", "dom")))
    return jax.shard_map(local, mesh=mesh, in_specs=in_specs, out_specs=out_specs, check_vma=False)
```

time: 434 us -> 94.8 us (0.22); the launches traced: 426 us -> 94.3 us
  matrix products: 175 us -> 0 us
  blocking collectives: 120 us -> 34.8 us
  waiting for transfers between devices: 45.5 us -> 0.02 us
  Pallas kernels: 0 us -> 31.9 us
  other arithmetic: 24 us -> 0.16 us
  local copies, waits for them, and re-layouts: 41.9 us -> 20.5 us
  starting transfers between devices: 17.8 us -> 6.19 us
    dot_general x26 -> x0, matrix products: 175 us -> none  [the longest x12 166 us: apply_rows(): jnp.einsum('ikab,rikb->ria', matrix, gathered, precision=lax.Precision.HI...]
    psum x2 -> x0, blocking collectives: 120 us -> none  [local(): gram = lax.psum(local_gram, 'dom')]
    ppermute x8 -> x7, waiting for transfers between devices: 45.5 us -> 0.02 us  [the longest x6 0.02 us: local(): even = lax.ppermute(even, 'dom', swap_even)]
    pallas_call x0 -> x11, Pallas kernels: none -> 31.9 us  [the longest x6 22 us: local(): pl.pallas_call(functools.partial(steps_kernel, first, steps, [SHIFTS[(don...]
    all_gather x0 -> x5, blocking collectives: none -> 22.2 us  [local(): odd = lax.all_gather(odd, axes, axis_index_groups=pairs)]
    another operation x29 -> x0, local copies, waits for them, and re-layouts: 14.4 us -> none  [the longest x28 14.4 us: local(): jnp.stack(vectors, 1).reshape(rhs_count, S + 1, row_blocks * block_size)]
    unnamed x44 -> x25, local copies, waits for them, and re-layouts: 6.73 us -> 20.1 us
    all_to_all x0 -> x1, blocking collectives: none -> 12.6 us  [local(): gram = lax.all_to_all(gram, 'dom', 0, 0)]
  transfers between devices with their start and end apart: 8 -> 7, of which waited for: 1 -> 0; matrix products, arithmetic and copies ran while one was open for 2% -> 0% of each run, Pallas kernels for 0% -> 7%
where the time goes in v1:
time: 94.8 us; the launch traced here: 94.3 us
  blocking collectives  34.8 us (37%)
  Pallas kernels  31.9 us (34%)
  local copies, waits for them, and re-layouts  20.5 us (22%)
  starting transfers between devices  6.19 us (7%)
    all_gather x5, blocking collectives, local(): odd = lax.all_gather(odd, axes, axis_index_groups=pairs)  22.2 us
    pallas_call x6, Pallas kernels, local(): pl.pallas_call(functools.partial(steps_kernel, first, steps, [SHIFTS[(don...  22 us
    unnamed x25, local copies, waits for them, and re-layouts  20.1 us
    all_to_all x1, blocking collectives, local(): gram = lax.all_to_all(gram, 'dom', 0, 0)  12.6 us
    pallas_call x1, Pallas kernels, local(): pl.pallas_call(functools.partial(convert_kernel, 4), out_shape=[pair_shap...  6.42 us
    ppermute x6, starting transfers between devices, local(): even = lax.ppermute(even, 'dom', swap_even)  5.5 us
  transfers between devices with their start and end apart: 7, of which 0 were waited for; matrix products, arithmetic and copies ran while one was open for 0% of the time, Pallas kernels for 7%

profile of v1, /device:TPU:0, one launch (start us, length us, event | category | flops | bytes accessed | tf_op | source)
XLA Modules:
  0.0 94.3 jit_solution(9963943843289184830)
XLA Ops:
  0.6 0.8 copy.13.offs
  1.4 0.1 pad_add_fusion.1.info.refs_0_
  1.5 0.0 copy-start.6
  1.5 4.0 %copy-done.6 = f32[40,4,128,128]{3,2,1,0:T(8,128)S(1)} copy-done((f32[40,4,128,128]{3,2,1,0:T(8,128)S(1)}, f32[40,4,128,128]{3,2,1,0:T(8,128)}, u32[]{:S(2)}) %copy-start.6) | copy-done | bytes 10485784
  5.5 0.0 copy-start.8
  5.5 0.9 copy-done.8
  6.4 0.0 copy-start.9
  6.4 0.7 copy-done.9
  7.1 0.7 prepare.1
  7.8 0.7 collective-permute-start
  8.5 4.4 %collective-permute-start.1 = (f32[1064,128]{1,0:T(8,128)S(1)}, f32[1064,128]{1,0:T(8,128)S(1)}, u32[]{:S(2)}, u32[]{:S(2)}) collective-permute-start(f32[1064,128]{1,0:T(8,128)S(1)} %get-tuple-element.35), channel_id=1, source_target_pairs={{0,1},{1,0},{2,3},{3,2},{4,5},{5,4},{6,7},{7,6},{8,9},{9,8},{10,11... | collective-permute-start | bytes 1634312 | tf_op jit(solution)/shard_map/ppermute | solution.py:418
  12.8 0.0 copy-start.7
  12.8 4.0 %copy-done.7 = f32[40,4,128,128]{3,2,1,0:T(8,128)S(1)} copy-done((f32[40,4,128,128]{3,2,1,0:T(8,128)S(1)}, f32[40,4,128,128]{3,2,1,0:T(8,128)}, u32[]{:S(2)}) %copy-start.7) | copy-done | bytes 10485784
  16.8 0.0 copy-start.11
  16.8 0.0 copy-start.10
  16.8 6.4 %convert.2 = (bf16[20,512,256]{2,1,0:T(8,128)(2,1)S(1)}, bf16[20,512,256]{2,1,0:T(8,128)(2,1)S(1)}) custom-call(f32[20480,128]{1,0:T(8,128)S(1)} %bitcast.10), custom_call_target="tpu_custom_call" | custom-call | tf_op jit(solution)/shard_map/convert/pallas_call | solution.py:421
  23.3 0.0 copy-start
  23.3 2.3 %copy-done = bf16[20,512,256]{2,1,0:T(8,128)(2,1)} copy-done((bf16[20,512,256]{2,1,0:T(8,128)(2,1)}, bf16[20,512,256]{2,1,0:T(8,128)(2,1)S(1)}, u32[]{:S(2)}) %copy-start) | copy-done | bytes 5242904
  25.6 0.0 copy-start.3
  25.6 2.4 %copy-done.3 = bf16[20,512,256]{2,1,0:T(8,128)(2,1)} copy-done((bf16[20,512,256]{2,1,0:T(8,128)(2,1)}, bf16[20,512,256]{2,1,0:T(8,128)(2,1)S(1)}, u32[]{:S(2)}) %copy-start.3) | copy-done | bytes 5242904
  28.0 0.0 collective-permute-done.odd
  28.0 0.0 collective-permute-done.1.even
  28.0 0.1 copy.14
  28.1 0.1 copy.15
  28.2 0.0 copy-done.11
  28.2 0.1 pad_add_fusion
  28.2 0.1 copy.16
  28.4 0.1 reshape.15.refs_1_
  28.5 0.0 copy-done.10
  28.5 0.9 halo.1
  29.4 0.0 copy-start.1
  29.4 2.5 %copy-done.1 = bf16[20,512,256]{2,1,0:T(8,128)(2,1)S(1)} copy-done((bf16[20,512,256]{2,1,0:T(8,128)(2,1)S(1)}, bf16[20,512,256]{2,1,0:T(8,128)(2,1)}, u32[]{:S(2)}) %copy-start.1) | copy-done | bytes 5242904
  31.9 0.0 copy-start.4
  31.9 2.5 %copy-done.4 = bf16[20,512,256]{2,1,0:T(8,128)(2,1)S(1)} copy-done((bf16[20,512,256]{2,1,0:T(8,128)(2,1)S(1)}, bf16[20,512,256]{2,1,0:T(8,128)(2,1)}, u32[]{:S(2)}) %copy-start.4) | copy-done | bytes 5242904
  34.3 0.0 copy-start.2
  34.3 0.0 copy-start.5
  34.3 3.7 %steps.6 = (f32[40,8,128]{2,1,0:T(8,128)S(1)}, f32[40,8,128]{2,1,0:T(8,128)S(1)}, f32[4,8,128]{2,1,0:T(8,128)S(1)}, f32[4,8,128]{2,1,0:T(8,128)S(1)}) custom-call(s32[2]{0:T(128)S(1)} %pad_add_fusion.1.info.refs_0_, s32[176]{0:T(256)S(1)} %reshape.15.refs_1_, bf16[20,512,256]{2,1,0:T(8,128)(2,1)S(1)} %copy-done.1, bf16[20,512,256]{2,1,0:T(8,128)(2,1)S(1)} %copy-done.4, ...), custom_call_target="tpu_custom_call" | custom-call | tf_op jit(solution)/shard_map/steps/pallas_call | solution.py:459
  38.0 0.1 collective-permute-start.2
  38.1 4.4 %all-gather = f32[8,8,128]{2,1,0:T(8,128)S(1)} all-gather(f32[4,8,128]{2,1,0:T(8,128)S(1)} %get-tuple-element.45), channel_id=2, replica_groups={{1,2},{3,4},{5,6},{7,8},{9,10},{11,12},{13,14},{17,18},{19,20},{21,22},..., dimensions={0}, use_global_device_ids=true | all-gather | bytes 49152 | tf_op jit(solution)/shard_map/all_gather | solution.py:475
  42.5 0.0 collective-permute-done.2.refs_8_
  42.5 0.0 copy-done.2
  42.5 0.0 copy-done.5
  42.5 3.7 %steps.7 = (f32[40,8,128]{2,1,0:T(8,128)S(1)}, f32[40,8,128]{2,1,0:T(8,128)S(1)}, f32[4,8,128]{2,1,0:T(8,128)S(1)}, f32[4,8,128]{2,1,0:T(8,128)S(1)}) custom-call(s32[2]{0:T(128)S(1)} %pad_add_fusion.1.info.refs_0_, s32[176]{0:T(256)S(1)} %reshape.15.refs_1_, bf16[20,512,256]{2,1,0:T(8,128)(2,1)S(1)} %copy-done.2, bf16[20,512,256]{2,1,0:T(8,128)(2,1)S(1)} %copy-done.5, ...), custom_call_target="tpu_custom_call" | custom-call | tf_op jit(solution)/shard_map/steps/pallas_call | solution.py:459
  46.2 0.2 collective-permute-start.3
  46.4 4.4 %all-gather.1 = f32[8,8,128]{2,1,0:T(8,128)S(1)} all-gather(f32[4,8,128]{2,1,0:T(8,128)S(1)} %get-tuple-element.49), channel_id=3, replica_groups={{1,2},{3,4},{5,6},{7,8},{9,10},{11,12},{13,14},{17,18},{19,20},{21,22},..., dimensions={0}, use_global_device_ids=true | all-gather | bytes 49152 | tf_op jit(solution)/shard_map/all_gather | solution.py:475
  50.8 0.0 collective-permute-done.3.refs_8_
  50.8 3.7 %steps.8 = (f32[40,8,128]{2,1,0:T(8,128)S(1)}, f32[40,8,128]{2,1,0:T(8,128)S(1)}, f32[4,8,128]{2,1,0:T(8,128)S(1)}, f32[4,8,128]{2,1,0:T(8,128)S(1)}) custom-call(s32[2]{0:T(128)S(1)} %pad_add_fusion.1.info.refs_0_, s32[176]{0:T(256)S(1)} %reshape.15.refs_1_, bf16[20,512,256]{2,1,0:T(8,128)(2,1)S(1)} %copy-done.2, bf16[20,512,256]{2,1,0:T(8,128)(2,1)S(1)} %copy-done.5, ...), custom_call_target="tpu_custom_call" | custom-call | tf_op jit(solution)/shard_map/steps/pallas_call | solution.py:459
  54.5 0.2 collective-permute-start.4
  54.7 4.6 %all-gather.2 = f32[8,8,128]{2,1,0:T(8,128)S(1)} all-gather(f32[4,8,128]{2,1,0:T(8,128)S(1)} %get-tuple-element.53), channel_id=4, replica_groups={{1,2},{3,4},{5,6},{7,8},{9,10},{11,12},{13,14},{17,18},{19,20},{21,22},..., dimensions={0}, use_global_device_ids=true | all-gather | bytes 49152 | tf_op jit(solution)/shard_map/all_gather | solution.py:475
  59.3 0.0 collective-permute-done.4.refs_8_
  59.3 3.7 %steps.9 = (f32[40,8,128]{2,1,0:T(8,128)S(1)}, f32[40,8,128]{2,1,0:T(8,128)S(1)}, f32[4,8,128]{2,1,0:T(8,128)S(1)}, f32[4,8,128]{2,1,0:T(8,128)S(1)}) custom-call(s32[2]{0:T(128)S(1)} %pad_add_fusion.1.info.refs_0_, s32[176]{0:T(256)S(1)} %reshape.15.refs_1_, bf16[20,512,256]{2,1,0:T(8,128)(2,1)S(1)} %copy-done.2, bf16[20,512,256]{2,1,0:T(8,128)(2,1)S(1)} %copy-done.5, ...), custom_call_target="tpu_custom_call" | custom-call | tf_op jit(solution)/shard_map/steps/pallas_call | solution.py:459
  63.0 0.3 collective-permute-start.5
  63.2 4.4 %all-gather.3 = f32[8,8,128]{2,1,0:T(8,128)S(1)} all-gather(f32[4,8,128]{2,1,0:T(8,128)S(1)} %get-tuple-element.57), channel_id=5, replica_groups={{1,2},{3,4},{5,6},{7,8},{9,10},{11,12},{13,14},{17,18},{19,20},{21,22},..., dimensions={0}, use_global_device_ids=true | all-gather | bytes 49152 | tf_op jit(solution)/shard_map/all_gather | solution.py:475
  67.6 0.0 collective-permute-done.5.refs_8_
  67.6 3.7 %steps.10 = (f32[40,8,128]{2,1,0:T(8,128)S(1)}, f32[40,8,128]{2,1,0:T(8,128)S(1)}, f32[4,8,128]{2,1,0:T(8,128)S(1)}, f32[4,8,128]{2,1,0:T(8,128)S(1)}) custom-call(s32[2]{0:T(128)S(1)} %pad_add_fusion.1.info.refs_0_, s32[176]{0:T(256)S(1)} %reshape.15.refs_1_, bf16[20,512,256]{2,1,0:T(8,128)(2,1)S(1)} %copy-done.2, bf16[20,512,256]{2,1,0:T(8,128)(2,1)S(1)} %copy-done.5, ...), custom_call_target="tpu_custom_call" | custom-call | tf_op jit(solution)/shard_map/steps/pallas_call | solution.py:459
  71.3 0.4 collective-permute-start.6
  71.7 4.4 %all-gather.4 = f32[8,8,128]{2,1,0:T(8,128)S(1)} all-gather(f32[4,8,128]{2,1,0:T(8,128)S(1)} %get-tuple-element.61), channel_id=6, replica_groups={{1,2},{3,4},{5,6},{7,8},{9,10},{11,12},{13,14},{17,18},{19,20},{21,22},..., dimensions={0}, use_global_device_ids=true | all-gather | bytes 49152 | tf_op jit(solution)/shard_map/all_gather | solution.py:475
  76.1 0.0 collective-permute-done.6.refs_8_
  76.1 3.7 %steps.11 = (f32[40,8,128]{2,1,0:T(8,128)S(1)}, f32[40,8,128]{2,1,0:T(8,128)S(1)}) custom-call(s32[2]{0:T(128)S(1)} %pad_add_fusion.1.info.refs_0_, s32[176]{0:T(256)S(1)} %reshape.15.refs_1_, bf16[20,512,256]{2,1,0:T(8,128)(2,1)S(1)} %copy-done.2, bf16[20,512,256]{2,1,0:T(8,128)(2,1)S(1)} %copy-done.5, bf16[2,512,256]{2,1,0:T(8,128)(2,1)S(1)} %get-tuple-element.38.refs_4_, ...), custom_call_target="tpu_custom_call" | custom-call | tf_op jit(solution)/shard_map/steps/pallas_call | solution.py:459
  79.8 0.6 gram.1
  80.4 12.6 %all_to_all.5.grams = f32[16,8,128]{2,1,0:T(8,128)S(1)} all-to-all(f32[16,8,128]{2,1,0:T(8,128)S(1)} %gram.1), channel_id=1, replica_groups=mesh['groups'=2,'dom'=16] {'dom'}, dimensions={0} | all-to-all | bytes 131072 | tf_op jit(solution)/shard_map/all_to_all | solution.py:485
  93.0 1.3 %finish.1 = (f32[4,5120]{1,0:T(4,128)}, f32[4,5120]{1,0:T(4,128)}) custom-call(f32[16,8,128]{2,1,0:T(8,128)S(1)} %all_to_all.5.grams, f32[40,8,128]{2,1,0:T(8,128)S(1)} %get-tuple-element.33.refs_7_.refs_0_, f32[40,8,128]{2,1,0:T(8,128)S(1)} %get-tuple-element.42.refs_1_, f32[40,8,128]{2,1,0:T(8,128)S(1)} %get-tuple-element.43.refs_7_.refs_2_, ...), custom_call_target="tpu_custom_call" | custom-call | tf_op jit(solution)/shard_map/finish/pallas_call | solution.py:487
  (1 shorter events, 0.0 us)
Async XLA Ops:
  1.5 4.0 %copy-start.6 = (f32[40,4,128,128]{3,2,1,0:T(8,128)S(1)}, f32[40,4,128,128]{3,2,1,0:T(8,128)}, u32[]{:S(2)}) copy-start(f32[40,4,128,128]{3,2,1,0:T(8,128)} %param.4) | copy-start | bytes 31457284
  5.5 0.9 copy-start.8
  6.4 0.7 copy-start.9
  7.8 20.2 %collective-permute-start = (f32[1064,128]{1,0:T(8,128)S(1)}, f32[1064,128]{1,0:T(8,128)S(1)}, u32[]{:S(2)}, u32[]{:S(2)}) collective-permute-start(f32[1064,128]{1,0:T(8,128)S(1)} %get-tuple-element.34), channel_id=1, source_target_pairs={{1,2},{3,4},{5,6},{7,8},{9,10},{11,12},{13,14},{2,1},{4,3},{6,5},{... | collective-permute-start | bytes 1634312 | tf_op jit(solution)/shard_map/ppermute | solution.py:417
  8.5 19.5 %collective-permute-start.1 = (f32[1064,128]{1,0:T(8,128)S(1)}, f32[1064,128]{1,0:T(8,128)S(1)}, u32[]{:S(2)}, u32[]{:S(2)}) collective-permute-start(f32[1064,128]{1,0:T(8,128)S(1)} %get-tuple-element.35), channel_id=1, source_target_pairs={{0,1},{1,0},{2,3},{3,2},{4,5},{5,4},{6,7},{7,6},{8,9},{9,8},{10,11... | collective-permute-start | bytes 1634312 | tf_op jit(solution)/shard_map/ppermute | solution.py:418
  12.8 4.0 %copy-start.7 = (f32[40,4,128,128]{3,2,1,0:T(8,128)S(1)}, f32[40,4,128,128]{3,2,1,0:T(8,128)}, u32[]{:S(2)}) copy-start(f32[40,4,128,128]{3,2,1,0:T(8,128)} %param.4) | copy-start | bytes 31457284
  16.8 11.3 %copy-start.11 = (s32[40,4]{0,1:T(4,128)S(1)}, s32[40,4]{0,1:T(4,128)}, u32[]{:S(2)}) copy-start(s32[40,4]{0,1:T(4,128)} %param.5) | copy-start | bytes 1924
  16.8 11.6 %copy-start.10 = (f32[5120]{0:T(1024)S(1)}, f32[5120]{0:T(1024)}, u32[]{:S(2)}) copy-start(f32[5120]{0:T(1024)} %param.6) | copy-start | bytes 61444
  23.3 2.3 %copy-start = (bf16[20,512,256]{2,1,0:T(8,128)(2,1)}, bf16[20,512,256]{2,1,0:T(8,128)(2,1)S(1)}, u32[]{:S(2)}) copy-start(bf16[20,512,256]{2,1,0:T(8,128)(2,1)S(1)} %get-tuple-element.36.refs_2_) | copy-start | bytes 15728644
  25.6 2.4 %copy-start.3 = (bf16[20,512,256]{2,1,0:T(8,128)(2,1)}, bf16[20,512,256]{2,1,0:T(8,128)(2,1)S(1)}, u32[]{:S(2)}) copy-start(bf16[20,512,256]{2,1,0:T(8,128)(2,1)S(1)} %get-tuple-element.37.refs_3_) | copy-start | bytes 15728644
  29.4 2.5 %copy-start.1 = (bf16[20,512,256]{2,1,0:T(8,128)(2,1)S(1)}, bf16[20,512,256]{2,1,0:T(8,128)(2,1)}, u32[]{:S(2)}) copy-start(bf16[20,512,256]{2,1,0:T(8,128)(2,1)} %copy-done) | copy-start | bytes 15728644
  31.9 2.5 %copy-start.4 = (bf16[20,512,256]{2,1,0:T(8,128)(2,1)S(1)}, bf16[20,512,256]{2,1,0:T(8,128)(2,1)}, u32[]{:S(2)}) copy-start(bf16[20,512,256]{2,1,0:T(8,128)(2,1)} %copy-done.3) | copy-start | bytes 15728644
  34.3 8.2 %copy-start.2 = (bf16[20,512,256]{2,1,0:T(8,128)(2,1)S(1)}, bf16[20,512,256]{2,1,0:T(8,128)(2,1)}, u32[]{:S(2)}) copy-start(bf16[20,512,256]{2,1,0:T(8,128)(2,1)} %copy-done) | copy-start | bytes 15728644
  34.3 8.2 %copy-start.5 = (bf16[20,512,256]{2,1,0:T(8,128)(2,1)S(1)}, bf16[20,512,256]{2,1,0:T(8,128)(2,1)}, u32[]{:S(2)}) copy-start(bf16[20,512,256]{2,1,0:T(8,128)(2,1)} %copy-done.3) | copy-start | bytes 15728644
  38.0 4.5 %collective-permute-start.2 = (f32[4,8,128]{2,1,0:T(8,128)S(1)}, f32[4,8,128]{2,1,0:T(8,128)S(1)}, u32[]{:S(2)}, u32[]{:S(2)}) collective-permute-start(f32[4,8,128]{2,1,0:T(8,128)S(1)} %get-tuple-element.44), channel_id=1, source_target_pairs={{0,1},{1,0},{2,3},{3,2},{4,5},{5,4},{6,7},{7,6},{8,9},{9,8},{10,11... | collective-permute-start | bytes 49160 | tf_op jit(solution)/shard_map/ppermute | solution.py:474
  46.2 4.6 %collective-permute-start.3 = (f32[4,8,128]{2,1,0:T(8,128)S(1)}, f32[4,8,128]{2,1,0:T(8,128)S(1)}, u32[]{:S(2)}, u32[]{:S(2)}) collective-permute-start(f32[4,8,128]{2,1,0:T(8,128)S(1)} %get-tuple-element.48), channel_id=1, source_target_pairs={{0,1},{1,0},{2,3},{3,2},{4,5},{5,4},{6,7},{7,6},{8,9},{9,8},{10,11... | collective-permute-start | bytes 49160 | tf_op jit(solution)/shard_map/ppermute | solution.py:474
  54.5 4.8 %collective-permute-start.4 = (f32[4,8,128]{2,1,0:T(8,128)S(1)}, f32[4,8,128]{2,1,0:T(8,128)S(1)}, u32[]{:S(2)}, u32[]{:S(2)}) collective-permute-start(f32[4,8,128]{2,1,0:T(8,128)S(1)} %get-tuple-element.52), channel_id=1, source_target_pairs={{0,1},{1,0},{2,3},{3,2},{4,5},{5,4},{6,7},{7,6},{8,9},{9,8},{10,11... | collective-permute-start | bytes 49160 | tf_op jit(solution)/shard_map/ppermute | solution.py:474
  63.0 4.7 %collective-permute-start.5 = (f32[4,8,128]{2,1,0:T(8,128)S(1)}, f32[4,8,128]{2,1,0:T(8,128)S(1)}, u32[]{:S(2)}, u32[]{:S(2)}) collective-permute-start(f32[4,8,128]{2,1,0:T(8,128)S(1)} %get-tuple-element.56), channel_id=1, source_target_pairs={{0,1},{1,0},{2,3},{3,2},{4,5},{5,4},{6,7},{7,6},{8,9},{9,8},{10,11... | collective-permute-start | bytes 49160 | tf_op jit(solution)/shard_map/ppermute | solution.py:474
  71.3 4.8 %collective-permute-start.6 = (f32[4,8,128]{2,1,0:T(8,128)S(1)}, f32[4,8,128]{2,1,0:T(8,128)S(1)}, u32[]{:S(2)}, u32[]{:S(2)}) collective-permute-start(f32[4,8,128]{2,1,0:T(8,128)S(1)} %get-tuple-element.60), channel_id=1, source_target_pairs={{0,1},{1,0},{2,3},{3,2},{4,5},{5,4},{6,7},{7,6},{8,9},{9,8},{10,11... | collective-permute-start | bytes 49160 | tf_op jit(solution)/shard_map/ppermute | solution.py:474

commit v2 on v1

--- a/solution.py
+++ b/solution.py
@@ -49,41 +49,144 @@
     low_ref[pair, rows, cols] = low
 
 
-def prep_kernel(depth, margin, info, blocks, rhs, diag, offs, start, even, odd, sems):
+def prep_kernel(depth, margin, info, blocks, rhs, diag, offs, start, scaled, even, odd, rhs_buf, diag_buf, offs_buf, sems):
     rows = diag.shape[0]
     parity = info[0]
-    copies = []
-    for place, (ref, at) in enumerate(((even, 1 - parity), (odd, parity))):
+    sides = ((even, 1 - parity), (odd, parity))
+    copies = [
+        pltpu.make_async_copy(rhs, rhs_buf, sems.at[0]),
+        pltpu.make_async_copy(diag, diag_buf, sems.at[1]),
+        pltpu.make_async_copy(offs, offs_buf, sems.at[2]),
+    ]
+    for place, (ref, at) in enumerate(sides):
         first = pl.multiple_of(at * (rows - margin) * 512, 512)
         copies.append(
             pltpu.make_async_copy(
                 blocks.at[pl.ds(first, margin * 512)],
                 ref.at[pl.ds(0, margin * 512)],
-                sems.at[place],
+                sems.at[3 + place],
             )
         )
-        copies[-1].start()
+    for copy in copies:
+        copy.start()
+    for copy in copies[:3]:
+        copy.wait()
     for i in range(rows):
-        part = rhs[:, i * 128 : (i + 1) * 128]
+        part = rhs_buf[:, i * 128 : (i + 1) * 128]
         start[i] = jnp.concatenate([part, part], 0)
-    fill = jnp.zeros((margin, 124), F32)
-    for ref, at in ((even, 1 - parity), (odd, parity)):
+        scaled[i] = diag_buf[i : i + 1, :] * SCALE
+    places = offs_buf[...].astype(F32)
+    places = jnp.concatenate([places, jnp.zeros((4, 128 - rows), F32)], 1)
+    for ref, at in sides:
         base = margin * 512
         for i in range(depth):
             ref[base + 8 * i : base + 8 * i + 8, :] = start[at * (rows - depth) + i]
         base += 8 * depth
-        is_high = at == 1
-        diag_part = jnp.where(is_high, diag[rows - margin :, :], diag[:margin, :])
-        offs_part = jnp.where(is_high, offs[rows - margin :, :], offs[:margin, :]).astype(F32)
-        ref[base : base + margin, :] = diag_part
-        ref[base + margin : base + 2 * margin, :] = jnp.concatenate([offs_part, fill], 1)
-        if margin % 4:
-            ref[base + 2 * margin : base + 8, :] = jnp.zeros((8 - 2 * margin, 128), F32)
-    for copy in copies:
+        ref[base : base + 4, :] = places
+        own = jnp.where(at == 1, diag_buf[rows - margin :, :], diag_buf[:margin, :])
+        ref[base + 4 : base + 4 + margin, :] = own
+        if margin < 4:
+            ref[base + 4 + margin : base + 8, :] = jnp.zeros((4 - margin, 128), F32)
+    for copy in copies[3:]:
         copy.wait()
 
 
-def convert_kernel(slots, blocks, high, low, buf, sems):
+def take_message(depth, margin, rows, parity, even, odd, high, low, scaled, places, halo):
+    for ref, side in ((even, 1 - parity), (odd, parity)):
+        for m in range(margin):
+            for k in range(4):
+                first = (m * 4 + k) * 128
+                store_pair(
+                    ref[first : first + 128, :], high, low, side * (margin // 2) + m // 2, m % 2, k
+                )
+        base = margin * 512
+        for i in range(depth):
+            halo[side, i] = ref[base + 8 * i : base + 8 * i + 8, :]
+        base += 8 * depth
+        for m in range(margin):
+            scaled[side * margin + m] = ref[base + 4 + m : base + 5 + m, :] * SCALE
+            for k in range(4):
+                line = ref[base + k : base + k + 1, :]
+                at_left, at_right = rows - margin + m, m
+                one = jnp.where(
+                    side == 0, line[:, at_left : at_left + 1], line[:, at_right : at_right + 1]
+                )
+                places[(side * margin + m) * 4 + k] = jnp.broadcast_to(one, (8, 128))
+
+
+class Chain:
+    def __init__(self, rows, margin, steps, shifts, offs, high, low, scaled, halo_parts=None):
+        self.rows, self.margin, self.steps, self.shifts = rows, margin, steps, shifts
+        self.offs, self.high, self.low, self.scaled = offs, high, low, scaled
+        self.halo_parts = halo_parts
+        self.mask = halves()
+
+    def halo_at(self, row):
+        return row + self.margin if row < 0 else self.margin + row - self.rows
+
+    def mats(self, row):
+        if 0 <= row < self.rows:
+            return self.high[row // 2], self.low[row // 2]
+        at = self.halo_at(row) // 2
+        return self.halo_parts[0][at], self.halo_parts[1][at]
+
+    def diagonal(self, row):
+        if 0 <= row < self.rows:
+            return self.scaled[row]
+        return self.halo_parts[2][self.halo_at(row)]
+
+    def gather(self, source, reach, row, k):
+        if 0 <= row < self.rows:
+            return source[self.offs[k, row] + (row + reach)]
+        place = self.halo_parts[3][self.halo_at(row) * 4 + k]
+        total = jnp.zeros((8, 128), F32)
+        for c in range(-W, W + 1):
+            total = jnp.where(place == c, source[row + c + reach], total)
+        return total
+
+    def run(self, plan, values, known, splits, store):
+        for step in range(self.steps):
+            source, reach = splits[step], W * (self.steps - step)
+            needed = {row + c for first in plan[step] for row in (first, first + 1) for c in range(-W, W + 1)}
+            for row in sorted(needed & set(known[step])):
+                source[row + reach] = split(values(step, row), self.mask)
+            streamed = []
+            for row in plan[step]:
+                parts = []
+                for k in range(4):
+                    tiles = [self.gather(source, reach, row + h, k) for h in range(2)]
+                    parts.append(jnp.concatenate(tiles, 0).astype(BF16))
+                streamed.append(jnp.concatenate(parts, 1))
+            sums = []
+            for row, left in zip(plan[step], streamed):
+                high, low = self.mats(row)
+                sums.append(
+                    jnp.dot(left, high, preferred_element_type=F32)
+                    + jnp.dot(left, low, preferred_element_type=F32)
+                )
+            for row, total in zip(plan[step], sums):
+                for h in range(2):
+                    at = row + h
+                    part = total[8 * h : 8 * h + 8, 128 * h : 128 * h + 128]
+                    part = part + pltpu.roll(part, 4, 0)
+                    tile = part + (self.diagonal(at) - SCALE * self.shifts[step]) * values(step, at)
+                    store(step, at, tile)
+                    if step < self.steps - 1:
+                        splits[step + 1][at + reach - W] = split(tile, self.mask)
+
+
+def inner_plan(rows, steps):
+    return [list(range(W * (j + 1), rows - W * (j + 1), 2)) for j in range(steps)]
+
+
+def whole_plan(rows, steps):
+    return [list(range(-W * (steps - 1 - j), rows + W * (steps - 1 - j), 2)) for j in range(steps)]
+
+
+def convert_kernel(slots, steps, shifts, *refs):
+    offs, blocks, scaled, start, high, low = refs[:6]
+    outs, splits = refs[6 : 6 + steps], refs[6 + steps : 6 + 2 * steps]
+    buf, sems = refs[6 + 2 * steps :]
     rows = blocks.shape[0] // 512
 
     def fetch(i, slot):
@@ -114,118 +217,96 @@
         return carry
 
     lax.fori_loop(0, rows // slots, body, 0)
-
-
-def halo_kernel(depth, margin, info, even, odd, diag, high, low, scaled, halo):
-    rows = diag.shape[0]
+    chain = Chain(rows, 0, steps, shifts, offs, high, low, scaled)
+    plan = inner_plan(rows, steps)
+
+    def values(step, row):
+        return start[row] if step == 0 else outs[step - 1][row]
+
+    def store(step, row, tile):
+        outs[step][row] = tile
+
+    chain.run(plan, values, [range(rows)] + [[]] * (steps - 1), splits, store)
+
+
+def send(parity, last, depth, to_even, to_odd):
+    rows = last.shape[0]
+    for i in range(depth):
+        to_even[i] = last[(1 - parity) * (rows - depth) + i]
+        to_odd[i] = last[parity * (rows - depth) + i]
+
+
+def first_kernel(steps, shifts, margin, next_depth, *refs):
+    refs = list(refs)
+    info, offs, even, odd, high, low, scaled, own = refs[:8]
+    del refs[:8]
+    begun, outs = refs[:steps], refs[steps + 4 : 2 * steps + 4]
+    parts = refs[steps : steps + 4]
+    del refs[: 2 * steps + 4]
+    to_even, to_odd = refs[:2]
+    splits, halo, inner = refs[2 : 2 + steps], refs[2 + steps], refs[3 + steps :]
+    rows = own.shape[0]
     parity = info[0]
-    for i in range(rows):
-        scaled[margin + i] = diag[i : i + 1, :] * SCALE
-    for ref, side in ((even, 1 - parity), (odd, parity)):
-        for m in range(margin):
-            for k in range(4):
-                first = (m * 4 + k) * 128
-                store_pair(
-                    ref[first : first + 128, :], high, low, side * (margin // 2) + m // 2, m % 2, k
-                )
-        base = margin * 512
-        for i in range(depth):
-            halo[side, i] = ref[base + 8 * i : base + 8 * i + 8, :]
-        base += 8 * depth
-        for m in range(margin):
-            scaled[side * (rows + margin) + m] = ref[base + m : base + m + 1, :] * SCALE
-
-
-def steps_kernel(first, steps, shifts, margin, next_depth, *refs):
+    take_message(W * steps, margin, rows, parity, even, odd, *parts, halo)
+    chain = Chain(rows, margin, steps, shifts, offs, high, low, scaled, parts)
+    before, whole = inner_plan(rows, steps), whole_plan(rows, steps)
+    plan = [[row for row in w if row not in b] for b, w in zip(before, whole)]
+    done = [[row + h for row in b for h in range(2)] for b in before]
+    for j in range(steps):
+        for row in done[j]:
+            outs[j][row] = begun[j][row]
+    values, store = vector_access(rows, steps, own, outs, halo, inner)
+    known = [range(-W * steps, rows + W * steps)] + done[:-1]
+    chain.run(plan, values, known, splits, store)
+    send(parity, outs[-1], next_depth, to_even, to_odd)
+
+
+def vector_access(rows, steps, own, outs, halo, inner):
+    depth = W * steps
+
+    def values(step, row):
+        if 0 <= row < rows:
+            return own[row] if step == 0 else outs[step - 1][row]
+        if step == 0:
+            return halo[0, row + depth] if row < 0 else halo[1, row - rows]
+        keep = W * (steps - step)
+        return inner[step - 1][row + keep if row < 0 else keep + row - rows]
+
+    def store(step, row, tile):
+        if 0 <= row < rows:
+            outs[step][row] = tile
+        else:
+            keep = W * (steps - 1 - step)
+            inner[step][row + keep if row < 0 else keep + row - rows] = tile
+
+    return values, store
+
+
+def steps_kernel(steps, shifts, margin, next_depth, *refs):
     refs = list(refs)
-    info, offs, high, low, halo_high, halo_low, scaled, own = refs[:8]
-    del refs[:8]
-    depth = W * steps
-    if first:
-        halo = refs.pop(0)
-    else:
-        from_even, from_odd = refs[:2]
-        del refs[:2]
+    info, offs, high, low, scaled, own = refs[:6]
+    parts = refs[6:10]
+    from_even, from_odd = refs[10:12]
+    del refs[:12]
     outs = refs[:steps]
     del refs[:steps]
     if next_depth:
         to_even, to_odd = refs[:2]
         del refs[:2]
-    splits = refs[:steps]
-    del refs[:steps]
-    if not first:
-        halo = refs.pop(0)
-    inner = refs
+    splits, halo, inner = refs[:steps], refs[steps], refs[steps + 1 :]
     rows = own.shape[0]
-    parity = info[0]
-    mask = halves()
-    if not first:
-        there = info[1] == 1
-        for i in range(depth):
-            halo[1 - parity, i] = from_even[i]
-            tile = from_odd[parity, i]
-            halo[parity, i] = jnp.where(there, tile, jnp.zeros_like(tile))
+    depth = W * steps
+    parity, there = info[0], info[1] == 1
     for i in range(depth):
-        splits[0][i] = split(halo[0, i], mask)
-        splits[0][depth + rows + i] = split(halo[1, i], mask)
-    for i in range(rows):
-        splits[0][depth + i] = split(own[i], mask)
-
-    def value(step, row):
-        if 0 <= row < rows:
-            return own[row] if step == 0 else outs[step - 1][row]
-        if step == 0:
-            return halo[0, row + depth] if row < 0 else halo[1, row - rows]
-        keep = W * (steps - step)
-        ref = inner[step - 1]
-        return ref[row + keep] if row < 0 else ref[keep + row - rows]
-
-    for step in range(steps):
-        keep = W * (steps - 1 - step)
-        reach = keep + W
-        source = splits[step]
-        pairs = list(range(-keep, rows + keep, 2))
-        streamed = []
-        for row in pairs:
-            parts = []
-            for k in range(4):
-                tiles = [
-                    source[offs[(row + h + margin) * 4 + k] + (row + h + reach)] for h in range(2)
-                ]
-                parts.append(jnp.concatenate(tiles, 0).astype(BF16))
-            streamed.append(jnp.concatenate(parts, 1))
-        sums = []
-        for row, left in zip(pairs, streamed):
-            if row < 0:
-                mats = halo_high[(row + margin) // 2], halo_low[(row + margin) // 2]
-            elif row >= rows:
-                at = margin // 2 + (row - rows) // 2
-                mats = halo_high[at], halo_low[at]
-            else:
-                mats = high[row // 2], low[row // 2]
-            sums.append(
-                jnp.dot(left, mats[0], preferred_element_type=F32)
-                + jnp.dot(left, mats[1], preferred_element_type=F32)
-            )
-        for row, total in zip(pairs, sums):
-            for h in range(2):
-                at = row + h
-                part = total[8 * h : 8 * h + 8, 128 * h : 128 * h + 128]
-                part = part + pltpu.roll(part, 4, 0)
-                tile = part + (scaled[at + margin] - SCALE * shifts[step]) * value(step, at)
-                if 0 <= at < rows:
-                    outs[step][at] = tile
-                elif at < 0:
-                    inner[step][at + keep] = tile
-                else:
-                    inner[step][keep + at - rows] = tile
-                if step < steps - 1:
-                    splits[step + 1][at + keep] = split(tile, mask)
+        halo[1 - parity, i] = from_even[i]
+        tile = from_odd[parity, i]
+        halo[parity, i] = jnp.where(there, tile, jnp.zeros_like(tile))
+    chain = Chain(rows, margin, steps, shifts, offs, high, low, scaled, parts)
+    values, store = vector_access(rows, steps, own, outs, halo, inner)
+    known = [range(-depth, rows + depth)] + [[]] * (steps - 1)
+    chain.run(whole_plan(rows, steps), values, known, splits, store)
     if next_depth:
-        last = outs[-1]
-        for i in range(next_depth):
-            to_even[i] = last[(1 - parity) * (rows - next_depth) + i]
-            to_odd[i] = last[parity * (rows - next_depth) + i]
+        send(parity, outs[-1], next_depth, to_even, to_odd)
 
 
 def pair_list():
@@ -389,19 +470,30 @@
     linked = jnp.logical_and(me > 0, me < count - 1)
     info = jnp.stack([parity, linked.astype(jnp.int32)])
     margin = W * (max(GROUPS) - 1)
-    depth = W * GROUPS[0]
-    flat = blocks.reshape(rows * per_row * size, size)
+    steps = GROUPS[0]
+    depth, next_depth = W * steps, W * GROUPS[1]
+    flat = pltpu.with_memory_space_constraint(blocks.reshape(rows * per_row * size, size), pltpu.HBM)
+    offs = offsets.T
     diag = diag_shift.reshape(rows, size)
-    message = shape(margin * 512 + 8 * depth + -(-2 * margin // 8) * 8, size)
-    start, even, odd = pl.pallas_call(
+    message = shape(margin * 512 + 8 * depth + 8, size)
+    start, scaled, even, odd = pl.pallas_call(
         functools.partial(prep_kernel, depth, margin),
-        out_shape=[shape(rows, 8, size), message, message],
-        in_specs=[SM, HB, VM, VM, VM],
-        out_specs=[VM] * 3,
-        scratch_shapes=[pltpu.SemaphoreType.DMA((2,))],
+        out_shape=[shape(rows, 8, size), shape(rows, 1, size), message, message],
+        in_specs=[SM, HB, HB, HB, HB],
+        out_specs=[VM] * 4,
+        scratch_shapes=[
+            pltpu.VMEM(right_side.shape, F32),
+            pltpu.VMEM(diag.shape, F32),
+            pltpu.VMEM(offs.shape, jnp.int32),
+            pltpu.SemaphoreType.DMA((5,)),
+        ],
         compiler_params=params(8),
         name="prepare",
-    )(info, flat, right_side, diag, offsets)
+    )(
+        info,
+        flat,
+        *[pltpu.with_memory_space_constraint(x, pltpu.HBM) for x in (right_side, diag, offs)],
+    )
 
     swap_even = [(i, i ^ 1) for i in range(count)]
     swap_odd = [(i, i + 1) for i in range(1, count - 1, 2)]
@@ -417,62 +509,60 @@
     odd = lax.ppermute(odd, "dom", swap_odd)
     even = lax.ppermute(even, "dom", swap_even)
 
-    pair_shape = shape(rows // 2, per_row * size, 2 * size, kind=BF16)
-    high, low = pl.pallas_call(
-        functools.partial(convert_kernel, 4),
-        out_shape=[pair_shape] * 2,
-        in_specs=[HB],
-        out_specs=[VM] * 2,
-        scratch_shapes=[pltpu.VMEM((4, per_row * size, size), F32), pltpu.SemaphoreType.DMA((4,))],
+    vector = shape(rows, 8, size)
+    pair_shape = pltpu.VMEM((rows // 2, per_row * size, 2 * size), BF16)
+    split_scratch = [pltpu.VMEM((rows + 2 * W * (steps - j), 8, size), F32) for j in range(steps)]
+    high, low, *begun = pl.pallas_call(
+        functools.partial(convert_kernel, 4, steps, SHIFTS[:steps]),
+        out_shape=[pair_shape] * 2 + [vector] * steps,
+        in_specs=[SM, HB, VM, VM],
+        out_specs=[VM] * (2 + steps),
+        scratch_shapes=split_scratch
+        + [pltpu.VMEM((4, per_row * size, size), F32), pltpu.SemaphoreType.DMA((4,))],
         compiler_params=params(16),
         name="convert",
-    )(flat)
-
-    halo_shape = shape(margin, per_row * size, 2 * size, kind=BF16)
-    halo_high, halo_low, scaled, halo = pl.pallas_call(
-        functools.partial(halo_kernel, depth, margin),
-        out_shape=[halo_shape, halo_shape, shape(rows + 2 * margin, 1, size), shape(2, depth, 8, size)],
-        in_specs=[SM] + [VM] * 3,
-        out_specs=[VM] * 4,
-        compiler_params=params(8),
-        name="halo",
-    )(info, even, odd, diag)
-
-    at = margin * 512 + 8 * depth + margin
-    even_offs, odd_offs = even[at : at + margin, :per_row], odd[at : at + margin, :per_row]
-    left = jnp.where(parity == 0, odd_offs, even_offs).astype(jnp.int32)
-    right = jnp.where(parity == 0, even_offs, odd_offs).astype(jnp.int32)
-    all_offs = jnp.concatenate([left, offsets, right], 0).reshape(-1)
-
-    vectors = [start]
-    done = 0
-    for number, steps in enumerate(GROUPS):
-        first = number == 0
+    )(offs, flat, scaled, start)
+
+    halo_shape = pltpu.VMEM((margin, per_row * size, 2 * size), BF16)
+    results = pl.pallas_call(
+        functools.partial(first_kernel, steps, SHIFTS[:steps], margin, next_depth),
+        out_shape=[halo_shape, halo_shape, shape(2 * margin, 1, size), shape(8 * margin, 8, size)]
+        + [vector] * steps
+        + [shape(next_depth, 8, size)] * 2,
+        in_specs=[SM, SM] + [VM] * (6 + steps),
+        out_specs=[VM] * (6 + steps),
+        scratch_shapes=split_scratch
+        + [pltpu.VMEM((2, depth, 8, size), F32)]
+        + [pltpu.VMEM((2 * W * (steps - 1 - j), 8, size), F32) for j in range(steps - 1)],
+        compiler_params=params(16),
+        name="first",
+    )(info, offs, even, odd, high, low, scaled, start, *begun)
+    parts = results[:4]
+    vectors = [start, *results[4 : 4 + steps]]
+    even, odd = results[4 + steps :]
+    done = steps
+    for number, steps in enumerate(GROUPS[1:], 1):
+        even = lax.ppermute(even, "dom", swap_even)
+        odd = lax.all_gather(odd, axes, axis_index_groups=pairs)
         next_depth = W * GROUPS[number + 1] if number + 1 < len(GROUPS) else 0
-        depth = W * steps
-        outs = [shape(rows, 8, size)] * steps + [shape(next_depth, 8, size)] * (2 if next_depth else 0)
-        scratch = [pltpu.VMEM((rows + 2 * W * (steps - j), 8, size), F32) for j in range(steps)]
-        if not first:
-            scratch.append(pltpu.VMEM((2, depth, 8, size), F32))
-        scratch += [pltpu.VMEM((2 * W * (steps - 1 - j), 8, size), F32) for j in range(steps - 1)]
-        received = [halo] if first else [even, odd]
+        outs = [vector] * steps + [shape(next_depth, 8, size)] * (2 if next_depth else 0)
         results = pl.pallas_call(
             functools.partial(
-                steps_kernel, first, steps, [SHIFTS[(done + j) % S] for j in range(steps)], margin, next_depth
+                steps_kernel, steps, [SHIFTS[(done + j) % S] for j in range(steps)], margin, next_depth
             ),
             out_shape=outs,
-            in_specs=[SM, SM] + [VM] * (6 + len(received)),
+            in_specs=[SM, SM] + [VM] * 10,
             out_specs=[VM] * len(outs),
-            scratch_shapes=scratch,
+            scratch_shapes=[pltpu.VMEM((rows + 2 * W * (steps - j), 8, size), F32) for j in range(steps)]
+            + [pltpu.VMEM((2, W * steps, 8, size), F32)]
+            + [pltpu.VMEM((2 * W * (steps - 1 - j), 8, size), F32) for j in range(steps - 1)],
             compiler_params=params(16),
             name="steps",
-        )(info, all_offs, high, low, halo_high, halo_low, scaled, vectors[-1], *received)
+        )(info, offs, high, low, scaled, vectors[-1], *parts, even, odd)
         vectors += results[:steps]
         done += steps
         if next_depth:
             even, odd = results[steps:]
-            even = lax.ppermute(even, "dom", swap_even)
-            odd = lax.all_gather(odd, axes, axis_index_groups=pairs)
 
     gram = pl.pallas_call(
         gram_kernel,

time: 94.8 us -> 80.2 us (0.85)
  local copies, waits for them, and re-layouts: 20.5 us -> 0.01 us
  Pallas kernels: 31.9 us -> 37.9 us
    unnamed x25 -> x2, local copies, waits for them, and re-layouts: 20.1 us -> 0.01 us
    pallas_call x8 -> x7, Pallas kernels: 29.3 us -> 34.1 us  [the longest x5 18.5 us: local(): pl.pallas_call(functools.partial(steps_kernel, steps, [SHIFTS[(done + j)...]
    pallas_call x1, Pallas kernels: 0.66 us -> 1.86 us  [local(): pl.pallas_call(functools.partial(prep_kernel, depth, margin), out_shape=[...]
  transfers between devices with their start and end apart: 7 -> 7, of which waited for: 0 -> 0; matrix products, arithmetic and copies ran while one was open for 0% -> 0% of each run, Pallas kernels for 7% -> 17%
where the time goes in v2:
time: 80.2 us; the launch traced here: 79.7 us
  Pallas kernels  37.9 us (47%)
  blocking collectives  35.2 us (44%)
  starting transfers between devices  5.79 us (7%)
    all_gather x5, blocking collectives, local(): odd = lax.all_gather(odd, axes, axis_index_groups=pairs)  22.2 us
    pallas_call x5, Pallas kernels, local(): pl.pallas_call(functools.partial(steps_kernel, steps, [SHIFTS[(done + j)...  18.5 us
    pallas_call x1, Pallas kernels, local(): pl.pallas_call(functools.partial(convert_kernel, 4, steps, SHIFTS[:steps]...  13.8 us
    all_to_all x1, blocking collectives, local(): gram = lax.all_to_all(gram, 'dom', 0, 0)  13 us
    ppermute x6, starting transfers between devices, local(): even = lax.ppermute(even, 'dom', swap_even)  5.11 us
    pallas_call x1, Pallas kernels, local(): pl.pallas_call(functools.partial(prep_kernel, depth, margin), out_shape=[...  1.86 us
    pallas_call x1, Pallas kernels, local(): pl.pallas_call(functools.partial(first_kernel, steps, SHIFTS[:steps], mar...  1.77 us
  transfers between devices with their start and end apart: 7, of which 0 were waited for; matrix products, arithmetic and copies ran while one was open for 0% of the time, Pallas kernels for 17%

profile of v2, /device:TPU:0, one launch (start us, length us, event | category | flops | bytes accessed | tf_op | source)
XLA Modules:
  0.0 79.7 jit_solution(11727425930618703776)
XLA Ops:
  0.6 0.1 pad_add_fusion.info.refs_0_
  0.7 0.0 copy-start
  0.7 1.9 %prepare.1 = (f32[40,8,128]{2,1,0:T(8,128)S(1)}, f32[40,1,128]{2,1,0:T(1,128)S(1)}, f32[1064,128]{1,0:T(8,128)S(1)}, f32[1064,128]{1,0:T(8,128)S(1)}) custom-call(s32[2]{0:T(128)S(1)} %pad_add_fusion.info.refs_0_, f32[20480,128]{1,0:T(8,128)} %bitcast.23, f32[4,5120]{1,0:T(4,128)} %rhs.1, f32[40,128]{1,0:T(8,128)} %bitcast.25, s32[4,40]{1,0:T(4,128)} %bitcast.15), custom_call_target="tpu_custom_call" | custom-call | tf_op jit(solution)/shard_map/prepare/pallas_call | solution.py:479
  2.6 0.5 collective-permute-start
  3.1 0.7 collective-permute-start.1
  3.8 0.0 copy-done
  3.8 13.8 %convert.2 = (bf16[20,512,256]{2,1,0:T(8,128)(2,1)S(1)}, bf16[20,512,256]{2,1,0:T(8,128)(2,1)S(1)}, f32[40,8,128]{2,1,0:T(8,128)S(1)}, f32[40,8,128]{2,1,0:T(8,128)S(1)}) custom-call(s32[4,40]{1,0:T(4,128)S(1)} %bitcast.16, f32[20480,128]{1,0:T(8,128)} %bitcast.24, f32[40,1,128]{2,1,0:T(1,128)S(1)} %get-tuple-element.39.refs_2_.refs_6_.refs_4_, ...), custom_call_target="tpu_custom_call" | custom-call | tf_op jit(solution)/shard_map/convert/pallas_call | solution.py:515
  17.7 0.0 collective-permute-done.refs_2_
  17.7 0.0 collective-permute-done.1.refs_3_
  17.7 1.8 %first.1 = (bf16[2,512,256]{2,1,0:T(8,128)(2,1)S(1)}, bf16[2,512,256]{2,1,0:T(8,128)(2,1)S(1)}, f32[4,1,128]{2,1,0:T(1,128)S(1)}, f32[16,8,128]{2,1,0:T(8,128)S(...) custom-call(s32[2]{0:T(128)S(1)} %pad_add_fusion.info.refs_0_, ...), custom_call_target="tpu_custom_call" | custom-call | tf_op jit(solution)/shard_map/first/pallas_call | solution.py:527
  19.4 3.9 %collective-permute-start.2 = (f32[4,8,128]{2,1,0:T(8,128)S(1)}, f32[4,8,128]{2,1,0:T(8,128)S(1)}, u32[]{:S(2)}, u32[]{:S(2)}) collective-permute-start(f32[4,8,128]{2,1,0:T(8,128)S(1)} %get-tuple-element.50), channel_id=1, source_target_pairs={{0,1},{1,0},{2,3},{3,2},{4,5},{5,4},{6,7},{7,6},{8,9},{9,8},{10,11... | collective-permute-start | bytes 49160 | tf_op jit(solution)/shard_map/ppermute | solution.py:545
  23.4 4.4 %all-gather = f32[8,8,128]{2,1,0:T(8,128)S(1)} all-gather(f32[4,8,128]{2,1,0:T(8,128)S(1)} %get-tuple-element.51), channel_id=2, replica_groups={{1,2},{3,4},{5,6},{7,8},{9,10},{11,12},{13,14},{17,18},{19,20},{21,22},..., dimensions={0}, use_global_device_ids=true | all-gather | bytes 49152 | tf_op jit(solution)/shard_map/all_gather | solution.py:546
  27.8 0.0 collective-permute-done.2.refs_10_
  27.8 3.7 %steps.5 = (f32[40,8,128]{2,1,0:T(8,128)S(1)}, f32[40,8,128]{2,1,0:T(8,128)S(1)}, f32[4,8,128]{2,1,0:T(8,128)S(1)}, f32[4,8,128]{2,1,0:T(8,128)S(1)}) custom-call(s32[2]{0:T(128)S(1)} %pad_add_fusion.info.refs_0_, s32[4,40]{1,0:T(4,128)S(1)} %bitcast.18, bf16[20,512,256]{2,1,0:T(8,128)(2,1)S(1)} %get-tuple-element.40.refs_4_.refs_2_, ...), custom_call_target="tpu_custom_call" | custom-call | tf_op jit(solution)/shard_map/steps/pallas_call | solution.py:549
  31.5 0.1 collective-permute-start.3
  31.6 4.4 %all-gather.1 = f32[8,8,128]{2,1,0:T(8,128)S(1)} all-gather(f32[4,8,128]{2,1,0:T(8,128)S(1)} %get-tuple-element.55), channel_id=3, replica_groups={{1,2},{3,4},{5,6},{7,8},{9,10},{11,12},{13,14},{17,18},{19,20},{21,22},..., dimensions={0}, use_global_device_ids=true | all-gather | bytes 49152 | tf_op jit(solution)/shard_map/all_gather | solution.py:546
  36.0 0.0 collective-permute-done.3.refs_10_
  36.0 3.7 %steps.6 = (f32[40,8,128]{2,1,0:T(8,128)S(1)}, f32[40,8,128]{2,1,0:T(8,128)S(1)}, f32[4,8,128]{2,1,0:T(8,128)S(1)}, f32[4,8,128]{2,1,0:T(8,128)S(1)}) custom-call(s32[2]{0:T(128)S(1)} %pad_add_fusion.info.refs_0_, s32[4,40]{1,0:T(4,128)S(1)} %bitcast.19, bf16[20,512,256]{2,1,0:T(8,128)(2,1)S(1)} %get-tuple-element.40.refs_4_.refs_2_, ...), custom_call_target="tpu_custom_call" | custom-call | tf_op jit(solution)/shard_map/steps/pallas_call | solution.py:549
  39.7 0.2 collective-permute-start.4
  39.9 4.4 %all-gather.2 = f32[8,8,128]{2,1,0:T(8,128)S(1)} all-gather(f32[4,8,128]{2,1,0:T(8,128)S(1)} %get-tuple-element.59), channel_id=4, replica_groups={{1,2},{3,4},{5,6},{7,8},{9,10},{11,12},{13,14},{17,18},{19,20},{21,22},..., dimensions={0}, use_global_device_ids=true | all-gather | bytes 49152 | tf_op jit(solution)/shard_map/all_gather | solution.py:546
  44.3 0.0 collective-permute-done.4.refs_10_
  44.3 3.7 %steps.7 = (f32[40,8,128]{2,1,0:T(8,128)S(1)}, f32[40,8,128]{2,1,0:T(8,128)S(1)}, f32[4,8,128]{2,1,0:T(8,128)S(1)}, f32[4,8,128]{2,1,0:T(8,128)S(1)}) custom-call(s32[2]{0:T(128)S(1)} %pad_add_fusion.info.refs_0_, s32[4,40]{1,0:T(4,128)S(1)} %bitcast.20, bf16[20,512,256]{2,1,0:T(8,128)(2,1)S(1)} %get-tuple-element.40.refs_4_.refs_2_, ...), custom_call_target="tpu_custom_call" | custom-call | tf_op jit(solution)/shard_map/steps/pallas_call | solution.py:549
  48.0 0.2 collective-permute-start.5
  48.2 4.6 %all-gather.3 = f32[8,8,128]{2,1,0:T(8,128)S(1)} all-gather(f32[4,8,128]{2,1,0:T(8,128)S(1)} %get-tuple-element.63), channel_id=5, replica_groups={{1,2},{3,4},{5,6},{7,8},{9,10},{11,12},{13,14},{17,18},{19,20},{21,22},..., dimensions={0}, use_global_device_ids=true | all-gather | bytes 49152 | tf_op jit(solution)/shard_map/all_gather | solution.py:546
  52.8 0.0 collective-permute-done.5.refs_10_
  52.8 3.7 %steps.8 = (f32[40,8,128]{2,1,0:T(8,128)S(1)}, f32[40,8,128]{2,1,0:T(8,128)S(1)}, f32[4,8,128]{2,1,0:T(8,128)S(1)}, f32[4,8,128]{2,1,0:T(8,128)S(1)}) custom-call(s32[2]{0:T(128)S(1)} %pad_add_fusion.info.refs_0_, s32[4,40]{1,0:T(4,128)S(1)} %bitcast.21, bf16[20,512,256]{2,1,0:T(8,128)(2,1)S(1)} %get-tuple-element.40.refs_4_.refs_2_, ...), custom_call_target="tpu_custom_call" | custom-call | tf_op jit(solution)/shard_map/steps/pallas_call | solution.py:549
  56.5 0.2 collective-permute-start.6
  56.7 4.4 %all-gather.4 = f32[8,8,128]{2,1,0:T(8,128)S(1)} all-gather(f32[4,8,128]{2,1,0:T(8,128)S(1)} %get-tuple-element.67), channel_id=6, replica_groups={{1,2},{3,4},{5,6},{7,8},{9,10},{11,12},{13,14},{17,18},{19,20},{21,22},..., dimensions={0}, use_global_device_ids=true | all-gather | bytes 49152 | tf_op jit(solution)/shard_map/all_gather | solution.py:546
  61.1 0.0 collective-permute-done.6.refs_10_
  61.1 3.7 %steps.9 = (f32[40,8,128]{2,1,0:T(8,128)S(1)}, f32[40,8,128]{2,1,0:T(8,128)S(1)}) custom-call(s32[2]{0:T(128)S(1)} %pad_add_fusion.info.refs_0_, s32[4,40]{1,0:T(4,128)S(1)} %bitcast.22, bf16[20,512,256]{2,1,0:T(8,128)(2,1)S(1)} %get-tuple-element.40.refs_4_.refs_2_, bf16[20,512,256]{2,1,0:T(8,128)(2,1)S(1)} %get-tuple-element.41.refs_5_.refs_3_, ...), custom_call_target="tpu_custom_call" | custom-call | tf_op jit(solution)/shard_map/steps/pallas_call | solution.py:549
  64.8 0.6 gram.1
  65.4 13.0 %all_to_all.5.grams = f32[16,8,128]{2,1,0:T(8,128)S(1)} all-to-all(f32[16,8,128]{2,1,0:T(8,128)S(1)} %gram.1), channel_id=1, replica_groups=mesh['groups'=2,'dom'=16] {'dom'}, dimensions={0} | all-to-all | bytes 131072 | tf_op jit(solution)/shard_map/all_to_all | solution.py:575
  78.4 1.3 %finish.1 = (f32[4,5120]{1,0:T(4,128)}, f32[4,5120]{1,0:T(4,128)}) custom-call(f32[16,8,128]{2,1,0:T(8,128)S(1)} %all_to_all.5.grams, f32[40,8,128]{2,1,0:T(8,128)S(1)} %get-tuple-element.36.refs_3_.refs_7_.refs_0_, f32[40,8,128]{2,1,0:T(8,128)S(1)} %get-tuple-element.44.refs_1_, f32[40,8,128]{2,1,0:T(8,128)S(1)} %get-tuple-element.45.refs_5_.refs_2_, ...), custom_call_target="tpu_custom_call" | custom-call | tf_op jit(solution)/shard_map/finish/pallas_call | solution.py:577
Async XLA Ops:
  0.7 3.1 %copy-start = (s32[40,4]{0,1:T(4,128)S(1)}, s32[40,4]{0,1:T(4,128)}, u32[]{:S(2)}) copy-start(s32[40,4]{0,1:T(4,128)} %param.5) | copy-start | bytes 1924
  2.6 15.1 %collective-permute-start = (f32[1064,128]{1,0:T(8,128)S(1)}, f32[1064,128]{1,0:T(8,128)S(1)}, u32[]{:S(2)}, u32[]{:S(2)}) collective-permute-start(f32[1064,128]{1,0:T(8,128)S(1)} %get-tuple-element.37), channel_id=1, source_target_pairs={{0,1},{1,0},{2,3},{3,2},{4,5},{5,4},{6,7},{7,6},{8,9},{9,8},{10,11... | collective-permute-start | bytes 1634312 | tf_op jit(solution)/shard_map/ppermute | solution.py:510
  3.1 14.6 %collective-permute-start.1 = (f32[1064,128]{1,0:T(8,128)S(1)}, f32[1064,128]{1,0:T(8,128)S(1)}, u32[]{:S(2)}, u32[]{:S(2)}) collective-permute-start(f32[1064,128]{1,0:T(8,128)S(1)} %get-tuple-element.38), channel_id=1, source_target_pairs={{1,2},{3,4},{5,6},{7,8},{9,10},{11,12},{13,14},{2,1},{4,3},{6,5},{... | collective-permute-start | bytes 1634312 | tf_op jit(solution)/shard_map/ppermute | solution.py:509
  19.4 8.3 %collective-permute-start.2 = (f32[4,8,128]{2,1,0:T(8,128)S(1)}, f32[4,8,128]{2,1,0:T(8,128)S(1)}, u32[]{:S(2)}, u32[]{:S(2)}) collective-permute-start(f32[4,8,128]{2,1,0:T(8,128)S(1)} %get-tuple-element.50), channel_id=1, source_target_pairs={{0,1},{1,0},{2,3},{3,2},{4,5},{5,4},{6,7},{7,6},{8,9},{9,8},{10,11... | collective-permute-start | bytes 49160 | tf_op jit(solution)/shard_map/ppermute | solution.py:545
  31.5 4.5 %collective-permute-start.3 = (f32[4,8,128]{2,1,0:T(8,128)S(1)}, f32[4,8,128]{2,1,0:T(8,128)S(1)}, u32[]{:S(2)}, u32[]{:S(2)}) collective-permute-start(f32[4,8,128]{2,1,0:T(8,128)S(1)} %get-tuple-element.54), channel_id=1, source_target_pairs={{0,1},{1,0},{2,3},{3,2},{4,5},{5,4},{6,7},{7,6},{8,9},{9,8},{10,11... | collective-permute-start | bytes 49160 | tf_op jit(solution)/shard_map/ppermute | solution.py:545
  39.7 4.6 %collective-permute-start.4 = (f32[4,8,128]{2,1,0:T(8,128)S(1)}, f32[4,8,128]{2,1,0:T(8,128)S(1)}, u32[]{:S(2)}, u32[]{:S(2)}) collective-permute-start(f32[4,8,128]{2,1,0:T(8,128)S(1)} %get-tuple-element.58), channel_id=1, source_target_pairs={{0,1},{1,0},{2,3},{3,2},{4,5},{5,4},{6,7},{7,6},{8,9},{9,8},{10,11... | collective-permute-start | bytes 49160 | tf_op jit(solution)/shard_map/ppermute | solution.py:545
  48.0 4.8 %collective-permute-start.5 = (f32[4,8,128]{2,1,0:T(8,128)S(1)}, f32[4,8,128]{2,1,0:T(8,128)S(1)}, u32[]{:S(2)}, u32[]{:S(2)}) collective-permute-start(f32[4,8,128]{2,1,0:T(8,128)S(1)} %get-tuple-element.62), channel_id=1, source_target_pairs={{0,1},{1,0},{2,3},{3,2},{4,5},{5,4},{6,7},{7,6},{8,9},{9,8},{10,11... | collective-permute-start | bytes 49160 | tf_op jit(solution)/shard_map/ppermute | solution.py:545
  56.5 4.6 %collective-permute-start.6 = (f32[4,8,128]{2,1,0:T(8,128)S(1)}, f32[4,8,128]{2,1,0:T(8,128)S(1)}, u32[]{:S(2)}, u32[]{:S(2)}) collective-permute-start(f32[4,8,128]{2,1,0:T(8,128)S(1)} %get-tuple-element.66), channel_id=1, source_target_pairs={{0,1},{1,0},{2,3},{3,2},{4,5},{5,4},{6,7},{7,6},{8,9},{9,8},{10,11... | collective-permute-start | bytes 49160 | tf_op jit(solution)/shard_map/ppermute | solution.py:545

commit v3 on v2

--- a/solution.py
+++ b/solution.py
@@ -14,6 +14,8 @@
 CYCLES = 2
 CHAIN = S * CYCLES
 GROUPS = (2, 2, 2, 2, 2, 2)
+AHEAD = 4
+INNER_SECOND = False
 SCALE = 0.125
 GROW = 1.0 / SCALE
 SHIFTS = [
@@ -41,15 +43,15 @@
 
 
 def store_pair(block, high_ref, low_ref, pair, half, k):
-    turned = block.T * SCALE
-    high = turned.astype(BF16)
-    low = (turned - high.astype(F32)).astype(BF16)
+    block = block * SCALE
+    high = block.astype(BF16)
+    low = (block - high.astype(F32)).astype(BF16)
     rows, cols = slice(k * 128, (k + 1) * 128), slice(half * 128, (half + 1) * 128)
-    high_ref[pair, rows, cols] = high
-    low_ref[pair, rows, cols] = low
-
-
-def prep_kernel(depth, margin, info, blocks, rhs, diag, offs, start, scaled, even, odd, rhs_buf, diag_buf, offs_buf, sems):
+    high_ref[pair, rows, cols] = high.T
+    low_ref[pair, rows, cols] = low.T
+
+
+def prep_kernel(depth, margin, info, blocks, rhs, diag, offs, even, odd, rhs_buf, diag_buf, offs_buf, sems):
     rows = diag.shape[0]
     parity = info[0]
     sides = ((even, 1 - parity), (odd, parity))
@@ -71,16 +73,14 @@
         copy.start()
     for copy in copies[:3]:
         copy.wait()
-    for i in range(rows):
-        part = rhs_buf[:, i * 128 : (i + 1) * 128]
-        start[i] = jnp.concatenate([part, part], 0)
-        scaled[i] = diag_buf[i : i + 1, :] * SCALE
     places = offs_buf[...].astype(F32)
     places = jnp.concatenate([places, jnp.zeros((4, 128 - rows), F32)], 1)
     for ref, at in sides:
         base = margin * 512
         for i in range(depth):
-            ref[base + 8 * i : base + 8 * i + 8, :] = start[at * (rows - depth) + i]
+            low, top = i * 128, (rows - depth + i) * 128
+            part = jnp.where(at == 1, rhs_buf[:, top : top + 128], rhs_buf[:, low : low + 128])
+            ref[base + 8 * i : base + 8 * i + 8, :] = jnp.concatenate([part, part], 0)
         base += 8 * depth
         ref[base : base + 4, :] = places
         own = jnp.where(at == 1, diag_buf[rows - margin :, :], diag_buf[:margin, :])
@@ -175,93 +175,25 @@
                         splits[step + 1][at + reach - W] = split(tile, self.mask)
 
 
-def inner_plan(rows, steps):
-    return [list(range(W * (j + 1), rows - W * (j + 1), 2)) for j in range(steps)]
-
-
-def whole_plan(rows, steps):
-    return [list(range(-W * (steps - 1 - j), rows + W * (steps - 1 - j), 2)) for j in range(steps)]
-
-
-def convert_kernel(slots, steps, shifts, *refs):
-    offs, blocks, scaled, start, high, low = refs[:6]
-    outs, splits = refs[6 : 6 + steps], refs[6 + steps : 6 + 2 * steps]
-    buf, sems = refs[6 + 2 * steps :]
-    rows = blocks.shape[0] // 512
-
-    def fetch(i, slot):
-        first = pl.multiple_of(i * 512, 512)
-        return pltpu.make_async_copy(blocks.at[pl.ds(first, 512)], buf.at[slot], sems.at[slot])
-
-    for slot in range(slots):
-        fetch(slot, slot).start()
-
-    def body(q, carry):
-        for slot in range(slots):
-            i = q * slots + slot
-            fetch(i, slot).wait()
-            for k in range(4):
-                store_pair(
-                    buf[slot, k * 128 : (k + 1) * 128, :],
-                    high,
-                    low,
-                    q * (slots // 2) + slot // 2,
-                    slot % 2,
-                    k,
-                )
-
-            @pl.when(i + slots < rows)
-            def _():
-                fetch(i + slots, slot).start()
-
-        return carry
-
-    lax.fori_loop(0, rows // slots, body, 0)
-    chain = Chain(rows, 0, steps, shifts, offs, high, low, scaled)
-    plan = inner_plan(rows, steps)
-
-    def values(step, row):
-        return start[row] if step == 0 else outs[step - 1][row]
-
-    def store(step, row, tile):
-        outs[step][row] = tile
-
-    chain.run(plan, values, [range(rows)] + [[]] * (steps - 1), splits, store)
-
-
-def send(parity, last, depth, to_even, to_odd):
-    rows = last.shape[0]
-    for i in range(depth):
-        to_even[i] = last[(1 - parity) * (rows - depth) + i]
-        to_odd[i] = last[parity * (rows - depth) + i]
-
-
-def first_kernel(steps, shifts, margin, next_depth, *refs):
-    refs = list(refs)
-    info, offs, even, odd, high, low, scaled, own = refs[:8]
-    del refs[:8]
-    begun, outs = refs[:steps], refs[steps + 4 : 2 * steps + 4]
-    parts = refs[steps : steps + 4]
-    del refs[: 2 * steps + 4]
-    to_even, to_odd = refs[:2]
-    splits, halo, inner = refs[2 : 2 + steps], refs[2 + steps], refs[3 + steps :]
-    rows = own.shape[0]
-    parity = info[0]
-    take_message(W * steps, margin, rows, parity, even, odd, *parts, halo)
-    chain = Chain(rows, margin, steps, shifts, offs, high, low, scaled, parts)
-    before, whole = inner_plan(rows, steps), whole_plan(rows, steps)
-    plan = [[row for row in w if row not in b] for b, w in zip(before, whole)]
-    done = [[row + h for row in b for h in range(2)] for b in before]
-    for j in range(steps):
-        for row in done[j]:
-            outs[j][row] = begun[j][row]
-    values, store = vector_access(rows, steps, own, outs, halo, inner)
-    known = [range(-W * steps, rows + W * steps)] + done[:-1]
-    chain.run(plan, values, known, splits, store)
-    send(parity, outs[-1], next_depth, to_even, to_odd)
-
-
-def vector_access(rows, steps, own, outs, halo, inner):
+def inner_rows(rows, step):
+    return list(range(W * step, rows - W * step)) if rows > 2 * W * step else []
+
+
+def without(rows, done):
+    return [row for row in rows[::2] if row not in set(done)]
+
+
+def whole_rows(rows, steps, step):
+    return list(range(-W * (steps - step), rows + W * (steps - step)))
+
+
+def copy_rows(begun, outs, done):
+    for old, new, rows in zip(begun, outs, done):
+        for row in rows:
+            new[row] = old[row]
+
+
+def vector_access(rows, steps, own, outs, halo=None, inner=None):
     depth = W * steps
 
     def values(step, row):
@@ -282,12 +214,60 @@
     return values, store
 
 
-def steps_kernel(steps, shifts, margin, next_depth, *refs):
+def convert_kernel(steps, shifts, *refs):
+    offs, blocks, rhs, diag, start, scaled, high, low = refs[:8]
+    outs, splits = refs[8 : 8 + steps], refs[8 + steps : 8 + 2 * steps]
+    buf, sems = refs[8 + 2 * steps :]
+    rows = buf.shape[0]
+
+    def fetch(i):
+        first = pl.multiple_of(i * 512, 512)
+        return pltpu.make_async_copy(blocks.at[pl.ds(first, 512)], buf.at[i], sems.at[i])
+
+    for i in range(rows):
+        fetch(i).start()
+    for i in range(rows):
+        part = rhs[:, i * 128 : (i + 1) * 128]
+        start[i] = jnp.concatenate([part, part], 0)
+        scaled[i] = diag[i : i + 1, :] * SCALE
+
+    def body(p, carry):
+        for half in range(2):
+            i = 2 * p + half
+            fetch(i).wait()
+            for k in range(4):
+                store_pair(buf[i, k * 128 : (k + 1) * 128, :], high, low, p, half, k)
+        return carry
+
+    lax.fori_loop(0, rows // 2, body, 0)
+    chain = Chain(rows, 0, steps, shifts, offs, high, low, scaled)
+    plan = [without(inner_rows(rows, j + 1), []) for j in range(steps)]
+    values, store = vector_access(rows, steps, start, outs)
+    chain.run(plan, values, [range(rows)] + [[]] * (steps - 1), splits, store)
+
+
+def inner_kernel(steps, shifts, done, *refs):
+    offs, high, low, scaled, own = refs[:5]
+    begun = refs[5 : 5 + len(done)]
+    outs = refs[5 + len(done) : 5 + len(done) + steps]
+    splits = refs[5 + len(done) + steps :]
+    rows = own.shape[0]
+    copy_rows(begun, outs, done)
+    done = list(done) + [[]] * (steps - len(done))
+    chain = Chain(rows, 0, steps, shifts, offs, high, low, scaled)
+    plan = [without(inner_rows(rows, j + 1), done[j]) for j in range(steps)]
+    values, store = vector_access(rows, steps, own, outs)
+    chain.run(plan, values, [range(rows)] + done[:-1], splits, store)
+
+
+def rest_kernel(first, steps, shifts, margin, done, next_depth, *refs):
     refs = list(refs)
-    info, offs, high, low, scaled, own = refs[:6]
-    parts = refs[6:10]
-    from_even, from_odd = refs[10:12]
-    del refs[:12]
+    info, offs, high, low, scaled, own, from_even, from_odd = refs[:8]
+    del refs[:8]
+    begun = refs[:steps]
+    del refs[:steps]
+    parts = refs[:4]
+    del refs[:4]
     outs = refs[:steps]
     del refs[:steps]
     if next_depth:
@@ -296,17 +276,24 @@
     splits, halo, inner = refs[:steps], refs[steps], refs[steps + 1 :]
     rows = own.shape[0]
     depth = W * steps
-    parity, there = info[0], info[1] == 1
-    for i in range(depth):
-        halo[1 - parity, i] = from_even[i]
-        tile = from_odd[parity, i]
-        halo[parity, i] = jnp.where(there, tile, jnp.zeros_like(tile))
+    parity = info[0]
+    if first:
+        take_message(depth, margin, rows, parity, from_even, from_odd, *parts, halo)
+    else:
+        for i in range(depth):
+            halo[1 - parity, i] = from_even[i]
+            halo[parity, i] = from_odd[i]
+    copy_rows(begun, outs, done)
     chain = Chain(rows, margin, steps, shifts, offs, high, low, scaled, parts)
+    plan = [without(whole_rows(rows, steps, j + 1), done[j]) for j in range(steps)]
     values, store = vector_access(rows, steps, own, outs, halo, inner)
-    known = [range(-depth, rows + depth)] + [[]] * (steps - 1)
-    chain.run(whole_plan(rows, steps), values, known, splits, store)
+    known = [range(-depth, rows + depth)] + list(done[:-1])
+    chain.run(plan, values, known, splits, store)
     if next_depth:
-        send(parity, outs[-1], next_depth, to_even, to_odd)
+        last = outs[-1]
+        for i in range(next_depth):
+            to_even[i] = last[(1 - parity) * (rows - next_depth) + i]
+            to_odd[i] = last[parity * (rows - next_depth) + i]
 
 
 def pair_list():
@@ -341,8 +328,7 @@
             total = products if total is None else [a + b for a, b in zip(total, products)]
         for pair, one in zip(pairs, total):
             tile = jnp.where(lane == PLACES[pair], jnp.sum(one, axis=1, keepdims=True), tile)
-    for d in range(out.shape[0]):
-        out[d] = tile
+    out[...] = tile + pltpu.roll(tile, 4, 0)
 
 
 def small_solve(gram):
@@ -385,16 +371,11 @@
     return coeffs, combine
 
 
-def final_kernel(grams, *refs):
+def final_kernel(total_gram, *refs):
     vectors, solution_ref, residual_ref = refs[:-2], refs[-2], refs[-1]
     count = vectors[0].shape[0] // 2
     mask = halves()
-    parts = [grams[d] for d in range(grams.shape[0])]
-    while len(parts) > 1:
-        parts = [a + b for a, b in zip(parts[::2], parts[1::2])] + (
-            parts[-1:] if len(parts) % 2 else []
-        )
-    tile = parts[0] + pltpu.roll(parts[0], 4, 0)
+    tile = total_gram[...]
     gram = {
         pair: jnp.broadcast_to(tile[:, at : at + 1], (8, 128)) for pair, at in PLACES.items()
     }
@@ -461,26 +442,27 @@
     return jax.ShapeDtypeStruct(dims, kind)
 
 
+def cost(block_rows):
+    return pl.CostEstimate(flops=block_rows * 2**21, bytes_accessed=block_rows * 2**18, transcendentals=0)
+
+
 def local(blocks, offsets, diag_shift, right_side):
     rhs_count = right_side.shape[0]
     rows, per_row, size = blocks.shape[0], blocks.shape[1], blocks.shape[2]
-    count, copies = lax.axis_size("dom"), lax.axis_size("groups")
-    me = lax.axis_index("dom")
-    parity = me % 2
-    linked = jnp.logical_and(me > 0, me < count - 1)
-    info = jnp.stack([parity, linked.astype(jnp.int32)])
+    count = lax.axis_size("dom")
+    info = (lax.axis_index("dom") % 2).reshape(1)
     margin = W * (max(GROUPS) - 1)
     steps = GROUPS[0]
-    depth, next_depth = W * steps, W * GROUPS[1]
+    depth = W * steps
     flat = pltpu.with_memory_space_constraint(blocks.reshape(rows * per_row * size, size), pltpu.HBM)
     offs = offsets.T
     diag = diag_shift.reshape(rows, size)
     message = shape(margin * 512 + 8 * depth + 8, size)
-    start, scaled, even, odd = pl.pallas_call(
+    even, odd = pl.pallas_call(
         functools.partial(prep_kernel, depth, margin),
-        out_shape=[shape(rows, 8, size), shape(rows, 1, size), message, message],
+        out_shape=[message, message],
         in_specs=[SM, HB, HB, HB, HB],
-        out_specs=[VM] * 4,
+        out_specs=[VM] * 2,
         scratch_shapes=[
             pltpu.VMEM(right_side.shape, F32),
             pltpu.VMEM(diag.shape, F32),
@@ -498,81 +480,91 @@
     swap_even = [(i, i ^ 1) for i in range(count)]
     swap_odd = [(i, i + 1) for i in range(1, count - 1, 2)]
     swap_odd = swap_odd + [(b, a) for a, b in swap_odd]
-    if copies % 2:
-        axes, pairs = "dom", [[i, (i + 1) % count] for i in range(1, count, 2)]
-    else:
-        axes = ("groups", "dom")
-        pairs = [[g * count + i, g * count + i + 1] for g in range(copies) for i in range(1, count - 1, 2)]
-        for g in range(0, copies, 2):
-            pairs += [[g * count + e, (g + 1) * count + e] for e in (0, count - 1)]
-
-    odd = lax.ppermute(odd, "dom", swap_odd)
-    even = lax.ppermute(even, "dom", swap_even)
+
+    def exchange(even, odd):
+        odd = lax.ppermute(odd, "dom", swap_odd)
+        return lax.ppermute(even, "dom", swap_even), odd
+
+    even, odd = exchange(even, odd)
 
     vector = shape(rows, 8, size)
     pair_shape = pltpu.VMEM((rows // 2, per_row * size, 2 * size), BF16)
-    split_scratch = [pltpu.VMEM((rows + 2 * W * (steps - j), 8, size), F32) for j in range(steps)]
-    high, low, *begun = pl.pallas_call(
-        functools.partial(convert_kernel, 4, steps, SHIFTS[:steps]),
-        out_shape=[pair_shape] * 2 + [vector] * steps,
+
+    def buffers(steps):
+        return [pltpu.VMEM((rows + 2 * W * (steps - j), 8, size), F32) for j in range(steps)]
+
+    started = [inner_rows(rows, j + 1) for j in range(AHEAD)]
+    start, scaled, high, low, *ahead = pl.pallas_call(
+        functools.partial(convert_kernel, AHEAD, [SHIFTS[j % S] for j in range(AHEAD)]),
+        out_shape=[vector, shape(rows, 1, size)] + [pair_shape] * 2 + [vector] * AHEAD,
         in_specs=[SM, HB, VM, VM],
-        out_specs=[VM] * (2 + steps),
-        scratch_shapes=split_scratch
-        + [pltpu.VMEM((4, per_row * size, size), F32), pltpu.SemaphoreType.DMA((4,))],
-        compiler_params=params(16),
+        out_specs=[VM] * (4 + AHEAD),
+        scratch_shapes=buffers(AHEAD)
+        + [pltpu.VMEM((rows, per_row * size, size), F32), pltpu.SemaphoreType.DMA((rows,))],
+        compiler_params=params(24),
+        cost_estimate=cost(2 * rows + sum(len(r) for r in started)),
         name="convert",
-    )(offs, flat, scaled, start)
-
+    )(offs, flat, right_side, diag)
+
+    vectors = [start]
     halo_shape = pltpu.VMEM((margin, per_row * size, 2 * size), BF16)
-    results = pl.pallas_call(
-        functools.partial(first_kernel, steps, SHIFTS[:steps], margin, next_depth),
-        out_shape=[halo_shape, halo_shape, shape(2 * margin, 1, size), shape(8 * margin, 8, size)]
-        + [vector] * steps
-        + [shape(next_depth, 8, size)] * 2,
-        in_specs=[SM, SM] + [VM] * (6 + steps),
-        out_specs=[VM] * (6 + steps),
-        scratch_shapes=split_scratch
-        + [pltpu.VMEM((2, depth, 8, size), F32)]
-        + [pltpu.VMEM((2 * W * (steps - 1 - j), 8, size), F32) for j in range(steps - 1)],
-        compiler_params=params(16),
-        name="first",
-    )(info, offs, even, odd, high, low, scaled, start, *begun)
-    parts = results[:4]
-    vectors = [start, *results[4 : 4 + steps]]
-    even, odd = results[4 + steps :]
-    done = steps
-    for number, steps in enumerate(GROUPS[1:], 1):
-        even = lax.ppermute(even, "dom", swap_even)
-        odd = lax.all_gather(odd, axes, axis_index_groups=pairs)
+    parts = None
+    at = 0
+    for number, steps in enumerate(GROUPS):
+        shifts = [SHIFTS[(at + j) % S] for j in range(steps)]
+        depth = W * steps
+        begun, done = ahead[at : at + steps], started[at : at + steps]
+        inner = [inner_rows(rows, j + 1) for j in range(steps)]
+        if done != inner and (number > 1 or INNER_SECOND or not begun):
+            begun = pl.pallas_call(
+                functools.partial(inner_kernel, steps, shifts, done),
+                out_shape=[vector] * steps,
+                in_specs=[SM] + [VM] * (4 + len(begun)),
+                out_specs=[VM] * steps,
+                scratch_shapes=buffers(steps),
+                compiler_params=params(16),
+                cost_estimate=cost(sum(len(r) for r in inner)),
+                name="inner",
+            )(offs, high, low, scaled, vectors[-1], *begun)
+            done = inner
         next_depth = W * GROUPS[number + 1] if number + 1 < len(GROUPS) else 0
+        first = number == 0
         outs = [vector] * steps + [shape(next_depth, 8, size)] * (2 if next_depth else 0)
+        if first:
+            outs = [halo_shape, halo_shape, shape(2 * margin, 1, size), shape(8 * margin, 8, size)] + outs
         results = pl.pallas_call(
-            functools.partial(
-                steps_kernel, steps, [SHIFTS[(done + j) % S] for j in range(steps)], margin, next_depth
-            ),
+            functools.partial(rest_kernel, first, steps, shifts, margin, done, next_depth),
             out_shape=outs,
-            in_specs=[SM, SM] + [VM] * 10,
+            in_specs=[SM, SM] + [VM] * (6 + steps + (0 if first else 4)),
             out_specs=[VM] * len(outs),
-            scratch_shapes=[pltpu.VMEM((rows + 2 * W * (steps - j), 8, size), F32) for j in range(steps)]
-            + [pltpu.VMEM((2, W * steps, 8, size), F32)]
+            scratch_shapes=buffers(steps)
+            + [pltpu.VMEM((2, depth, 8, size), F32)]
             + [pltpu.VMEM((2 * W * (steps - 1 - j), 8, size), F32) for j in range(steps - 1)],
             compiler_params=params(16),
-            name="steps",
-        )(info, offs, high, low, scaled, vectors[-1], *parts, even, odd)
+            cost_estimate=cost(16),
+            name="rest",
+        )(info, offs, high, low, scaled, vectors[-1], even, odd, *begun, *(parts or []))
+        results = list(results)
+        if first:
+            parts, results = results[:4], results[4:]
         vectors += results[:steps]
-        done += steps
+        at += steps
         if next_depth:
-            even, odd = results[steps:]
+            even, odd = exchange(*results[steps:])
 
     gram = pl.pallas_call(
         gram_kernel,
-        out_shape=shape(count, 8, size),
+        out_shape=shape(8, size),
         in_specs=[VM] * len(vectors),
         out_specs=VM,
         compiler_params=params(16),
         name="gram",
     )(*vectors)
-    gram = lax.all_to_all(gram, "dom", 0, 0)
+    if count & (count - 1):
+        gram = lax.psum(gram, "dom")
+    else:
+        for stage in range(count.bit_length() - 1):
+            gram = gram + lax.ppermute(gram, "dom", [(i, i ^ (1 << stage)) for i in range(count)])
     return tuple(
         pl.pallas_call(
             final_kernel,

time: 80.2 us -> 77.5 us (0.966)
  blocking collectives: 35.2 us -> 0 us
  starting transfers between devices: 5.79 us -> 32.6 us
  waiting for transfers between devices: 0.02 us -> 7.32 us
  Pallas kernels: 37.9 us -> 36.4 us
    ppermute x7 -> x16, starting transfers between devices: 5.79 us -> 32.6 us  [the longest x6 20.4 us: exchange(): return (lax.ppermute(even, 'dom', swap_even), odd)]
    all_gather x5 -> x0, blocking collectives: 22.2 us -> none  [local(): odd = lax.all_gather(odd, axes, axis_index_groups=pairs)]
    all_to_all x1 -> x0, blocking collectives: 13 us -> none  [local(): gram = lax.all_to_all(gram, 'dom', 0, 0)]
    ppermute x7 -> x16, waiting for transfers between devices: 0.02 us -> 7.32 us  [the longest x4 7.1 us: local(): lax.ppermute(gram, 'dom', [(i, i ^ 1 << stage) for i in range(count)])]
    pallas_call x8 -> x12, Pallas kernels: 34.7 us -> 33.7 us  [the longest x4 12.5 us: local(): pl.pallas_call(functools.partial(inner_kernel, steps, shifts, done), out_...]
  transfers between devices with their start and end apart: 7 -> 16, of which waited for: 0 -> 5; matrix products, arithmetic and copies ran while one was open for 0% -> 0% of each run, Pallas kernels for 17% -> 31%
where the time goes in v3:
time: 77.5 us; the launch traced here: 77.2 us
  Pallas kernels  36.4 us (47%)
  starting transfers between devices  32.6 us (42%)
  waiting for transfers between devices  7.32 us (9%)
  between operations  0.85 us (1%)
    ppermute x6, starting transfers between devices, exchange(): return (lax.ppermute(even, 'dom', swap_even), odd)  20.4 us
    pallas_call x4, Pallas kernels, local(): pl.pallas_call(functools.partial(inner_kernel, steps, shifts, done), out_...  12.5 us
    pallas_call x1, Pallas kernels, local(): pl.pallas_call(functools.partial(convert_kernel, AHEAD, [SHIFTS[j % S] fo...  11.5 us
    pallas_call x6, Pallas kernels, local(): pl.pallas_call(functools.partial(rest_kernel, first, steps, shifts, margi...  9.12 us
    ppermute x4, starting transfers between devices, local(): lax.ppermute(gram, 'dom', [(i, i ^ 1 << stage) for i in range(count)])  8.36 us
    ppermute x4, waiting for transfers between devices, local(): lax.ppermute(gram, 'dom', [(i, i ^ 1 << stage) for i in range(count)])  7.1 us
    ppermute x6, starting transfers between devices, exchange(): odd = lax.ppermute(odd, 'dom', swap_odd)  3.93 us
  transfers between devices with their start and end apart: 16, of which 5 were waited for; matrix products, arithmetic and copies ran while one was open for 0% of the time, Pallas kernels for 31%

profile of v3, /device:TPU:0, one launch (start us, length us, event | category | flops | bytes accessed | tf_op | source)
XLA Modules:
  0.0 77.2 jit_solution(15115271613417129992)
XLA Ops:
  0.6 0.0 copy-start
  0.7 0.0 copy-start.1
  0.7 0.0 copy-start.2
  0.7 1.4 %prepare.1 = (f32[1064,128]{1,0:T(8,128)S(1)}, f32[1064,128]{1,0:T(8,128)S(1)}) custom-call(s32[1]{0:T(128)} %bitcast.3.info.refs_0_, f32[20480,128]{1,0:T(8,128)} %bitcast.18, f32[4,5120]{1,0:T(4,128)} %rhs.1, f32[40,128]{1,0:T(8,128)} %bitcast.16, s32[4,40]{1,0:T(4,128)} %bitcast.4), custom_call_target="tpu_custom_call" | custom-call | tf_op jit(solution)/shard_map/prepare/pallas_call | solution.py:461
  2.0 0.5 collective-permute-start
  2.6 0.7 collective-permute-start.1
  3.2 0.0 copy-done
  3.3 0.0 copy-done.1
  3.3 0.0 copy-done.2
  3.3 11.5 %convert.1 = (f32[40,8,128]{2,1,0:T(8,128)S(1)}, f32[40,1,128]{2,1,0:T(1,128)S(1)}, bf16[20,512,256]{2,1,0:T(8,128)(2,1)S(1)}, bf16[20,512,256]{2,1,0:T(8,128)(2...) custom-call(s32[4,40]{1,0:T(4,128)S(1)} %bitcast.5, ...), custom_call_target="tpu_custom_call" | custom-call | flops 419430400 | bytes 52428800 | tf_op jit(solution)/shard_map/convert/pallas_call | solution.py:497
  14.8 0.0 collective-permute-done.refs_6_
  14.8 0.0 collective-permute-done.1.refs_7_
  14.8 1.8 %rest.6 = (bf16[2,512,256]{2,1,0:T(8,128)(2,1)S(1)}, bf16[2,512,256]{2,1,0:T(8,128)(2,1)S(1)}, f32[4,1,128]{2,1,0:T(1,128)S(1)}, f32[16,8,128]{2,1,0:T(8,128)S(1...) custom-call(s32[1]{0:T(128)} %bitcast.3.info.refs_0_, ...), custom_call_target="tpu_custom_call" | custom-call | flops 33554432 | bytes 4194304 | tf_op jit(solution)/shard_map/rest/pallas_call | solution.py:535
  16.6 4.5 %collective-permute-start.2 = (f32[4,8,128]{2,1,0:T(8,128)S(1)}, f32[4,8,128]{2,1,0:T(8,128)S(1)}, u32[]{:S(2)}, u32[]{:S(2)}) collective-permute-start(f32[4,8,128]{2,1,0:T(8,128)S(1)} %get-tuple-element.56), channel_id=1, source_target_pairs={{0,1},{1,0},{2,3},{3,2},{4,5},{5,4},{6,7},{7,6},{8,9},{9,8},{10,11... | collective-permute-start | bytes 49160 | tf_op jit(solution)/shard_map/ppermute | solution.py:486
  21.1 0.7 collective-permute-start.3
  21.7 0.2 collective-permute-done.2.refs_6_
  21.9 0.0 collective-permute-done.3.refs_7_
  21.9 1.9 %rest.7 = (f32[40,8,128]{2,1,0:T(8,128)S(1)}, f32[40,8,128]{2,1,0:T(8,128)S(1)}, f32[4,8,128]{2,1,0:T(8,128)S(1)}, f32[4,8,128]{2,1,0:T(8,128)S(1)}) custom-call(s32[1]{0:T(128)} %bitcast.3.info.refs_0_, s32[4,40]{1,0:T(4,128)S(1)} %bitcast.7, bf16[20,512,256]{2,1,0:T(8,128)(2,1)S(1)} %get-tuple-element.47.refs_2_.refs_1_, ...), custom_call_target="tpu_custom_call" | custom-call | flops 33554432 | bytes 4194304 | tf_op jit(solution)/shard_map/rest/pallas_call | solution.py:535
  23.8 5.0 %collective-permute-start.4 = (f32[4,8,128]{2,1,0:T(8,128)S(1)}, f32[4,8,128]{2,1,0:T(8,128)S(1)}, u32[]{:S(2)}, u32[]{:S(2)}) collective-permute-start(f32[4,8,128]{2,1,0:T(8,128)S(1)} %get-tuple-element.66), channel_id=1, source_target_pairs={{0,1},{1,0},{2,3},{3,2},{4,5},{5,4},{6,7},{7,6},{8,9},{9,8},{10,11... | collective-permute-start | bytes 49160 | tf_op jit(solution)/shard_map/ppermute | solution.py:486
  28.9 0.7 collective-permute-start.5
  29.5 3.1 %inner.4 = (f32[40,8,128]{2,1,0:T(8,128)S(1)}, f32[40,8,128]{2,1,0:T(8,128)S(1)}) custom-call(s32[4,40]{1,0:T(4,128)S(1)} %bitcast.8, bf16[20,512,256]{2,1,0:T(8,128)(2,1)S(1)} %get-tuple-element.47.refs_2_.refs_1_, bf16[20,512,256]{2,1,0:T(8,128)(2,1)S(1)} %get-tuple-element.48.refs_3_.refs_2_, f32[40,1,128]{2,1,0:T(1,128)S(1)} %get-tuple-element.49.refs_4_.refs_3_, ...), custom_call_target="tpu_custom_call" | custom-call | flops 142606336 | bytes 17825792 | tf_op jit(solution)/shard_map/inner/pallas_call | solution.py:519
  32.6 0.0 collective-permute-done.4.refs_6_
  32.7 0.0 collective-permute-done.5.refs_7_
  32.7 1.4 %rest.8 = (f32[40,8,128]{2,1,0:T(8,128)S(1)}, f32[40,8,128]{2,1,0:T(8,128)S(1)}, f32[4,8,128]{2,1,0:T(8,128)S(1)}, f32[4,8,128]{2,1,0:T(8,128)S(1)}) custom-call(s32[1]{0:T(128)} %bitcast.3.info.refs_0_, s32[4,40]{1,0:T(4,128)S(1)} %bitcast.9, bf16[20,512,256]{2,1,0:T(8,128)(2,1)S(1)} %get-tuple-element.47.refs_2_.refs_1_, ...), custom_call_target="tpu_custom_call" | custom-call | flops 33554432 | bytes 4194304 | tf_op jit(solution)/shard_map/rest/pallas_call | solution.py:535
  34.0 4.4 %collective-permute-start.6 = (f32[4,8,128]{2,1,0:T(8,128)S(1)}, f32[4,8,128]{2,1,0:T(8,128)S(1)}, u32[]{:S(2)}, u32[]{:S(2)}) collective-permute-start(f32[4,8,128]{2,1,0:T(8,128)S(1)} %get-tuple-element.72), channel_id=1, source_target_pairs={{0,1},{1,0},{2,3},{3,2},{4,5},{5,4},{6,7},{7,6},{8,9},{9,8},{10,11... | collective-permute-start | bytes 49160 | tf_op jit(solution)/shard_map/ppermute | solution.py:486
  38.5 0.7 collective-permute-start.7
  39.1 3.1 %inner.5 = (f32[40,8,128]{2,1,0:T(8,128)S(1)}, f32[40,8,128]{2,1,0:T(8,128)S(1)}) custom-call(s32[4,40]{1,0:T(4,128)S(1)} %bitcast.10, bf16[20,512,256]{2,1,0:T(8,128)(2,1)S(1)} %get-tuple-element.47.refs_2_.refs_1_, bf16[20,512,256]{2,1,0:T(8,128)(2,1)S(1)} %get-tuple-element.48.refs_3_.refs_2_, f32[40,1,128]{2,1,0:T(1,128)S(1)} %get-tuple-element.49.refs_4_.refs_3_, ...), custom_call_target="tpu_custom_call" | custom-call | flops 142606336 | bytes 17825792 | tf_op jit(solution)/shard_map/inner/pallas_call | solution.py:519
  42.2 0.0 collective-permute-done.6.refs_6_
  42.2 0.0 collective-permute-done.7.refs_7_
  42.3 1.4 %rest.9 = (f32[40,8,128]{2,1,0:T(8,128)S(1)}, f32[40,8,128]{2,1,0:T(8,128)S(1)}, f32[4,8,128]{2,1,0:T(8,128)S(1)}, f32[4,8,128]{2,1,0:T(8,128)S(1)}) custom-call(s32[1]{0:T(128)} %bitcast.3.info.refs_0_, s32[4,40]{1,0:T(4,128)S(1)} %bitcast.11, bf16[20,512,256]{2,1,0:T(8,128)(2,1)S(1)} %get-tuple-element.47.refs_2_.refs_1_, ...), custom_call_target="tpu_custom_call" | custom-call | flops 33554432 | bytes 4194304 | tf_op jit(solution)/shard_map/rest/pallas_call | solution.py:535
  43.6 2.9 %collective-permute-start.8 = (f32[4,8,128]{2,1,0:T(8,128)S(1)}, f32[4,8,128]{2,1,0:T(8,128)S(1)}, u32[]{:S(2)}, u32[]{:S(2)}) collective-permute-start(f32[4,8,128]{2,1,0:T(8,128)S(1)} %get-tuple-element.78), channel_id=1, source_target_pairs={{0,1},{1,0},{2,3},{3,2},{4,5},{5,4},{6,7},{7,6},{8,9},{9,8},{10,11... | collective-permute-start | bytes 49160 | tf_op jit(solution)/shard_map/ppermute | solution.py:486
  46.6 0.7 collective-permute-start.9
  47.2 3.1 %inner.6 = (f32[40,8,128]{2,1,0:T(8,128)S(1)}, f32[40,8,128]{2,1,0:T(8,128)S(1)}) custom-call(s32[4,40]{1,0:T(4,128)S(1)} %bitcast.12, bf16[20,512,256]{2,1,0:T(8,128)(2,1)S(1)} %get-tuple-element.47.refs_2_.refs_1_, bf16[20,512,256]{2,1,0:T(8,128)(2,1)S(1)} %get-tuple-element.48.refs_3_.refs_2_, f32[40,1,128]{2,1,0:T(1,128)S(1)} %get-tuple-element.49.refs_4_.refs_3_, ...), custom_call_target="tpu_custom_call" | custom-call | flops 142606336 | bytes 17825792 | tf_op jit(solution)/shard_map/inner/pallas_call | solution.py:519
  50.3 0.0 collective-permute-done.8.refs_6_
  50.4 0.0 collective-permute-done.9.refs_7_
  50.4 1.4 %rest.10 = (f32[40,8,128]{2,1,0:T(8,128)S(1)}, f32[40,8,128]{2,1,0:T(8,128)S(1)}, f32[4,8,128]{2,1,0:T(8,128)S(1)}, f32[4,8,128]{2,1,0:T(8,128)S(1)}) custom-call(s32[1]{0:T(128)} %bitcast.3.info.refs_0_, s32[4,40]{1,0:T(4,128)S(1)} %bitcast.13, bf16[20,512,256]{2,1,0:T(8,128)(2,1)S(1)} %get-tuple-element.47.refs_2_.refs_1_, ...), custom_call_target="tpu_custom_call" | custom-call | flops 33554432 | bytes 4194304 | tf_op jit(solution)/shard_map/rest/pallas_call | solution.py:535
  51.7 2.9 %collective-permute-start.10 = (f32[4,8,128]{2,1,0:T(8,128)S(1)}, f32[4,8,128]{2,1,0:T(8,128)S(1)}, u32[]{:S(2)}, u32[]{:S(2)}) collective-permute-start(f32[4,8,128]{2,1,0:T(8,128)S(1)} %get-tuple-element.84), channel_id=1, source_target_pairs={{0,1},{1,0},{2,3},{3,2},{4,5},{5,4},{6,7},{7,6},{8,9},{9,8},{10,11... | collective-permute-start | bytes 49160 | tf_op jit(solution)/shard_map/ppermute | solution.py:486
  54.7 0.7 collective-permute-start.11
  55.3 3.1 %inner.7 = (f32[40,8,128]{2,1,0:T(8,128)S(1)}, f32[40,8,128]{2,1,0:T(8,128)S(1)}) custom-call(s32[4,40]{1,0:T(4,128)S(1)} %bitcast.14, bf16[20,512,256]{2,1,0:T(8,128)(2,1)S(1)} %get-tuple-element.47.refs_2_.refs_1_, bf16[20,512,256]{2,1,0:T(8,128)(2,1)S(1)} %get-tuple-element.48.refs_3_.refs_2_, f32[40,1,128]{2,1,0:T(1,128)S(1)} %get-tuple-element.49.refs_4_.refs_3_, ...), custom_call_target="tpu_custom_call" | custom-call | flops 142606336 | bytes 17825792 | tf_op jit(solution)/shard_map/inner/pallas_call | solution.py:519
  58.5 0.0 collective-permute-done.10.refs_6_
  58.5 0.0 collective-permute-done.11.refs_7_
  58.5 1.4 %rest.11 = (f32[40,8,128]{2,1,0:T(8,128)S(1)}, f32[40,8,128]{2,1,0:T(8,128)S(1)}) custom-call(s32[1]{0:T(128)} %bitcast.3.info.refs_0_, s32[4,40]{1,0:T(4,128)S(1)} %bitcast.15, bf16[20,512,256]{2,1,0:T(8,128)(2,1)S(1)} %get-tuple-element.47.refs_2_.refs_1_, bf16[20,512,256]{2,1,0:T(8,128)(2,1)S(1)} %get-tuple-element.48.refs_3_.refs_2_, ...), custom_call_target="tpu_custom_call" | custom-call | flops 33554432 | bytes 4194304 | tf_op jit(solution)/shard_map/rest/pallas_call | solution.py:535
  59.8 0.6 gram.1
  60.5 2.9 %collective-permute-start.12 = (f32[8,128]{1,0:T(8,128)S(1)}, f32[8,128]{1,0:T(8,128)S(1)}, u32[]{:S(2)}, u32[]{:S(2)}) collective-permute-start(f32[8,128]{1,0:T(8,128)S(1)} %gram.1), channel_id=1, source_target_pairs={{0,1},{1,0},{2,3},{3,2},{4,5},{5,4},{6,7},{7,6},{8,9},{9,8},{10,11... | collective-permute-start | bytes 12296 | tf_op jit(solution)/shard_map/ppermute | solution.py:567
  63.4 0.8 %collective-permute-done.12 = f32[8,128]{1,0:T(8,128)S(1)} collective-permute-done((f32[8,128]{1,0:T(8,128)S(1)}, f32[8,128]{1,0:T(8,128)S(1)}, u32[]{:S(2)}, u32[]{:S(2)}) %collective-permute-start.12) | collective-permute-done | bytes 4128 | tf_op jit(solution)/shard_map/ppermute | solution.py:567
  64.2 1.5 %collective-permute-start.13 = (f32[8,128]{1,0:T(8,128)S(1)}, f32[8,128]{1,0:T(8,128)S(1)}, u32[]{:S(2)}, u32[]{:S(2)}) collective-permute-start(f32[8,128]{1,0:T(8,128)S(1)} %add.17), channel_id=1, source_target_pairs={{0,2},{1,3},{2,0},{3,1},{4,6},{5,7},{6,4},{7,5},{8,10},{9,11},{10,... | collective-permute-start | bytes 12296 | tf_op jit(solution)/shard_map/ppermute | solution.py:567
  65.7 2.1 %collective-permute-done.13 = f32[8,128]{1,0:T(8,128)S(1)} collective-permute-done((f32[8,128]{1,0:T(8,128)S(1)}, f32[8,128]{1,0:T(8,128)S(1)}, u32[]{:S(2)}, u32[]{:S(2)}) %collective-permute-start.13) | collective-permute-done | bytes 4128 | tf_op jit(solution)/shard_map/ppermute | solution.py:567
  67.8 1.6 %collective-permute-start.14 = (f32[8,128]{1,0:T(8,128)S(1)}, f32[8,128]{1,0:T(8,128)S(1)}, u32[]{:S(2)}, u32[]{:S(2)}) collective-permute-start(f32[8,128]{1,0:T(8,128)S(1)} %add.18), channel_id=1, source_target_pairs={{0,4},{1,5},{2,6},{3,7},{4,0},{5,1},{6,2},{7,3},{8,12},{9,13},{10,... | collective-permute-start | bytes 12296 | tf_op jit(solution)/shard_map/ppermute | solution.py:567
  69.4 2.0 %collective-permute-done.14 = f32[8,128]{1,0:T(8,128)S(1)} collective-permute-done((f32[8,128]{1,0:T(8,128)S(1)}, f32[8,128]{1,0:T(8,128)S(1)}, u32[]{:S(2)}, u32[]{:S(2)}) %collective-permute-start.14) | collective-permute-done | bytes 4128 | tf_op jit(solution)/shard_map/ppermute | solution.py:567
  71.4 2.3 %collective-permute-start.15 = (f32[8,128]{1,0:T(8,128)S(1)}, f32[8,128]{1,0:T(8,128)S(1)}, u32[]{:S(2)}, u32[]{:S(2)}) collective-permute-start(f32[8,128]{1,0:T(8,128)S(1)} %add.19), channel_id=1, source_target_pairs={{0,8},{1,9},{2,10},{3,11},{4,12},{5,13},{6,14},{7,15},{8,0},{9,1},... | collective-permute-start | bytes 12296 | tf_op jit(solution)/shard_map/ppermute | solution.py:567
  73.8 2.2 %collective-permute-done.15 = f32[8,128]{1,0:T(8,128)S(1)} collective-permute-done((f32[8,128]{1,0:T(8,128)S(1)}, f32[8,128]{1,0:T(8,128)S(1)}, u32[]{:S(2)}, u32[]{:S(2)}) %collective-permute-start.15) | collective-permute-done | bytes 4128 | tf_op jit(solution)/shard_map/ppermute | solution.py:567
  75.9 1.3 %finish.1 = (f32[4,5120]{1,0:T(4,128)}, f32[4,5120]{1,0:T(4,128)}) custom-call(f32[8,128]{1,0:T(8,128)S(1)} %add.20.total_gram, f32[40,8,128]{2,1,0:T(8,128)S(1)} %get-tuple-element.46.refs_5_.refs_0_, f32[40,8,128]{2,1,0:T(8,128)S(1)} %get-tuple-element.54.refs_1_, f32[40,8,128]{2,1,0:T(8,128)S(1)} %get-tuple-element.55.refs_5_.refs_2_, ...), custom_call_target="tpu_custom_call" | custom-call | tf_op jit(solution)/shard_map/finish/pallas_call | solution.py:569
  (4 shorter events, 0.0 us)
Async XLA Ops:
  0.6 2.6 %copy-start = (f32[4,5120]{1,0:T(4,128)S(1)}, f32[4,5120]{1,0:T(4,128)}, u32[]{:S(2)}) copy-start(f32[4,5120]{1,0:T(4,128)} %rhs.1) | copy-start | bytes 245764
  0.7 2.6 %copy-start.1 = (s32[40,4]{0,1:T(4,128)S(1)}, s32[40,4]{0,1:T(4,128)}, u32[]{:S(2)}) copy-start(s32[40,4]{0,1:T(4,128)} %param.5) | copy-start | bytes 1924
  0.7 2.6 %copy-start.2 = (f32[5120]{0:T(1024)S(1)}, f32[5120]{0:T(1024)}, u32[]{:S(2)}) copy-start(f32[5120]{0:T(1024)} %param.6) | copy-start | bytes 61444
  2.0 12.8 %collective-permute-start = (f32[1064,128]{1,0:T(8,128)S(1)}, f32[1064,128]{1,0:T(8,128)S(1)}, u32[]{:S(2)}, u32[]{:S(2)}) collective-permute-start(f32[1064,128]{1,0:T(8,128)S(1)} %get-tuple-element.50), channel_id=1, source_target_pairs={{0,1},{1,0},{2,3},{3,2},{4,5},{5,4},{6,7},{7,6},{8,9},{9,8},{10,11... | collective-permute-start | bytes 1634312 | tf_op jit(solution)/shard_map/ppermute | solution.py:486
  2.6 12.3 %collective-permute-start.1 = (f32[1064,128]{1,0:T(8,128)S(1)}, f32[1064,128]{1,0:T(8,128)S(1)}, u32[]{:S(2)}, u32[]{:S(2)}) collective-permute-start(f32[1064,128]{1,0:T(8,128)S(1)} %get-tuple-element.51), channel_id=1, source_target_pairs={{1,2},{3,4},{5,6},{7,8},{9,10},{11,12},{13,14},{2,1},{4,3},{6,5},{... | collective-permute-start | bytes 1634312 | tf_op jit(solution)/shard_map/ppermute | solution.py:485
  16.6 5.3 %collective-permute-start.2 = (f32[4,8,128]{2,1,0:T(8,128)S(1)}, f32[4,8,128]{2,1,0:T(8,128)S(1)}, u32[]{:S(2)}, u32[]{:S(2)}) collective-permute-start(f32[4,8,128]{2,1,0:T(8,128)S(1)} %get-tuple-element.56), channel_id=1, source_target_pairs={{0,1},{1,0},{2,3},{3,2},{4,5},{5,4},{6,7},{7,6},{8,9},{9,8},{10,11... | collective-permute-start | bytes 49160 | tf_op jit(solution)/shard_map/ppermute | solution.py:486
  21.1 0.8 %collective-permute-start.3 = (f32[4,8,128]{2,1,0:T(8,128)S(1)}, f32[4,8,128]{2,1,0:T(8,128)S(1)}, u32[]{:S(2)}, u32[]{:S(2)}) collective-permute-start(f32[4,8,128]{2,1,0:T(8,128)S(1)} %get-tuple-element.57), channel_id=1, source_target_pairs={{1,2},{3,4},{5,6},{7,8},{9,10},{11,12},{13,14},{2,1},{4,3},{6,5},{... | collective-permute-start | bytes 49160 | tf_op jit(solution)/shard_map/ppermute | solution.py:485
  23.8 8.8 %collective-permute-start.4 = (f32[4,8,128]{2,1,0:T(8,128)S(1)}, f32[4,8,128]{2,1,0:T(8,128)S(1)}, u32[]{:S(2)}, u32[]{:S(2)}) collective-permute-start(f32[4,8,128]{2,1,0:T(8,128)S(1)} %get-tuple-element.66), channel_id=1, source_target_pairs={{0,1},{1,0},{2,3},{3,2},{4,5},{5,4},{6,7},{7,6},{8,9},{9,8},{10,11... | collective-permute-start | bytes 49160 | tf_op jit(solution)/shard_map/ppermute | solution.py:486
  28.9 3.8 %collective-permute-start.5 = (f32[4,8,128]{2,1,0:T(8,128)S(1)}, f32[4,8,128]{2,1,0:T(8,128)S(1)}, u32[]{:S(2)}, u32[]{:S(2)}) collective-permute-start(f32[4,8,128]{2,1,0:T(8,128)S(1)} %get-tuple-element.67), channel_id=1, source_target_pairs={{1,2},{3,4},{5,6},{7,8},{9,10},{11,12},{13,14},{2,1},{4,3},{6,5},{... | collective-permute-start | bytes 49160 | tf_op jit(solution)/shard_map/ppermute | solution.py:485
  34.0 8.2 %collective-permute-start.6 = (f32[4,8,128]{2,1,0:T(8,128)S(1)}, f32[4,8,128]{2,1,0:T(8,128)S(1)}, u32[]{:S(2)}, u32[]{:S(2)}) collective-permute-start(f32[4,8,128]{2,1,0:T(8,128)S(1)} %get-tuple-element.72), channel_id=1, source_target_pairs={{0,1},{1,0},{2,3},{3,2},{4,5},{5,4},{6,7},{7,6},{8,9},{9,8},{10,11... | collective-permute-start | bytes 49160 | tf_op jit(solution)/shard_map/ppermute | solution.py:486
  38.5 3.8 %collective-permute-start.7 = (f32[4,8,128]{2,1,0:T(8,128)S(1)}, f32[4,8,128]{2,1,0:T(8,128)S(1)}, u32[]{:S(2)}, u32[]{:S(2)}) collective-permute-start(f32[4,8,128]{2,1,0:T(8,128)S(1)} %get-tuple-element.73), channel_id=1, source_target_pairs={{1,2},{3,4},{5,6},{7,8},{9,10},{11,12},{13,14},{2,1},{4,3},{6,5},{... | collective-permute-start | bytes 49160 | tf_op jit(solution)/shard_map/ppermute | solution.py:485
  43.6 6.7 %collective-permute-start.8 = (f32[4,8,128]{2,1,0:T(8,128)S(1)}, f32[4,8,128]{2,1,0:T(8,128)S(1)}, u32[]{:S(2)}, u32[]{:S(2)}) collective-permute-start(f32[4,8,128]{2,1,0:T(8,128)S(1)} %get-tuple-element.78), channel_id=1, source_target_pairs={{0,1},{1,0},{2,3},{3,2},{4,5},{5,4},{6,7},{7,6},{8,9},{9,8},{10,11... | collective-permute-start | bytes 49160 | tf_op jit(solution)/shard_map/ppermute | solution.py:486
  46.6 3.8 %collective-permute-start.9 = (f32[4,8,128]{2,1,0:T(8,128)S(1)}, f32[4,8,128]{2,1,0:T(8,128)S(1)}, u32[]{:S(2)}, u32[]{:S(2)}) collective-permute-start(f32[4,8,128]{2,1,0:T(8,128)S(1)} %get-tuple-element.79), channel_id=1, source_target_pairs={{1,2},{3,4},{5,6},{7,8},{9,10},{11,12},{13,14},{2,1},{4,3},{6,5},{... | collective-permute-start | bytes 49160 | tf_op jit(solution)/shard_map/ppermute | solution.py:485
  51.7 6.7 %collective-permute-start.10 = (f32[4,8,128]{2,1,0:T(8,128)S(1)}, f32[4,8,128]{2,1,0:T(8,128)S(1)}, u32[]{:S(2)}, u32[]{:S(2)}) collective-permute-start(f32[4,8,128]{2,1,0:T(8,128)S(1)} %get-tuple-element.84), channel_id=1, source_target_pairs={{0,1},{1,0},{2,3},{3,2},{4,5},{5,4},{6,7},{7,6},{8,9},{9,8},{10,11... | collective-permute-start | bytes 49160 | tf_op jit(solution)/shard_map/ppermute | solution.py:486
  54.7 3.8 %collective-permute-start.11 = (f32[4,8,128]{2,1,0:T(8,128)S(1)}, f32[4,8,128]{2,1,0:T(8,128)S(1)}, u32[]{:S(2)}, u32[]{:S(2)}) collective-permute-start(f32[4,8,128]{2,1,0:T(8,128)S(1)} %get-tuple-element.85), channel_id=1, source_target_pairs={{1,2},{3,4},{5,6},{7,8},{9,10},{11,12},{13,14},{2,1},{4,3},{6,5},{... | collective-permute-start | bytes 49160 | tf_op jit(solution)/shard_map/ppermute | solution.py:485
  60.5 3.7 %collective-permute-start.12 = (f32[8,128]{1,0:T(8,128)S(1)}, f32[8,128]{1,0:T(8,128)S(1)}, u32[]{:S(2)}, u32[]{:S(2)}) collective-permute-start(f32[8,128]{1,0:T(8,128)S(1)} %gram.1), channel_id=1, source_target_pairs={{0,1},{1,0},{2,3},{3,2},{4,5},{5,4},{6,7},{7,6},{8,9},{9,8},{10,11... | collective-permute-start | bytes 12296 | tf_op jit(solution)/shard_map/ppermute | solution.py:567
  64.2 3.6 %collective-permute-start.13 = (f32[8,128]{1,0:T(8,128)S(1)}, f32[8,128]{1,0:T(8,128)S(1)}, u32[]{:S(2)}, u32[]{:S(2)}) collective-permute-start(f32[8,128]{1,0:T(8,128)S(1)} %add.17), channel_id=1, source_target_pairs={{0,2},{1,3},{2,0},{3,1},{4,6},{5,7},{6,4},{7,5},{8,10},{9,11},{10,... | collective-permute-start | bytes 12296 | tf_op jit(solution)/shard_map/ppermute | solution.py:567
  67.8 3.6 %collective-permute-start.14 = (f32[8,128]{1,0:T(8,128)S(1)}, f32[8,128]{1,0:T(8,128)S(1)}, u32[]{:S(2)}, u32[]{:S(2)}) collective-permute-start(f32[8,128]{1,0:T(8,128)S(1)} %add.18), channel_id=1, source_target_pairs={{0,4},{1,5},{2,6},{3,7},{4,0},{5,1},{6,2},{7,3},{8,12},{9,13},{10,... | collective-permute-start | bytes 12296 | tf_op jit(solution)/shard_map/ppermute | solution.py:567
  71.4 4.5 %collective-permute-start.15 = (f32[8,128]{1,0:T(8,128)S(1)}, f32[8,128]{1,0:T(8,128)S(1)}, u32[]{:S(2)}, u32[]{:S(2)}) collective-permute-start(f32[8,128]{1,0:T(8,128)S(1)} %add.19), channel_id=1, source_target_pairs={{0,8},{1,9},{2,10},{3,11},{4,12},{5,13},{6,14},{7,15},{8,0},{9,1},... | collective-permute-start | bytes 12296 | tf_op jit(solution)/shard_map/ppermute | solution.py:567

commit v4 on v3

--- a/solution.py
+++ b/solution.py
@@ -25,7 +25,6 @@
 F32 = jnp.float32
 BF16 = jnp.bfloat16
 VM = pl.BlockSpec(memory_space=pltpu.VMEM)
-SM = pl.BlockSpec(memory_space=pltpu.SMEM)
 HB = pl.BlockSpec(memory_space=pltpu.HBM)
 
 
@@ -51,9 +50,9 @@
     low_ref[pair, rows, cols] = low.T
 
 
-def prep_kernel(depth, margin, info, blocks, rhs, diag, offs, even, odd, rhs_buf, diag_buf, offs_buf, sems):
+def prep_kernel(depth, margin, blocks, rhs, diag, offs, even, odd, rhs_buf, diag_buf, offs_buf, sems):
     rows = diag.shape[0]
-    parity = info[0]
+    parity = lax.axis_index("dom") % 2
     sides = ((even, 1 - parity), (odd, parity))
     copies = [
         pltpu.make_async_copy(rhs, rhs_buf, sems.at[0]),
@@ -105,19 +104,19 @@
         base += 8 * depth
         for m in range(margin):
             scaled[side * margin + m] = ref[base + 4 + m : base + 5 + m, :] * SCALE
-            for k in range(4):
+            for k in range(1, 4):
                 line = ref[base + k : base + k + 1, :]
                 at_left, at_right = rows - margin + m, m
                 one = jnp.where(
                     side == 0, line[:, at_left : at_left + 1], line[:, at_right : at_right + 1]
                 )
-                places[(side * margin + m) * 4 + k] = jnp.broadcast_to(one, (8, 128))
+                places[k - 1, side * margin + m] = jnp.broadcast_to(one, (1, 128))
 
 
 class Chain:
-    def __init__(self, rows, margin, steps, shifts, offs, high, low, scaled, halo_parts=None):
+    def __init__(self, rows, margin, steps, shifts, places, high, low, scaled, halo_parts=None):
         self.rows, self.margin, self.steps, self.shifts = rows, margin, steps, shifts
-        self.offs, self.high, self.low, self.scaled = offs, high, low, scaled
+        self.places, self.high, self.low, self.scaled = places, high, low, scaled
         self.halo_parts = halo_parts
         self.mask = halves()
 
@@ -136,11 +135,15 @@
         return self.halo_parts[2][self.halo_at(row)]
 
     def gather(self, source, reach, row, k):
+        if k == 0:
+            return source[row + reach]
         if 0 <= row < self.rows:
-            return source[self.offs[k, row] + (row + reach)]
-        place = self.halo_parts[3][self.halo_at(row) * 4 + k]
-        total = jnp.zeros((8, 128), F32)
-        for c in range(-W, W + 1):
+            place = self.places[k - 1, row]
+        else:
+            place = self.halo_parts[3][k - 1, self.halo_at(row)]
+        place = jnp.broadcast_to(place, (8, 128))
+        total = source[row + W + reach]
+        for c in (-W, 1 - W, W - 1):
             total = jnp.where(place == c, source[row + c + reach], total)
         return total
 
@@ -215,9 +218,9 @@
 
 
 def convert_kernel(steps, shifts, *refs):
-    offs, blocks, rhs, diag, start, scaled, high, low = refs[:8]
-    outs, splits = refs[8 : 8 + steps], refs[8 + steps : 8 + 2 * steps]
-    buf, sems = refs[8 + 2 * steps :]
+    blocks, rhs, diag, offs, start, scaled, places, high, low = refs[:9]
+    outs, splits = refs[9 : 9 + steps], refs[9 + steps : 9 + 2 * steps]
+    buf, sems = refs[9 + 2 * steps :]
     rows = buf.shape[0]
 
     def fetch(i):
@@ -230,6 +233,10 @@
         part = rhs[:, i * 128 : (i + 1) * 128]
         start[i] = jnp.concatenate([part, part], 0)
         scaled[i] = diag[i : i + 1, :] * SCALE
+    turned = jnp.concatenate([offs[...].astype(F32), jnp.zeros((4, 128 - rows), F32)], 1)
+    turned = jnp.concatenate([turned, jnp.zeros((4, 128), F32)], 0).T
+    for k in range(1, 4):
+        places[k - 1] = jnp.broadcast_to(turned[:rows, k : k + 1], (rows, 128)).reshape(rows, 1, 128)
 
     def body(p, carry):
         for half in range(2):
@@ -240,21 +247,21 @@
         return carry
 
     lax.fori_loop(0, rows // 2, body, 0)
-    chain = Chain(rows, 0, steps, shifts, offs, high, low, scaled)
+    chain = Chain(rows, 0, steps, shifts, places, high, low, scaled)
     plan = [without(inner_rows(rows, j + 1), []) for j in range(steps)]
     values, store = vector_access(rows, steps, start, outs)
     chain.run(plan, values, [range(rows)] + [[]] * (steps - 1), splits, store)
 
 
 def inner_kernel(steps, shifts, done, *refs):
-    offs, high, low, scaled, own = refs[:5]
+    places, high, low, scaled, own = refs[:5]
     begun = refs[5 : 5 + len(done)]
     outs = refs[5 + len(done) : 5 + len(done) + steps]
     splits = refs[5 + len(done) + steps :]
     rows = own.shape[0]
     copy_rows(begun, outs, done)
     done = list(done) + [[]] * (steps - len(done))
-    chain = Chain(rows, 0, steps, shifts, offs, high, low, scaled)
+    chain = Chain(rows, 0, steps, shifts, places, high, low, scaled)
     plan = [without(inner_rows(rows, j + 1), done[j]) for j in range(steps)]
     values, store = vector_access(rows, steps, own, outs)
     chain.run(plan, values, [range(rows)] + done[:-1], splits, store)
@@ -262,8 +269,8 @@
 
 def rest_kernel(first, steps, shifts, margin, done, next_depth, *refs):
     refs = list(refs)
-    info, offs, high, low, scaled, own, from_even, from_odd = refs[:8]
-    del refs[:8]
+    places, high, low, scaled, own, from_even, from_odd = refs[:7]
+    del refs[:7]
     begun = refs[:steps]
     del refs[:steps]
     parts = refs[:4]
@@ -276,7 +283,7 @@
     splits, halo, inner = refs[:steps], refs[steps], refs[steps + 1 :]
     rows = own.shape[0]
     depth = W * steps
-    parity = info[0]
+    parity = lax.axis_index("dom") % 2
     if first:
         take_message(depth, margin, rows, parity, from_even, from_odd, *parts, halo)
     else:
@@ -284,7 +291,7 @@
             halo[1 - parity, i] = from_even[i]
             halo[parity, i] = from_odd[i]
     copy_rows(begun, outs, done)
-    chain = Chain(rows, margin, steps, shifts, offs, high, low, scaled, parts)
+    chain = Chain(rows, margin, steps, shifts, places, high, low, scaled, parts)
     plan = [without(whole_rows(rows, steps, j + 1), done[j]) for j in range(steps)]
     values, store = vector_access(rows, steps, own, outs, halo, inner)
     known = [range(-depth, rows + depth)] + list(done[:-1])
@@ -450,7 +457,6 @@
     rhs_count = right_side.shape[0]
     rows, per_row, size = blocks.shape[0], blocks.shape[1], blocks.shape[2]
     count = lax.axis_size("dom")
-    info = (lax.axis_index("dom") % 2).reshape(1)
     margin = W * (max(GROUPS) - 1)
     steps = GROUPS[0]
     depth = W * steps
@@ -461,7 +467,7 @@
     even, odd = pl.pallas_call(
         functools.partial(prep_kernel, depth, margin),
         out_shape=[message, message],
-        in_specs=[SM, HB, HB, HB, HB],
+        in_specs=[HB, HB, HB, HB],
         out_specs=[VM] * 2,
         scratch_shapes=[
             pltpu.VMEM(right_side.shape, F32),
@@ -472,7 +478,6 @@
         compiler_params=params(8),
         name="prepare",
     )(
-        info,
         flat,
         *[pltpu.with_memory_space_constraint(x, pltpu.HBM) for x in (right_side, diag, offs)],
     )
@@ -494,17 +499,19 @@
         return [pltpu.VMEM((rows + 2 * W * (steps - j), 8, size), F32) for j in range(steps)]
 
     started = [inner_rows(rows, j + 1) for j in range(AHEAD)]
-    start, scaled, high, low, *ahead = pl.pallas_call(
+    start, scaled, places, high, low, *ahead = pl.pallas_call(
         functools.partial(convert_kernel, AHEAD, [SHIFTS[j % S] for j in range(AHEAD)]),
-        out_shape=[vector, shape(rows, 1, size)] + [pair_shape] * 2 + [vector] * AHEAD,
-        in_specs=[SM, HB, VM, VM],
-        out_specs=[VM] * (4 + AHEAD),
+        out_shape=[vector, shape(rows, 1, size), shape(per_row - 1, rows, 1, size)]
+        + [pair_shape] * 2
+        + [vector] * AHEAD,
+        in_specs=[HB, VM, VM, VM],
+        out_specs=[VM] * (5 + AHEAD),
         scratch_shapes=buffers(AHEAD)
         + [pltpu.VMEM((rows, per_row * size, size), F32), pltpu.SemaphoreType.DMA((rows,))],
         compiler_params=params(24),
         cost_estimate=cost(2 * rows + sum(len(r) for r in started)),
         name="convert",
-    )(offs, flat, right_side, diag)
+    )(flat, right_side, diag, offs)
 
     vectors = [start]
     halo_shape = pltpu.VMEM((margin, per_row * size, 2 * size), BF16)
@@ -519,23 +526,23 @@
             begun = pl.pallas_call(
                 functools.partial(inner_kernel, steps, shifts, done),
                 out_shape=[vector] * steps,
-                in_specs=[SM] + [VM] * (4 + len(begun)),
+                in_specs=[VM] * (5 + len(begun)),
                 out_specs=[VM] * steps,
                 scratch_shapes=buffers(steps),
                 compiler_params=params(16),
                 cost_estimate=cost(sum(len(r) for r in inner)),
                 name="inner",
-            )(offs, high, low, scaled, vectors[-1], *begun)
+            )(places, high, low, scaled, vectors[-1], *begun)
             done = inner
         next_depth = W * GROUPS[number + 1] if number + 1 < len(GROUPS) else 0
         first = number == 0
         outs = [vector] * steps + [shape(next_depth, 8, size)] * (2 if next_depth else 0)
         if first:
-            outs = [halo_shape, halo_shape, shape(2 * margin, 1, size), shape(8 * margin, 8, size)] + outs
+            outs = [halo_shape, halo_shape, shape(2 * margin, 1, size), shape(per_row - 1, 2 * margin, 1, size)] + outs
         results = pl.pallas_call(
             functools.partial(rest_kernel, first, steps, shifts, margin, done, next_depth),
             out_shape=outs,
-            in_specs=[SM, SM] + [VM] * (6 + steps + (0 if first else 4)),
+            in_specs=[VM] * (7 + steps + (0 if first else 4)),
             out_specs=[VM] * len(outs),
             scratch_shapes=buffers(steps)
             + [pltpu.VMEM((2, depth, 8, size), F32)]
@@ -543,7 +550,7 @@
             compiler_params=params(16),
             cost_estimate=cost(16),
             name="rest",
-        )(info, offs, high, low, scaled, vectors[-1], even, odd, *begun, *(parts or []))
+        )(places, high, low, scaled, vectors[-1], even, odd, *begun, *(parts or []))
         results = list(results)
         if first:
             parts, results = results[:4], results[4:]

time: 77.5 us -> 71 us (0.916)
  Pallas kernels: 36.4 us -> 29 us
  starting transfers between devices: 32.6 us -> 34.3 us
    pallas_call x6, Pallas kernels: 9.12 us -> 5.25 us  [local(): pl.pallas_call(functools.partial(rest_kernel, first, steps, shifts, margi...]
    pallas_call x4, Pallas kernels: 12.5 us -> 9.82 us  [local(): pl.pallas_call(functools.partial(inner_kernel, steps, shifts, done), out_...]
    pallas_call x1, Pallas kernels: 11.5 us -> 10.7 us  [local(): pl.pallas_call(functools.partial(convert_kernel, AHEAD, [SHIFTS[j % S] fo...]
  transfers between devices with their start and end apart: 16 -> 16, of which waited for: 5 -> 5; matrix products, arithmetic and copies ran while one was open for 0% -> 0% of each run, Pallas kernels for 31% -> 29%
where the time goes in v4:
time: 71 us; the launch traced here: 70.7 us
  starting transfers between devices  34.3 us (48%)
  Pallas kernels  29 us (41%)
  waiting for transfers between devices  6.56 us (9%)
  between operations  0.82 us (1%)
    ppermute x6, starting transfers between devices, exchange(): return (lax.ppermute(even, 'dom', swap_even), odd)  21.1 us
    pallas_call x1, Pallas kernels, local(): pl.pallas_call(functools.partial(convert_kernel, AHEAD, [SHIFTS[j % S] fo...  10.7 us
    pallas_call x4, Pallas kernels, local(): pl.pallas_call(functools.partial(inner_kernel, steps, shifts, done), out_...  9.82 us
    ppermute x4, starting transfers between devices, local(): lax.ppermute(gram, 'dom', [(i, i ^ 1 << stage) for i in range(count)])  9.11 us
    ppermute x4, waiting for transfers between devices, local(): lax.ppermute(gram, 'dom', [(i, i ^ 1 << stage) for i in range(count)])  6.35 us
    pallas_call x6, Pallas kernels, local(): pl.pallas_call(functools.partial(rest_kernel, first, steps, shifts, margi...  5.25 us
    ppermute x6, starting transfers between devices, exchange(): odd = lax.ppermute(odd, 'dom', swap_odd)  4.11 us
  transfers between devices with their start and end apart: 16, of which 5 were waited for; matrix products, arithmetic and copies ran while one was open for 0% of the time, Pallas kernels for 29%

profile of v4, /device:TPU:0, one launch (start us, length us, event | category | flops | bytes accessed | tf_op | source)
XLA Modules:
  0.0 70.7 jit_solution(14495588375622449579)
XLA Ops:
  0.6 0.0 copy-start
  0.6 0.0 copy-start.1
  0.7 0.0 copy-start.2
  0.7 1.4 %prepare.1 = (f32[1064,128]{1,0:T(8,128)S(1)}, f32[1064,128]{1,0:T(8,128)S(1)}) custom-call(f32[20480,128]{1,0:T(8,128)} %bitcast.7, f32[4,5120]{1,0:T(4,128)} %rhs.1, f32[40,128]{1,0:T(8,128)} %bitcast.3, s32[4,40]{1,0:T(4,128)} %bitcast.5), custom_call_target="tpu_custom_call" | custom-call | tf_op jit(solution)/shard_map/prepare/pallas_call | solution.py:467
  2.0 0.5 collective-permute-start
  2.5 0.7 collective-permute-start.1
  3.2 0.0 copy-done
  3.2 0.0 copy-done.1
  3.3 0.0 copy-done.2
  3.3 10.7 %convert.1 = (f32[40,8,128]{2,1,0:T(8,128)S(1)}, f32[40,1,128]{2,1,0:T(1,128)S(1)}, f32[3,40,1,128]{3,2,1,0:T(1,128)S(1)}, bf16[20,512,256]{2,1,0:T(8,128)(2,1)S...) custom-call(f32[20480,128]{1,0:T(8,128)} %bitcast.8, ...), custom_call_target="tpu_custom_call" | custom-call | flops 419430400 | bytes 52428800 | tf_op jit(solution)/shard_map/convert/pallas_call | solution.py:502
  14.0 0.0 collective-permute-done.refs_5_
  14.0 0.0 collective-permute-done.1.refs_6_
  14.0 1.2 %rest.6 = (bf16[2,512,256]{2,1,0:T(8,128)(2,1)S(1)}, bf16[2,512,256]{2,1,0:T(8,128)(2,1)S(1)}, f32[4,1,128]{2,1,0:T(1,128)S(1)}, f32[3,4,1,128]{3,2,1,0:T(1,128)...) custom-call(f32[3,40,1,128]{3,2,1,0:T(1,128)S(1)} %get-tuple-element, ...), custom_call_target="tpu_custom_call" | custom-call | flops 33554432 | bytes 4194304 | tf_op jit(solution)/shard_map/rest/pallas_call | solution.py:542
  15.2 5.3 %collective-permute-start.2 = (f32[4,8,128]{2,1,0:T(8,128)S(1)}, f32[4,8,128]{2,1,0:T(8,128)S(1)}, u32[]{:S(2)}, u32[]{:S(2)}) collective-permute-start(f32[4,8,128]{2,1,0:T(8,128)S(1)} %get-tuple-element.58), channel_id=1, source_target_pairs={{0,1},{1,0},{2,3},{3,2},{4,5},{5,4},{6,7},{7,6},{8,9},{9,8},{10,11... | collective-permute-start | bytes 49160 | tf_op jit(solution)/shard_map/ppermute | solution.py:491
  20.5 0.7 collective-permute-start.3
  21.2 0.2 collective-permute-done.2.refs_5_
  21.4 0.0 collective-permute-done.3.refs_6_
  21.4 1.2 %rest.7 = (f32[40,8,128]{2,1,0:T(8,128)S(1)}, f32[40,8,128]{2,1,0:T(8,128)S(1)}, f32[4,8,128]{2,1,0:T(8,128)S(1)}, f32[4,8,128]{2,1,0:T(8,128)S(1)}) custom-call(f32[3,40,1,128]{3,2,1,0:T(1,128)S(1)} %get-tuple-element.48.refs_0_, bf16[20,512,256]{2,1,0:T(8,128)(2,1)S(1)} %get-tuple-element.49.refs_1_, bf16[20,512,256]{2,1,0:T(8,128)(2,1)S(1)} %get-tuple-element.50.refs_2_, ...), custom_call_target="tpu_custom_call" | custom-call | flops 33554432 | bytes 4194304 | tf_op jit(solution)/shard_map/rest/pallas_call | solution.py:542
  22.6 5.0 %collective-permute-start.4 = (f32[4,8,128]{2,1,0:T(8,128)S(1)}, f32[4,8,128]{2,1,0:T(8,128)S(1)}, u32[]{:S(2)}, u32[]{:S(2)}) collective-permute-start(f32[4,8,128]{2,1,0:T(8,128)S(1)} %get-tuple-element.68), channel_id=1, source_target_pairs={{0,1},{1,0},{2,3},{3,2},{4,5},{5,4},{6,7},{7,6},{8,9},{9,8},{10,11... | collective-permute-start | bytes 49160 | tf_op jit(solution)/shard_map/ppermute | solution.py:491
  27.6 0.7 collective-permute-start.5
  28.3 2.5 %inner.4 = (f32[40,8,128]{2,1,0:T(8,128)S(1)}, f32[40,8,128]{2,1,0:T(8,128)S(1)}) custom-call(f32[3,40,1,128]{3,2,1,0:T(1,128)S(1)} %get-tuple-element.48.refs_0_, bf16[20,512,256]{2,1,0:T(8,128)(2,1)S(1)} %get-tuple-element.49.refs_1_, bf16[20,512,256]{2,1,0:T(8,128)(2,1)S(1)} %get-tuple-element.50.refs_2_, f32[40,1,128]{2,1,0:T(1,128)S(1)} %get-tuple-element.51.refs_3_, ...), custom_call_target="tpu_custom_call" | custom-call | flops 142606336 | bytes 17825792 | tf_op jit(solution)/shard_map/inner/pallas_call | solution.py:526
  30.8 0.0 collective-permute-done.4.refs_5_
  30.8 0.0 collective-permute-done.5.refs_6_
  30.8 0.7 rest.8
  31.5 4.4 %collective-permute-start.6 = (f32[4,8,128]{2,1,0:T(8,128)S(1)}, f32[4,8,128]{2,1,0:T(8,128)S(1)}, u32[]{:S(2)}, u32[]{:S(2)}) collective-permute-start(f32[4,8,128]{2,1,0:T(8,128)S(1)} %get-tuple-element.74), channel_id=1, source_target_pairs={{0,1},{1,0},{2,3},{3,2},{4,5},{5,4},{6,7},{7,6},{8,9},{9,8},{10,11... | collective-permute-start | bytes 49160 | tf_op jit(solution)/shard_map/ppermute | solution.py:491
  35.9 0.8 %collective-permute-start.7 = (f32[4,8,128]{2,1,0:T(8,128)S(1)}, f32[4,8,128]{2,1,0:T(8,128)S(1)}, u32[]{:S(2)}, u32[]{:S(2)}) collective-permute-start(f32[4,8,128]{2,1,0:T(8,128)S(1)} %get-tuple-element.75), channel_id=1, source_target_pairs={{1,2},{3,4},{5,6},{7,8},{9,10},{11,12},{13,14},{2,1},{4,3},{6,5},{... | collective-permute-start | bytes 49160 | tf_op jit(solution)/shard_map/ppermute | solution.py:490
  36.7 2.5 %inner.5 = (f32[40,8,128]{2,1,0:T(8,128)S(1)}, f32[40,8,128]{2,1,0:T(8,128)S(1)}) custom-call(f32[3,40,1,128]{3,2,1,0:T(1,128)S(1)} %get-tuple-element.48.refs_0_, bf16[20,512,256]{2,1,0:T(8,128)(2,1)S(1)} %get-tuple-element.49.refs_1_, bf16[20,512,256]{2,1,0:T(8,128)(2,1)S(1)} %get-tuple-element.50.refs_2_, f32[40,1,128]{2,1,0:T(1,128)S(1)} %get-tuple-element.51.refs_3_, ...), custom_call_target="tpu_custom_call" | custom-call | flops 142606336 | bytes 17825792 | tf_op jit(solution)/shard_map/inner/pallas_call | solution.py:526
  39.2 0.0 collective-permute-done.6.refs_5_
  39.2 0.0 collective-permute-done.7.refs_6_
  39.2 0.7 rest.9
  39.9 2.9 %collective-permute-start.8 = (f32[4,8,128]{2,1,0:T(8,128)S(1)}, f32[4,8,128]{2,1,0:T(8,128)S(1)}, u32[]{:S(2)}, u32[]{:S(2)}) collective-permute-start(f32[4,8,128]{2,1,0:T(8,128)S(1)} %get-tuple-element.80), channel_id=1, source_target_pairs={{0,1},{1,0},{2,3},{3,2},{4,5},{5,4},{6,7},{7,6},{8,9},{9,8},{10,11... | collective-permute-start | bytes 49160 | tf_op jit(solution)/shard_map/ppermute | solution.py:491
  42.8 0.7 collective-permute-start.9
  43.5 2.5 %inner.6 = (f32[40,8,128]{2,1,0:T(8,128)S(1)}, f32[40,8,128]{2,1,0:T(8,128)S(1)}) custom-call(f32[3,40,1,128]{3,2,1,0:T(1,128)S(1)} %get-tuple-element.48.refs_0_, bf16[20,512,256]{2,1,0:T(8,128)(2,1)S(1)} %get-tuple-element.49.refs_1_, bf16[20,512,256]{2,1,0:T(8,128)(2,1)S(1)} %get-tuple-element.50.refs_2_, f32[40,1,128]{2,1,0:T(1,128)S(1)} %get-tuple-element.51.refs_3_, ...), custom_call_target="tpu_custom_call" | custom-call | flops 142606336 | bytes 17825792 | tf_op jit(solution)/shard_map/inner/pallas_call | solution.py:526
  45.9 0.0 collective-permute-done.8.refs_5_
  45.9 0.0 collective-permute-done.9.refs_6_
  45.9 0.7 rest.10
  46.6 2.9 %collective-permute-start.10 = (f32[4,8,128]{2,1,0:T(8,128)S(1)}, f32[4,8,128]{2,1,0:T(8,128)S(1)}, u32[]{:S(2)}, u32[]{:S(2)}) collective-permute-start(f32[4,8,128]{2,1,0:T(8,128)S(1)} %get-tuple-element.86), channel_id=1, source_target_pairs={{0,1},{1,0},{2,3},{3,2},{4,5},{5,4},{6,7},{7,6},{8,9},{9,8},{10,11... | collective-permute-start | bytes 49160 | tf_op jit(solution)/shard_map/ppermute | solution.py:491
  49.5 0.7 collective-permute-start.11
  50.2 2.5 %inner.7 = (f32[40,8,128]{2,1,0:T(8,128)S(1)}, f32[40,8,128]{2,1,0:T(8,128)S(1)}) custom-call(f32[3,40,1,128]{3,2,1,0:T(1,128)S(1)} %get-tuple-element.48.refs_0_, bf16[20,512,256]{2,1,0:T(8,128)(2,1)S(1)} %get-tuple-element.49.refs_1_, bf16[20,512,256]{2,1,0:T(8,128)(2,1)S(1)} %get-tuple-element.50.refs_2_, f32[40,1,128]{2,1,0:T(1,128)S(1)} %get-tuple-element.51.refs_3_, ...), custom_call_target="tpu_custom_call" | custom-call | flops 142606336 | bytes 17825792 | tf_op jit(solution)/shard_map/inner/pallas_call | solution.py:526
  52.7 0.0 collective-permute-done.10.refs_5_
  52.7 0.0 collective-permute-done.11.refs_6_
  52.7 0.7 rest.11
  53.4 0.6 gram.1
  54.0 2.9 %collective-permute-start.12 = (f32[8,128]{1,0:T(8,128)S(1)}, f32[8,128]{1,0:T(8,128)S(1)}, u32[]{:S(2)}, u32[]{:S(2)}) collective-permute-start(f32[8,128]{1,0:T(8,128)S(1)} %gram.1), channel_id=1, source_target_pairs={{0,1},{1,0},{2,3},{3,2},{4,5},{5,4},{6,7},{7,6},{8,9},{9,8},{10,11... | collective-permute-start | bytes 12296 | tf_op jit(solution)/shard_map/ppermute | solution.py:574
  56.9 0.8 %collective-permute-done.12 = f32[8,128]{1,0:T(8,128)S(1)} collective-permute-done((f32[8,128]{1,0:T(8,128)S(1)}, f32[8,128]{1,0:T(8,128)S(1)}, u32[]{:S(2)}, u32[]{:S(2)}) %collective-permute-start.12) | collective-permute-done | bytes 4128 | tf_op jit(solution)/shard_map/ppermute | solution.py:574
  57.7 1.5 %collective-permute-start.13 = (f32[8,128]{1,0:T(8,128)S(1)}, f32[8,128]{1,0:T(8,128)S(1)}, u32[]{:S(2)}, u32[]{:S(2)}) collective-permute-start(f32[8,128]{1,0:T(8,128)S(1)} %add.12), channel_id=1, source_target_pairs={{0,2},{1,3},{2,0},{3,1},{4,6},{5,7},{6,4},{7,5},{8,10},{9,11},{10,... | collective-permute-start | bytes 12296 | tf_op jit(solution)/shard_map/ppermute | solution.py:574
  59.2 2.1 %collective-permute-done.13 = f32[8,128]{1,0:T(8,128)S(1)} collective-permute-done((f32[8,128]{1,0:T(8,128)S(1)}, f32[8,128]{1,0:T(8,128)S(1)}, u32[]{:S(2)}, u32[]{:S(2)}) %collective-permute-start.13) | collective-permute-done | bytes 4128 | tf_op jit(solution)/shard_map/ppermute | solution.py:574
  61.3 1.9 %collective-permute-start.14 = (f32[8,128]{1,0:T(8,128)S(1)}, f32[8,128]{1,0:T(8,128)S(1)}, u32[]{:S(2)}, u32[]{:S(2)}) collective-permute-start(f32[8,128]{1,0:T(8,128)S(1)} %add.13), channel_id=1, source_target_pairs={{0,4},{1,5},{2,6},{3,7},{4,0},{5,1},{6,2},{7,3},{8,12},{9,13},{10,... | collective-permute-start | bytes 12296 | tf_op jit(solution)/shard_map/ppermute | solution.py:574
  63.2 1.8 %collective-permute-done.14 = f32[8,128]{1,0:T(8,128)S(1)} collective-permute-done((f32[8,128]{1,0:T(8,128)S(1)}, f32[8,128]{1,0:T(8,128)S(1)}, u32[]{:S(2)}, u32[]{:S(2)}) %collective-permute-start.14) | collective-permute-done | bytes 4128 | tf_op jit(solution)/shard_map/ppermute | solution.py:574
  64.9 2.8 %collective-permute-start.15 = (f32[8,128]{1,0:T(8,128)S(1)}, f32[8,128]{1,0:T(8,128)S(1)}, u32[]{:S(2)}, u32[]{:S(2)}) collective-permute-start(f32[8,128]{1,0:T(8,128)S(1)} %add.14), channel_id=1, source_target_pairs={{0,8},{1,9},{2,10},{3,11},{4,12},{5,13},{6,14},{7,15},{8,0},{9,1},... | collective-permute-start | bytes 12296 | tf_op jit(solution)/shard_map/ppermute | solution.py:574
  67.8 1.7 %collective-permute-done.15 = f32[8,128]{1,0:T(8,128)S(1)} collective-permute-done((f32[8,128]{1,0:T(8,128)S(1)}, f32[8,128]{1,0:T(8,128)S(1)}, u32[]{:S(2)}, u32[]{:S(2)}) %collective-permute-start.15) | collective-permute-done | bytes 4128 | tf_op jit(solution)/shard_map/ppermute | solution.py:574
  69.5 1.3 %finish.1 = (f32[4,5120]{1,0:T(4,128)}, f32[4,5120]{1,0:T(4,128)}) custom-call(f32[8,128]{1,0:T(8,128)S(1)} %add.15.total_gram, f32[40,8,128]{2,1,0:T(8,128)S(1)} %get-tuple-element.47.refs_4_.refs_0_, f32[40,8,128]{2,1,0:T(8,128)S(1)} %get-tuple-element.56.refs_1_, f32[40,8,128]{2,1,0:T(8,128)S(1)} %get-tuple-element.57.refs_4_.refs_2_, ...), custom_call_target="tpu_custom_call" | custom-call | tf_op jit(solution)/shard_map/finish/pallas_call | solution.py:576
  (4 shorter events, 0.0 us)
Async XLA Ops:
  0.6 2.6 %copy-start = (f32[4,5120]{1,0:T(4,128)S(1)}, f32[4,5120]{1,0:T(4,128)}, u32[]{:S(2)}) copy-start(f32[4,5120]{1,0:T(4,128)} %rhs.1) | copy-start | bytes 245764
  0.6 2.6 %copy-start.1 = (f32[5120]{0:T(1024)S(1)}, f32[5120]{0:T(1024)}, u32[]{:S(2)}) copy-start(f32[5120]{0:T(1024)} %param.6) | copy-start | bytes 61444
  0.7 2.6 %copy-start.2 = (s32[40,4]{0,1:T(4,128)S(1)}, s32[40,4]{0,1:T(4,128)}, u32[]{:S(2)}) copy-start(s32[40,4]{0,1:T(4,128)} %param.5) | copy-start | bytes 1924
  2.0 11.9 %collective-permute-start = (f32[1064,128]{1,0:T(8,128)S(1)}, f32[1064,128]{1,0:T(8,128)S(1)}, u32[]{:S(2)}, u32[]{:S(2)}) collective-permute-start(f32[1064,128]{1,0:T(8,128)S(1)} %get-tuple-element.52), channel_id=1, source_target_pairs={{0,1},{1,0},{2,3},{3,2},{4,5},{5,4},{6,7},{7,6},{8,9},{9,8},{10,11... | collective-permute-start | bytes 1634312 | tf_op jit(solution)/shard_map/ppermute | solution.py:491
  2.5 11.4 %collective-permute-start.1 = (f32[1064,128]{1,0:T(8,128)S(1)}, f32[1064,128]{1,0:T(8,128)S(1)}, u32[]{:S(2)}, u32[]{:S(2)}) collective-permute-start(f32[1064,128]{1,0:T(8,128)S(1)} %get-tuple-element.53), channel_id=1, source_target_pairs={{1,2},{3,4},{5,6},{7,8},{9,10},{11,12},{13,14},{2,1},{4,3},{6,5},{... | collective-permute-start | bytes 1634312 | tf_op jit(solution)/shard_map/ppermute | solution.py:490
  15.2 6.1 %collective-permute-start.2 = (f32[4,8,128]{2,1,0:T(8,128)S(1)}, f32[4,8,128]{2,1,0:T(8,128)S(1)}, u32[]{:S(2)}, u32[]{:S(2)}) collective-permute-start(f32[4,8,128]{2,1,0:T(8,128)S(1)} %get-tuple-element.58), channel_id=1, source_target_pairs={{0,1},{1,0},{2,3},{3,2},{4,5},{5,4},{6,7},{7,6},{8,9},{9,8},{10,11... | collective-permute-start | bytes 49160 | tf_op jit(solution)/shard_map/ppermute | solution.py:491
  20.5 0.8 %collective-permute-start.3 = (f32[4,8,128]{2,1,0:T(8,128)S(1)}, f32[4,8,128]{2,1,0:T(8,128)S(1)}, u32[]{:S(2)}, u32[]{:S(2)}) collective-permute-start(f32[4,8,128]{2,1,0:T(8,128)S(1)} %get-tuple-element.59), channel_id=1, source_target_pairs={{1,2},{3,4},{5,6},{7,8},{9,10},{11,12},{13,14},{2,1},{4,3},{6,5},{... | collective-permute-start | bytes 49160 | tf_op jit(solution)/shard_map/ppermute | solution.py:490
  22.6 8.2 %collective-permute-start.4 = (f32[4,8,128]{2,1,0:T(8,128)S(1)}, f32[4,8,128]{2,1,0:T(8,128)S(1)}, u32[]{:S(2)}, u32[]{:S(2)}) collective-permute-start(f32[4,8,128]{2,1,0:T(8,128)S(1)} %get-tuple-element.68), channel_id=1, source_target_pairs={{0,1},{1,0},{2,3},{3,2},{4,5},{5,4},{6,7},{7,6},{8,9},{9,8},{10,11... | collective-permute-start | bytes 49160 | tf_op jit(solution)/shard_map/ppermute | solution.py:491
  27.6 3.1 %collective-permute-start.5 = (f32[4,8,128]{2,1,0:T(8,128)S(1)}, f32[4,8,128]{2,1,0:T(8,128)S(1)}, u32[]{:S(2)}, u32[]{:S(2)}) collective-permute-start(f32[4,8,128]{2,1,0:T(8,128)S(1)} %get-tuple-element.69), channel_id=1, source_target_pairs={{1,2},{3,4},{5,6},{7,8},{9,10},{11,12},{13,14},{2,1},{4,3},{6,5},{... | collective-permute-start | bytes 49160 | tf_op jit(solution)/shard_map/ppermute | solution.py:490
  31.5 7.7 %collective-permute-start.6 = (f32[4,8,128]{2,1,0:T(8,128)S(1)}, f32[4,8,128]{2,1,0:T(8,128)S(1)}, u32[]{:S(2)}, u32[]{:S(2)}) collective-permute-start(f32[4,8,128]{2,1,0:T(8,128)S(1)} %get-tuple-element.74), channel_id=1, source_target_pairs={{0,1},{1,0},{2,3},{3,2},{4,5},{5,4},{6,7},{7,6},{8,9},{9,8},{10,11... | collective-permute-start | bytes 49160 | tf_op jit(solution)/shard_map/ppermute | solution.py:491
  35.9 3.3 %collective-permute-start.7 = (f32[4,8,128]{2,1,0:T(8,128)S(1)}, f32[4,8,128]{2,1,0:T(8,128)S(1)}, u32[]{:S(2)}, u32[]{:S(2)}) collective-permute-start(f32[4,8,128]{2,1,0:T(8,128)S(1)} %get-tuple-element.75), channel_id=1, source_target_pairs={{1,2},{3,4},{5,6},{7,8},{9,10},{11,12},{13,14},{2,1},{4,3},{6,5},{... | collective-permute-start | bytes 49160 | tf_op jit(solution)/shard_map/ppermute | solution.py:490
  39.9 6.0 %collective-permute-start.8 = (f32[4,8,128]{2,1,0:T(8,128)S(1)}, f32[4,8,128]{2,1,0:T(8,128)S(1)}, u32[]{:S(2)}, u32[]{:S(2)}) collective-permute-start(f32[4,8,128]{2,1,0:T(8,128)S(1)} %get-tuple-element.80), channel_id=1, source_target_pairs={{0,1},{1,0},{2,3},{3,2},{4,5},{5,4},{6,7},{7,6},{8,9},{9,8},{10,11... | collective-permute-start | bytes 49160 | tf_op jit(solution)/shard_map/ppermute | solution.py:491
  42.8 3.1 %collective-permute-start.9 = (f32[4,8,128]{2,1,0:T(8,128)S(1)}, f32[4,8,128]{2,1,0:T(8,128)S(1)}, u32[]{:S(2)}, u32[]{:S(2)}) collective-permute-start(f32[4,8,128]{2,1,0:T(8,128)S(1)} %get-tuple-element.81), channel_id=1, source_target_pairs={{1,2},{3,4},{5,6},{7,8},{9,10},{11,12},{13,14},{2,1},{4,3},{6,5},{... | collective-permute-start | bytes 49160 | tf_op jit(solution)/shard_map/ppermute | solution.py:490
  46.6 6.0 %collective-permute-start.10 = (f32[4,8,128]{2,1,0:T(8,128)S(1)}, f32[4,8,128]{2,1,0:T(8,128)S(1)}, u32[]{:S(2)}, u32[]{:S(2)}) collective-permute-start(f32[4,8,128]{2,1,0:T(8,128)S(1)} %get-tuple-element.86), channel_id=1, source_target_pairs={{0,1},{1,0},{2,3},{3,2},{4,5},{5,4},{6,7},{7,6},{8,9},{9,8},{10,11... | collective-permute-start | bytes 49160 | tf_op jit(solution)/shard_map/ppermute | solution.py:491
  49.5 3.1 %collective-permute-start.11 = (f32[4,8,128]{2,1,0:T(8,128)S(1)}, f32[4,8,128]{2,1,0:T(8,128)S(1)}, u32[]{:S(2)}, u32[]{:S(2)}) collective-permute-start(f32[4,8,128]{2,1,0:T(8,128)S(1)} %get-tuple-element.87), channel_id=1, source_target_pairs={{1,2},{3,4},{5,6},{7,8},{9,10},{11,12},{13,14},{2,1},{4,3},{6,5},{... | collective-permute-start | bytes 49160 | tf_op jit(solution)/shard_map/ppermute | solution.py:490
  54.0 3.7 %collective-permute-start.12 = (f32[8,128]{1,0:T(8,128)S(1)}, f32[8,128]{1,0:T(8,128)S(1)}, u32[]{:S(2)}, u32[]{:S(2)}) collective-permute-start(f32[8,128]{1,0:T(8,128)S(1)} %gram.1), channel_id=1, source_target_pairs={{0,1},{1,0},{2,3},{3,2},{4,5},{5,4},{6,7},{7,6},{8,9},{9,8},{10,11... | collective-permute-start | bytes 12296 | tf_op jit(solution)/shard_map/ppermute | solution.py:574
  57.7 3.6 %collective-permute-start.13 = (f32[8,128]{1,0:T(8,128)S(1)}, f32[8,128]{1,0:T(8,128)S(1)}, u32[]{:S(2)}, u32[]{:S(2)}) collective-permute-start(f32[8,128]{1,0:T(8,128)S(1)} %add.12), channel_id=1, source_target_pairs={{0,2},{1,3},{2,0},{3,1},{4,6},{5,7},{6,4},{7,5},{8,10},{9,11},{10,... | collective-permute-start | bytes 12296 | tf_op jit(solution)/shard_map/ppermute | solution.py:574
  61.3 3.6 %collective-permute-start.14 = (f32[8,128]{1,0:T(8,128)S(1)}, f32[8,128]{1,0:T(8,128)S(1)}, u32[]{:S(2)}, u32[]{:S(2)}) collective-permute-start(f32[8,128]{1,0:T(8,128)S(1)} %add.13), channel_id=1, source_target_pairs={{0,4},{1,5},{2,6},{3,7},{4,0},{5,1},{6,2},{7,3},{8,12},{9,13},{10,... | collective-permute-start | bytes 12296 | tf_op jit(solution)/shard_map/ppermute | solution.py:574
  64.9 4.5 %collective-permute-start.15 = (f32[8,128]{1,0:T(8,128)S(1)}, f32[8,128]{1,0:T(8,128)S(1)}, u32[]{:S(2)}, u32[]{:S(2)}) collective-permute-start(f32[8,128]{1,0:T(8,128)S(1)} %add.14), channel_id=1, source_target_pairs={{0,8},{1,9},{2,10},{3,11},{4,12},{5,13},{6,14},{7,15},{8,0},{9,1},... | collective-permute-start | bytes 12296 | tf_op jit(solution)/shard_map/ppermute | solution.py:574

commit v5 on v4

--- a/solution.py
+++ b/solution.py
@@ -15,7 +15,7 @@
 CHAIN = S * CYCLES
 GROUPS = (2, 2, 2, 2, 2, 2)
 AHEAD = 4
-INNER_SECOND = False
+INNER_SECOND = True
 SCALE = 0.125
 GROW = 1.0 / SCALE
 SHIFTS = [
@@ -41,8 +41,8 @@
     return jnp.where(mask, high, tile - high)
 
 
-def store_pair(block, high_ref, low_ref, pair, half, k):
-    block = block * SCALE
+def store_pair(block, high_ref, low_ref, pair, half, k, factor=SCALE):
+    block = block * factor
     high = block.astype(BF16)
     low = (block - high.astype(F32)).astype(BF16)
     rows, cols = slice(k * 128, (k + 1) * 128), slice(half * 128, (half + 1) * 128)
@@ -90,18 +90,37 @@
         copy.wait()
 
 
+def at_inside():
+    me = lax.axis_index("dom")
+    return jnp.logical_and(me > 0, me < lax.axis_size("dom") - 1)
+
+
+def take_vectors(depth, parity, even, odd, halo):
+    inside = at_inside()
+    for i in range(depth):
+        halo[1 - parity, i] = even(i)
+        tile = odd(i)
+        halo[parity, i] = jnp.where(inside, tile, jnp.zeros_like(tile))
+
+
 def take_message(depth, margin, rows, parity, even, odd, high, low, scaled, places, halo):
-    for ref, side in ((even, 1 - parity), (odd, parity)):
+    base = margin * 512
+    take_vectors(
+        depth,
+        parity,
+        lambda i: even[base + 8 * i : base + 8 * i + 8, :],
+        lambda i: odd[base + 8 * i : base + 8 * i + 8, :],
+        halo,
+    )
+    factor = jnp.where(at_inside(), SCALE, 0.0)
+    for ref, side, by in ((even, 1 - parity, SCALE), (odd, parity, factor)):
         for m in range(margin):
             for k in range(4):
                 first = (m * 4 + k) * 128
                 store_pair(
-                    ref[first : first + 128, :], high, low, side * (margin // 2) + m // 2, m % 2, k
+                    ref[first : first + 128, :], high, low, side * (margin // 2) + m // 2, m % 2, k, by
                 )
-        base = margin * 512
-        for i in range(depth):
-            halo[side, i] = ref[base + 8 * i : base + 8 * i + 8, :]
-        base += 8 * depth
+        base = margin * 512 + 8 * depth
         for m in range(margin):
             scaled[side * margin + m] = ref[base + 4 + m : base + 5 + m, :] * SCALE
             for k in range(1, 4):
@@ -253,12 +272,22 @@
     chain.run(plan, values, [range(rows)] + [[]] * (steps - 1), splits, store)
 
 
-def inner_kernel(steps, shifts, done, *refs):
+def inner_kernel(steps, shifts, done, earlier, *refs):
     places, high, low, scaled, own = refs[:5]
-    begun = refs[5 : 5 + len(done)]
-    outs = refs[5 + len(done) : 5 + len(done) + steps]
-    splits = refs[5 + len(done) + steps :]
+    refs = list(refs[5:])
+    begun = refs[: len(done)]
+    del refs[: len(done)]
+    before = refs[:earlier]
+    del refs[:earlier]
+    outs = refs[:steps]
+    del refs[:steps]
     rows = own.shape[0]
+    if earlier:
+        products = refs.pop(0)
+        vectors = before + [own]
+        tile = jnp.zeros((8, 128), F32)
+        products[...] = add_products(tile, vectors, pair_blocks((earlier + 1) // 2, earlier + 1))
+    splits = refs
     copy_rows(begun, outs, done)
     done = list(done) + [[]] * (steps - len(done))
     chain = Chain(rows, 0, steps, shifts, places, high, low, scaled)
@@ -267,16 +296,21 @@
     chain.run(plan, values, [range(rows)] + done[:-1], splits, store)
 
 
-def rest_kernel(first, steps, shifts, margin, done, next_depth, *refs):
+def rest_kernel(first, steps, shifts, margin, done, next_depth, earlier, *refs):
     refs = list(refs)
     places, high, low, scaled, own, from_even, from_odd = refs[:7]
     del refs[:7]
     begun = refs[:steps]
     del refs[:steps]
+    if earlier:
+        products, before = refs[0], refs[1 : 1 + earlier]
+        del refs[: 1 + earlier]
     parts = refs[:4]
     del refs[:4]
     outs = refs[:steps]
     del refs[:steps]
+    if earlier:
+        gram = refs.pop(0)
     if next_depth:
         to_even, to_odd = refs[:2]
         del refs[:2]
@@ -287,9 +321,7 @@
     if first:
         take_message(depth, margin, rows, parity, from_even, from_odd, *parts, halo)
     else:
-        for i in range(depth):
-            halo[1 - parity, i] = from_even[i]
-            halo[parity, i] = from_odd[i]
+        take_vectors(depth, parity, lambda i: from_even[i], lambda i: from_odd[i], halo)
     copy_rows(begun, outs, done)
     chain = Chain(rows, margin, steps, shifts, places, high, low, scaled, parts)
     plan = [without(whole_rows(rows, steps, j + 1), done[j]) for j in range(steps)]
@@ -301,11 +333,15 @@
         for i in range(next_depth):
             to_even[i] = last[(1 - parity) * (rows - next_depth) + i]
             to_odd[i] = last[parity * (rows - next_depth) + i]
-
-
-def pair_list():
-    half = CHAIN // 2 + 1
-    low, top = range(half), range(half, CHAIN + 1)
+    if earlier:
+        vectors = list(before) + [own] + list(outs)
+        new = [(i, j) for j in range(earlier + 1, earlier + 1 + steps) for i in range(j + 1)]
+        tile = add_products(products[...], vectors, [new])
+        gram[...] = tile + pltpu.roll(tile, 4, 0)
+
+
+def pair_blocks(split, count):
+    low, top = range(split), range(split, count)
     return (
         [(i, j) for i in low for j in low if i <= j],
         [(i, j) for i in low for j in top],
@@ -313,20 +349,18 @@
     )
 
 
-PLACES = {pair: at for at, pair in enumerate(sum(pair_list(), []))}
+PLACES = {pair: at for at, pair in enumerate((i, j) for j in range(CHAIN + 1) for i in range(j + 1))}
 
 
 def dense(ref, p, mask):
     return jnp.where(mask, ref[2 * p], ref[2 * p + 1])
 
 
-def gram_kernel(*refs):
-    vectors, out = refs[:-1], refs[-1]
+def add_products(tile, vectors, blocks):
     count = vectors[0].shape[0] // 2
     mask = halves()
     lane = lax.broadcasted_iota(jnp.int32, (8, 128), 1)
-    tile = jnp.zeros((8, 128), F32)
-    for pairs in pair_list():
+    for pairs in blocks:
         used = sorted({i for pair in pairs for i in pair})
         total = None
         for p in range(count):
@@ -335,7 +369,7 @@
             total = products if total is None else [a + b for a, b in zip(total, products)]
         for pair, one in zip(pairs, total):
             tile = jnp.where(lane == PLACES[pair], jnp.sum(one, axis=1, keepdims=True), tile)
-    out[...] = tile + pltpu.roll(tile, 4, 0)
+    return tile
 
 
 def small_solve(gram):
@@ -483,11 +517,14 @@
     )
 
     swap_even = [(i, i ^ 1) for i in range(count)]
-    swap_odd = [(i, i + 1) for i in range(1, count - 1, 2)]
-    swap_odd = swap_odd + [(b, a) for a, b in swap_odd]
+    copies = lax.axis_size("groups")
+    swap_odd = [(g * count + i, g * count + i + 1) for g in range(copies) for i in range(1, count - 1, 2)]
+    for end in (0, count - 1):
+        swap_odd += [(g * count + end, (g + 1) * count + end) for g in range(0, copies - 1, 2)]
+    swap_odd += [(b, a) for a, b in swap_odd]
 
     def exchange(even, odd):
-        odd = lax.ppermute(odd, "dom", swap_odd)
+        odd = lax.ppermute(odd, ("groups", "dom"), swap_odd)
         return lax.ppermute(even, "dom", swap_even), odd
 
     even, odd = exchange(even, odd)
@@ -522,27 +559,30 @@
         depth = W * steps
         begun, done = ahead[at : at + steps], started[at : at + steps]
         inner = [inner_rows(rows, j + 1) for j in range(steps)]
+        last = number + 1 == len(GROUPS)
+        before = vectors[:-1] if last else []
         if done != inner and (number > 1 or INNER_SECOND or not begun):
             begun = pl.pallas_call(
-                functools.partial(inner_kernel, steps, shifts, done),
-                out_shape=[vector] * steps,
-                in_specs=[VM] * (5 + len(begun)),
-                out_specs=[VM] * steps,
+                functools.partial(inner_kernel, steps, shifts, done, len(before)),
+                out_shape=[vector] * steps + [shape(8, size)] * last,
+                in_specs=[VM] * (5 + len(begun) + len(before)),
+                out_specs=[VM] * (steps + last),
                 scratch_shapes=buffers(steps),
                 compiler_params=params(16),
                 cost_estimate=cost(sum(len(r) for r in inner)),
                 name="inner",
-            )(places, high, low, scaled, vectors[-1], *begun)
+            )(places, high, low, scaled, vectors[-1], *begun, *before)
             done = inner
+            begun, products = begun[:steps], begun[steps:]
         next_depth = W * GROUPS[number + 1] if number + 1 < len(GROUPS) else 0
         first = number == 0
-        outs = [vector] * steps + [shape(next_depth, 8, size)] * (2 if next_depth else 0)
+        outs = [vector] * steps + [shape(8, size)] * last + [shape(next_depth, 8, size)] * (0 if last else 2)
         if first:
             outs = [halo_shape, halo_shape, shape(2 * margin, 1, size), shape(per_row - 1, 2 * margin, 1, size)] + outs
         results = pl.pallas_call(
-            functools.partial(rest_kernel, first, steps, shifts, margin, done, next_depth),
+            functools.partial(rest_kernel, first, steps, shifts, margin, done, next_depth, len(before)),
             out_shape=outs,
-            in_specs=[VM] * (7 + steps + (0 if first else 4)),
+            in_specs=[VM] * (7 + steps + (0 if first else 4) + (1 + len(before) if last else 0)),
             out_specs=[VM] * len(outs),
             scratch_shapes=buffers(steps)
             + [pltpu.VMEM((2, depth, 8, size), F32)]
@@ -550,7 +590,7 @@
             compiler_params=params(16),
             cost_estimate=cost(16),
             name="rest",
-        )(places, high, low, scaled, vectors[-1], even, odd, *begun, *(parts or []))
+        )(places, high, low, scaled, vectors[-1], even, odd, *begun, *((*products, *before) if last else ()), *(parts or []))
         results = list(results)
         if first:
             parts, results = results[:4], results[4:]
@@ -559,14 +599,7 @@
         if next_depth:
             even, odd = exchange(*results[steps:])
 
-    gram = pl.pallas_call(
-        gram_kernel,
-        out_shape=shape(8, size),
-        in_specs=[VM] * len(vectors),
-        out_specs=VM,
-        compiler_params=params(16),
-        name="gram",
-    )(*vectors)
+    gram = results[steps]
     if count & (count - 1):
         gram = lax.psum(gram, "dom")
     else:

time: 71 us -> 59.1 us (0.83)
  starting transfers between devices: 34.3 us -> 19.9 us
  waiting for transfers between devices: 6.56 us -> 9.22 us
    ppermute x6, starting transfers between devices: 21.1 us -> 4.51 us  [exchange(): return (lax.ppermute(even, 'dom', swap_even), odd)]
    ppermute x6, starting transfers between devices: 4.11 us -> 10 us  [exchange(): odd = lax.ppermute(odd, ('groups', 'dom'), swap_odd)]
    ppermute x4, starting transfers between devices: 9.11 us -> 5.35 us  [local(): lax.ppermute(gram, 'dom', [(i, i ^ 1 << stage) for i in range(count)])]
    ppermute x6, waiting for transfers between devices: 0.02 us -> 1.6 us  [exchange(): odd = lax.ppermute(odd, ('groups', 'dom'), swap_odd)]
    ppermute x4, waiting for transfers between devices: 6.35 us -> 7.6 us  [local(): lax.ppermute(gram, 'dom', [(i, i ^ 1 << stage) for i in range(count)])]
  transfers between devices with their start and end apart: 16 -> 16, of which waited for: 5 -> 5; matrix products, arithmetic and copies ran while one was open for 0% -> 0% of each run, Pallas kernels for 29% -> 37%
where the time goes in v5:
time: 59.1 us; the launch traced here: 58.9 us
  Pallas kernels  29 us (49%)
  starting transfers between devices  19.9 us (34%)
  waiting for transfers between devices  9.22 us (16%)
  between operations  0.75 us (1%)
    pallas_call x5, Pallas kernels, local(): pl.pallas_call(functools.partial(inner_kernel, steps, shifts, done, len(b...  10.9 us
    pallas_call x1, Pallas kernels, local(): pl.pallas_call(functools.partial(convert_kernel, AHEAD, [SHIFTS[j % S] fo...  10.7 us
    ppermute x6, starting transfers between devices, exchange(): odd = lax.ppermute(odd, ('groups', 'dom'), swap_odd)  10 us
    ppermute x4, waiting for transfers between devices, local(): lax.ppermute(gram, 'dom', [(i, i ^ 1 << stage) for i in range(count)])  7.6 us
    ppermute x4, starting transfers between devices, local(): lax.ppermute(gram, 'dom', [(i, i ^ 1 << stage) for i in range(count)])  5.35 us
    pallas_call x6, Pallas kernels, local(): pl.pallas_call(functools.partial(rest_kernel, first, steps, shifts, margi...  4.86 us
    ppermute x6, starting transfers between devices, exchange(): return (lax.ppermute(even, 'dom', swap_even), odd)  4.51 us
    ppermute x6, waiting for transfers between devices, exchange(): odd = lax.ppermute(odd, ('groups', 'dom'), swap_odd)  1.6 us
  transfers between devices with their start and end apart: 16, of which 5 were waited for; matrix products, arithmetic and copies ran while one was open for 0% of the time, Pallas kernels for 37%

profile of v5, /device:TPU:0, one launch (start us, length us, event | category | flops | bytes accessed | tf_op | source)
XLA Modules:
  0.0 58.9 jit_solution(5954606608540391413)
XLA Ops:
  0.6 0.0 copy-start
  0.6 0.0 copy-start.1
  0.7 0.0 copy-start.2
  0.7 1.4 %prepare.1 = (f32[1064,128]{1,0:T(8,128)S(1)}, f32[1064,128]{1,0:T(8,128)S(1)}) custom-call(f32[20480,128]{1,0:T(8,128)} %bitcast.7, f32[4,5120]{1,0:T(4,128)} %rhs.1, f32[40,128]{1,0:T(8,128)} %bitcast.3, s32[4,40]{1,0:T(4,128)} %bitcast.5), custom_call_target="tpu_custom_call" | custom-call | tf_op jit(solution)/shard_map/prepare/pallas_call | solution.py:501
  2.0 0.5 collective-permute-start
  2.5 2.6 %collective-permute-start.1 = (f32[1064,128]{1,0:T(8,128)S(1)}, f32[1064,128]{1,0:T(8,128)S(1)}, u32[]{:S(2)}, u32[]{:S(2)}) collective-permute-start(f32[1064,128]{1,0:T(8,128)S(1)} %get-tuple-element.57), channel_id=1, source_target_pairs={{1,2},{3,4},{5,6},{7,8},{9,10},{11,12},{13,14},{17,18},{19,20},{21... | collective-permute-start | bytes 1634312 | tf_op jit(solution)/shard_map/ppermute | solution.py:527
  5.1 0.0 copy-done
  5.1 0.0 copy-done.1
  5.1 0.0 copy-done.2
  5.1 10.7 %convert.1 = (f32[40,8,128]{2,1,0:T(8,128)S(1)}, f32[40,1,128]{2,1,0:T(1,128)S(1)}, f32[3,40,1,128]{3,2,1,0:T(1,128)S(1)}, bf16[20,512,256]{2,1,0:T(8,128)(2,1)S...) custom-call(f32[20480,128]{1,0:T(8,128)} %bitcast.8, ...), custom_call_target="tpu_custom_call" | custom-call | flops 419430400 | bytes 52428800 | tf_op jit(solution)/shard_map/convert/pallas_call | solution.py:539
  15.8 0.0 collective-permute-done.refs_5_
  15.8 0.0 collective-permute-done.1.refs_6_
  15.8 1.2 %rest.6 = (bf16[2,512,256]{2,1,0:T(8,128)(2,1)S(1)}, bf16[2,512,256]{2,1,0:T(8,128)(2,1)S(1)}, f32[4,1,128]{2,1,0:T(1,128)S(1)}, f32[3,4,1,128]{3,2,1,0:T(1,128)...) custom-call(f32[3,40,1,128]{3,2,1,0:T(1,128)S(1)} %get-tuple-element, ...), custom_call_target="tpu_custom_call" | custom-call | flops 33554432 | bytes 4194304 | tf_op jit(solution)/shard_map/rest/pallas_call | solution.py:582
  17.0 1.6 %collective-permute-start.2 = (f32[4,8,128]{2,1,0:T(8,128)S(1)}, f32[4,8,128]{2,1,0:T(8,128)S(1)}, u32[]{:S(2)}, u32[]{:S(2)}) collective-permute-start(f32[4,8,128]{2,1,0:T(8,128)S(1)} %get-tuple-element.61), channel_id=1, source_target_pairs={{0,1},{1,0},{2,3},{3,2},{4,5},{5,4},{6,7},{7,6},{8,9},{9,8},{10,11... | collective-permute-start | bytes 49160 | tf_op jit(solution)/shard_map/ppermute | solution.py:528
  18.7 1.5 %collective-permute-start.3 = (f32[4,8,128]{2,1,0:T(8,128)S(1)}, f32[4,8,128]{2,1,0:T(8,128)S(1)}, u32[]{:S(2)}, u32[]{:S(2)}) collective-permute-start(f32[4,8,128]{2,1,0:T(8,128)S(1)} %get-tuple-element.62), channel_id=1, source_target_pairs={{1,2},{3,4},{5,6},{7,8},{9,10},{11,12},{13,14},{17,18},{19,20},{21... | collective-permute-start | bytes 49160 | tf_op jit(solution)/shard_map/ppermute | solution.py:527
  20.2 0.7 %inner.5 = (f32[40,8,128]{2,1,0:T(8,128)S(1)}, f32[40,8,128]{2,1,0:T(8,128)S(1)}) custom-call(f32[3,40,1,128]{3,2,1,0:T(1,128)S(1)} %get-tuple-element.51.refs_0_, bf16[20,512,256]{2,1,0:T(8,128)(2,1)S(1)} %get-tuple-element.52.refs_1_, bf16[20,512,256]{2,1,0:T(8,128)(2,1)S(1)} %get-tuple-element.53.refs_2_, f32[40,1,128]{2,1,0:T(1,128)S(1)} %get-tuple-element.54.refs_3_, ...), custom_call_target="tpu_custom_call" | custom-call | flops 142606336 | bytes 17825792 | tf_op jit(solution)/shard_map/inner/pallas_call | solution.py:565
  20.8 0.0 collective-permute-done.2.refs_5_
  20.8 1.6 %collective-permute-done.3.refs_6_ = f32[4,8,128]{2,1,0:T(8,128)S(1)} collective-permute-done((f32[4,8,128]{2,1,0:T(8,128)S(1)}, f32[4,8,128]{2,1,0:T(8,128)S(1)}, u32[]{:S(2)}, u32[]{:S(2)}) %collective-permute-start.3) | collective-permute-done | bytes 16416 | tf_op jit(solution)/shard_map/ppermute | solution.py:527
  22.4 0.7 %rest.7 = (f32[40,8,128]{2,1,0:T(8,128)S(1)}, f32[40,8,128]{2,1,0:T(8,128)S(1)}, f32[4,8,128]{2,1,0:T(8,128)S(1)}, f32[4,8,128]{2,1,0:T(8,128)S(1)}) custom-call(f32[3,40,1,128]{3,2,1,0:T(1,128)S(1)} %get-tuple-element.51.refs_0_, bf16[20,512,256]{2,1,0:T(8,128)(2,1)S(1)} %get-tuple-element.52.refs_1_, bf16[20,512,256]{2,1,0:T(8,128)(2,1)S(1)} %get-tuple-element.53.refs_2_, ...), custom_call_target="tpu_custom_call" | custom-call | flops 33554432 | bytes 4194304 | tf_op jit(solution)/shard_map/rest/pallas_call | solution.py:582
  23.1 0.3 collective-permute-start.4
  23.4 1.5 %collective-permute-start.5 = (f32[4,8,128]{2,1,0:T(8,128)S(1)}, f32[4,8,128]{2,1,0:T(8,128)S(1)}, u32[]{:S(2)}, u32[]{:S(2)}) collective-permute-start(f32[4,8,128]{2,1,0:T(8,128)S(1)} %get-tuple-element.73), channel_id=1, source_target_pairs={{1,2},{3,4},{5,6},{7,8},{9,10},{11,12},{13,14},{17,18},{19,20},{21... | collective-permute-start | bytes 49160 | tf_op jit(solution)/shard_map/ppermute | solution.py:527
  24.9 2.4 %inner.6 = (f32[40,8,128]{2,1,0:T(8,128)S(1)}, f32[40,8,128]{2,1,0:T(8,128)S(1)}) custom-call(f32[3,40,1,128]{3,2,1,0:T(1,128)S(1)} %get-tuple-element.51.refs_0_, bf16[20,512,256]{2,1,0:T(8,128)(2,1)S(1)} %get-tuple-element.52.refs_1_, bf16[20,512,256]{2,1,0:T(8,128)(2,1)S(1)} %get-tuple-element.53.refs_2_, f32[40,1,128]{2,1,0:T(1,128)S(1)} %get-tuple-element.54.refs_3_, ...), custom_call_target="tpu_custom_call" | custom-call | flops 142606336 | bytes 17825792 | tf_op jit(solution)/shard_map/inner/pallas_call | solution.py:565
  27.3 0.0 collective-permute-done.4.refs_5_
  27.3 0.0 collective-permute-done.5.refs_6_
  27.3 0.7 %rest.8 = (f32[40,8,128]{2,1,0:T(8,128)S(1)}, f32[40,8,128]{2,1,0:T(8,128)S(1)}, f32[4,8,128]{2,1,0:T(8,128)S(1)}, f32[4,8,128]{2,1,0:T(8,128)S(1)}) custom-call(f32[3,40,1,128]{3,2,1,0:T(1,128)S(1)} %get-tuple-element.51.refs_0_, bf16[20,512,256]{2,1,0:T(8,128)(2,1)S(1)} %get-tuple-element.52.refs_1_, bf16[20,512,256]{2,1,0:T(8,128)(2,1)S(1)} %get-tuple-element.53.refs_2_, ...), custom_call_target="tpu_custom_call" | custom-call | flops 33554432 | bytes 4194304 | tf_op jit(solution)/shard_map/rest/pallas_call | solution.py:582
  28.0 1.6 %collective-permute-start.6 = (f32[4,8,128]{2,1,0:T(8,128)S(1)}, f32[4,8,128]{2,1,0:T(8,128)S(1)}, u32[]{:S(2)}, u32[]{:S(2)}) collective-permute-start(f32[4,8,128]{2,1,0:T(8,128)S(1)} %get-tuple-element.77), channel_id=1, source_target_pairs={{0,1},{1,0},{2,3},{3,2},{4,5},{5,4},{6,7},{7,6},{8,9},{9,8},{10,11... | collective-permute-start | bytes 49160 | tf_op jit(solution)/shard_map/ppermute | solution.py:528
  29.7 1.5 %collective-permute-start.7 = (f32[4,8,128]{2,1,0:T(8,128)S(1)}, f32[4,8,128]{2,1,0:T(8,128)S(1)}, u32[]{:S(2)}, u32[]{:S(2)}) collective-permute-start(f32[4,8,128]{2,1,0:T(8,128)S(1)} %get-tuple-element.78), channel_id=1, source_target_pairs={{1,2},{3,4},{5,6},{7,8},{9,10},{11,12},{13,14},{17,18},{19,20},{21... | collective-permute-start | bytes 49160 | tf_op jit(solution)/shard_map/ppermute | solution.py:527
  31.1 2.4 %inner.7 = (f32[40,8,128]{2,1,0:T(8,128)S(1)}, f32[40,8,128]{2,1,0:T(8,128)S(1)}) custom-call(f32[3,40,1,128]{3,2,1,0:T(1,128)S(1)} %get-tuple-element.51.refs_0_, bf16[20,512,256]{2,1,0:T(8,128)(2,1)S(1)} %get-tuple-element.52.refs_1_, bf16[20,512,256]{2,1,0:T(8,128)(2,1)S(1)} %get-tuple-element.53.refs_2_, f32[40,1,128]{2,1,0:T(1,128)S(1)} %get-tuple-element.54.refs_3_, ...), custom_call_target="tpu_custom_call" | custom-call | flops 142606336 | bytes 17825792 | tf_op jit(solution)/shard_map/inner/pallas_call | solution.py:565
  33.6 0.0 collective-permute-done.6.refs_5_
  33.6 0.0 collective-permute-done.7.refs_6_
  33.6 0.7 %rest.9 = (f32[40,8,128]{2,1,0:T(8,128)S(1)}, f32[40,8,128]{2,1,0:T(8,128)S(1)}, f32[4,8,128]{2,1,0:T(8,128)S(1)}, f32[4,8,128]{2,1,0:T(8,128)S(1)}) custom-call(f32[3,40,1,128]{3,2,1,0:T(1,128)S(1)} %get-tuple-element.51.refs_0_, bf16[20,512,256]{2,1,0:T(8,128)(2,1)S(1)} %get-tuple-element.52.refs_1_, bf16[20,512,256]{2,1,0:T(8,128)(2,1)S(1)} %get-tuple-element.53.refs_2_, ...), custom_call_target="tpu_custom_call" | custom-call | flops 33554432 | bytes 4194304 | tf_op jit(solution)/shard_map/rest/pallas_call | solution.py:582
  34.3 0.2 collective-permute-start.8
  34.5 1.5 %collective-permute-start.9 = (f32[4,8,128]{2,1,0:T(8,128)S(1)}, f32[4,8,128]{2,1,0:T(8,128)S(1)}, u32[]{:S(2)}, u32[]{:S(2)}) collective-permute-start(f32[4,8,128]{2,1,0:T(8,128)S(1)} %get-tuple-element.83), channel_id=1, source_target_pairs={{1,2},{3,4},{5,6},{7,8},{9,10},{11,12},{13,14},{17,18},{19,20},{21... | collective-permute-start | bytes 49160 | tf_op jit(solution)/shard_map/ppermute | solution.py:527
  36.0 2.6 %inner.8 = (f32[40,8,128]{2,1,0:T(8,128)S(1)}, f32[40,8,128]{2,1,0:T(8,128)S(1)}) custom-call(f32[3,40,1,128]{3,2,1,0:T(1,128)S(1)} %get-tuple-element.51.refs_0_, bf16[20,512,256]{2,1,0:T(8,128)(2,1)S(1)} %get-tuple-element.52.refs_1_, bf16[20,512,256]{2,1,0:T(8,128)(2,1)S(1)} %get-tuple-element.53.refs_2_, f32[40,1,128]{2,1,0:T(1,128)S(1)} %get-tuple-element.54.refs_3_, ...), custom_call_target="tpu_custom_call" | custom-call | flops 142606336 | bytes 17825792 | tf_op jit(solution)/shard_map/inner/pallas_call | solution.py:565
  38.6 0.0 collective-permute-done.8.refs_5_
  38.6 0.0 collective-permute-done.9.refs_6_
  38.6 0.7 %rest.10 = (f32[40,8,128]{2,1,0:T(8,128)S(1)}, f32[40,8,128]{2,1,0:T(8,128)S(1)}, f32[4,8,128]{2,1,0:T(8,128)S(1)}, f32[4,8,128]{2,1,0:T(8,128)S(1)}) custom-call(f32[3,40,1,128]{3,2,1,0:T(1,128)S(1)} %get-tuple-element.51.refs_0_, bf16[20,512,256]{2,1,0:T(8,128)(2,1)S(1)} %get-tuple-element.52.refs_1_, bf16[20,512,256]{2,1,0:T(8,128)(2,1)S(1)} %get-tuple-element.53.refs_2_, ...), custom_call_target="tpu_custom_call" | custom-call | flops 33554432 | bytes 4194304 | tf_op jit(solution)/shard_map/rest/pallas_call | solution.py:582
  39.3 0.2 collective-permute-start.10
  39.6 1.5 %collective-permute-start.11 = (f32[4,8,128]{2,1,0:T(8,128)S(1)}, f32[4,8,128]{2,1,0:T(8,128)S(1)}, u32[]{:S(2)}, u32[]{:S(2)}) collective-permute-start(f32[4,8,128]{2,1,0:T(8,128)S(1)} %get-tuple-element.88), channel_id=1, source_target_pairs={{1,2},{3,4},{5,6},{7,8},{9,10},{11,12},{13,14},{17,18},{19,20},{21... | collective-permute-start | bytes 49160 | tf_op jit(solution)/shard_map/ppermute | solution.py:527
  41.0 2.7 %inner.9 = (f32[40,8,128]{2,1,0:T(8,128)S(1)}, f32[40,8,128]{2,1,0:T(8,128)S(1)}, f32[8,128]{1,0:T(8,128)S(1)}) custom-call(f32[3,40,1,128]{3,2,1,0:T(1,128)S(1)} %get-tuple-element.51.refs_0_, bf16[20,512,256]{2,1,0:T(8,128)(2,1)S(1)} %get-tuple-element.52.refs_1_, bf16[20,512,256]{2,1,0:T(8,128)(2,1)S(1)} %get-tuple-element.53.refs_2_, ...), custom_call_target="tpu_custom_call" | custom-call | flops 142606336 | bytes 17825792 | tf_op jit(solution)/shard_map/inner/pallas_call | solution.py:565
  43.8 0.0 collective-permute-done.10.refs_5_
  43.8 0.0 collective-permute-done.11.refs_6_
  43.8 0.9 %rest.11 = (f32[40,8,128]{2,1,0:T(8,128)S(1)}, f32[40,8,128]{2,1,0:T(8,128)S(1)}, f32[8,128]{1,0:T(8,128)S(1)}) custom-call(f32[3,40,1,128]{3,2,1,0:T(1,128)S(1)} %get-tuple-element.51.refs_0_, bf16[20,512,256]{2,1,0:T(8,128)(2,1)S(1)} %get-tuple-element.52.refs_1_, bf16[20,512,256]{2,1,0:T(8,128)(2,1)S(1)} %get-tuple-element.53.refs_2_, ...), custom_call_target="tpu_custom_call" | custom-call | flops 33554432 | bytes 4194304 | tf_op jit(solution)/shard_map/rest/pallas_call | solution.py:582
  44.6 0.2 collective-permute-start.12
  44.9 1.0 %collective-permute-done.12 = f32[8,128]{1,0:T(8,128)S(1)} collective-permute-done((f32[8,128]{1,0:T(8,128)S(1)}, f32[8,128]{1,0:T(8,128)S(1)}, u32[]{:S(2)}, u32[]{:S(2)}) %collective-permute-start.12) | collective-permute-done | bytes 4128 | tf_op jit(solution)/shard_map/ppermute | solution.py:607
  45.9 1.3 %collective-permute-start.13 = (f32[8,128]{1,0:T(8,128)S(1)}, f32[8,128]{1,0:T(8,128)S(1)}, u32[]{:S(2)}, u32[]{:S(2)}) collective-permute-start(f32[8,128]{1,0:T(8,128)S(1)} %add.12), channel_id=1, source_target_pairs={{0,2},{1,3},{2,0},{3,1},{4,6},{5,7},{6,4},{7,5},{8,10},{9,11},{10,... | collective-permute-start | bytes 12296 | tf_op jit(solution)/shard_map/ppermute | solution.py:607
  47.2 2.3 %collective-permute-done.13 = f32[8,128]{1,0:T(8,128)S(1)} collective-permute-done((f32[8,128]{1,0:T(8,128)S(1)}, f32[8,128]{1,0:T(8,128)S(1)}, u32[]{:S(2)}, u32[]{:S(2)}) %collective-permute-start.13) | collective-permute-done | bytes 4128 | tf_op jit(solution)/shard_map/ppermute | solution.py:607
  49.5 1.4 %collective-permute-start.14 = (f32[8,128]{1,0:T(8,128)S(1)}, f32[8,128]{1,0:T(8,128)S(1)}, u32[]{:S(2)}, u32[]{:S(2)}) collective-permute-start(f32[8,128]{1,0:T(8,128)S(1)} %add.13), channel_id=1, source_target_pairs={{0,4},{1,5},{2,6},{3,7},{4,0},{5,1},{6,2},{7,3},{8,12},{9,13},{10,... | collective-permute-start | bytes 12296 | tf_op jit(solution)/shard_map/ppermute | solution.py:607
  50.9 2.2 %collective-permute-done.14 = f32[8,128]{1,0:T(8,128)S(1)} collective-permute-done((f32[8,128]{1,0:T(8,128)S(1)}, f32[8,128]{1,0:T(8,128)S(1)}, u32[]{:S(2)}, u32[]{:S(2)}) %collective-permute-start.14) | collective-permute-done | bytes 4128 | tf_op jit(solution)/shard_map/ppermute | solution.py:607
  53.1 2.4 %collective-permute-start.15 = (f32[8,128]{1,0:T(8,128)S(1)}, f32[8,128]{1,0:T(8,128)S(1)}, u32[]{:S(2)}, u32[]{:S(2)}) collective-permute-start(f32[8,128]{1,0:T(8,128)S(1)} %add.14), channel_id=1, source_target_pairs={{0,8},{1,9},{2,10},{3,11},{4,12},{5,13},{6,14},{7,15},{8,0},{9,1},... | collective-permute-start | bytes 12296 | tf_op jit(solution)/shard_map/ppermute | solution.py:607
  55.5 2.1 %collective-permute-done.15 = f32[8,128]{1,0:T(8,128)S(1)} collective-permute-done((f32[8,128]{1,0:T(8,128)S(1)}, f32[8,128]{1,0:T(8,128)S(1)}, u32[]{:S(2)}, u32[]{:S(2)}) %collective-permute-start.15) | collective-permute-done | bytes 4128 | tf_op jit(solution)/shard_map/ppermute | solution.py:607
  57.6 1.3 %finish.1 = (f32[4,5120]{1,0:T(4,128)}, f32[4,5120]{1,0:T(4,128)}) custom-call(f32[8,128]{1,0:T(8,128)S(1)} %add.15.total_gram, f32[40,8,128]{2,1,0:T(8,128)S(1)} %get-tuple-element.55.refs_4_.refs_5_.refs_10_.refs_0_, f32[40,8,128]{2,1,0:T(8,128)S(1)} %get-tuple-element.89.refs_6_.refs_11_.refs_1_, ...), custom_call_target="tpu_custom_call" | custom-call | tf_op jit(solution)/shard_map/finish/pallas_call | solution.py:609
  (4 shorter events, 0.0 us)
Async XLA Ops:
  0.6 4.5 %copy-start = (f32[4,5120]{1,0:T(4,128)S(1)}, f32[4,5120]{1,0:T(4,128)}, u32[]{:S(2)}) copy-start(f32[4,5120]{1,0:T(4,128)} %rhs.1) | copy-start | bytes 245764
  0.6 4.5 %copy-start.1 = (f32[5120]{0:T(1024)S(1)}, f32[5120]{0:T(1024)}, u32[]{:S(2)}) copy-start(f32[5120]{0:T(1024)} %param.6) | copy-start | bytes 61444
  0.7 4.5 %copy-start.2 = (s32[40,4]{0,1:T(4,128)S(1)}, s32[40,4]{0,1:T(4,128)}, u32[]{:S(2)}) copy-start(s32[40,4]{0,1:T(4,128)} %param.5) | copy-start | bytes 1924
  2.0 13.8 %collective-permute-start = (f32[1064,128]{1,0:T(8,128)S(1)}, f32[1064,128]{1,0:T(8,128)S(1)}, u32[]{:S(2)}, u32[]{:S(2)}) collective-permute-start(f32[1064,128]{1,0:T(8,128)S(1)} %get-tuple-element.56), channel_id=1, source_target_pairs={{0,1},{1,0},{2,3},{3,2},{4,5},{5,4},{6,7},{7,6},{8,9},{9,8},{10,11... | collective-permute-start | bytes 1634312 | tf_op jit(solution)/shard_map/ppermute | solution.py:528
  2.5 13.3 %collective-permute-start.1 = (f32[1064,128]{1,0:T(8,128)S(1)}, f32[1064,128]{1,0:T(8,128)S(1)}, u32[]{:S(2)}, u32[]{:S(2)}) collective-permute-start(f32[1064,128]{1,0:T(8,128)S(1)} %get-tuple-element.57), channel_id=1, source_target_pairs={{1,2},{3,4},{5,6},{7,8},{9,10},{11,12},{13,14},{17,18},{19,20},{21... | collective-permute-start | bytes 1634312 | tf_op jit(solution)/shard_map/ppermute | solution.py:527
  17.0 3.8 %collective-permute-start.2 = (f32[4,8,128]{2,1,0:T(8,128)S(1)}, f32[4,8,128]{2,1,0:T(8,128)S(1)}, u32[]{:S(2)}, u32[]{:S(2)}) collective-permute-start(f32[4,8,128]{2,1,0:T(8,128)S(1)} %get-tuple-element.61), channel_id=1, source_target_pairs={{0,1},{1,0},{2,3},{3,2},{4,5},{5,4},{6,7},{7,6},{8,9},{9,8},{10,11... | collective-permute-start | bytes 49160 | tf_op jit(solution)/shard_map/ppermute | solution.py:528
  18.7 3.7 %collective-permute-start.3 = (f32[4,8,128]{2,1,0:T(8,128)S(1)}, f32[4,8,128]{2,1,0:T(8,128)S(1)}, u32[]{:S(2)}, u32[]{:S(2)}) collective-permute-start(f32[4,8,128]{2,1,0:T(8,128)S(1)} %get-tuple-element.62), channel_id=1, source_target_pairs={{1,2},{3,4},{5,6},{7,8},{9,10},{11,12},{13,14},{17,18},{19,20},{21... | collective-permute-start | bytes 49160 | tf_op jit(solution)/shard_map/ppermute | solution.py:527
  23.1 4.2 %collective-permute-start.4 = (f32[4,8,128]{2,1,0:T(8,128)S(1)}, f32[4,8,128]{2,1,0:T(8,128)S(1)}, u32[]{:S(2)}, u32[]{:S(2)}) collective-permute-start(f32[4,8,128]{2,1,0:T(8,128)S(1)} %get-tuple-element.72), channel_id=1, source_target_pairs={{0,1},{1,0},{2,3},{3,2},{4,5},{5,4},{6,7},{7,6},{8,9},{9,8},{10,11... | collective-permute-start | bytes 49160 | tf_op jit(solution)/shard_map/ppermute | solution.py:528
  23.4 3.9 %collective-permute-start.5 = (f32[4,8,128]{2,1,0:T(8,128)S(1)}, f32[4,8,128]{2,1,0:T(8,128)S(1)}, u32[]{:S(2)}, u32[]{:S(2)}) collective-permute-start(f32[4,8,128]{2,1,0:T(8,128)S(1)} %get-tuple-element.73), channel_id=1, source_target_pairs={{1,2},{3,4},{5,6},{7,8},{9,10},{11,12},{13,14},{17,18},{19,20},{21... | collective-permute-start | bytes 49160 | tf_op jit(solution)/shard_map/ppermute | solution.py:527
  28.0 5.5 %collective-permute-start.6 = (f32[4,8,128]{2,1,0:T(8,128)S(1)}, f32[4,8,128]{2,1,0:T(8,128)S(1)}, u32[]{:S(2)}, u32[]{:S(2)}) collective-permute-start(f32[4,8,128]{2,1,0:T(8,128)S(1)} %get-tuple-element.77), channel_id=1, source_target_pairs={{0,1},{1,0},{2,3},{3,2},{4,5},{5,4},{6,7},{7,6},{8,9},{9,8},{10,11... | collective-permute-start | bytes 49160 | tf_op jit(solution)/shard_map/ppermute | solution.py:528
  29.7 3.9 %collective-permute-start.7 = (f32[4,8,128]{2,1,0:T(8,128)S(1)}, f32[4,8,128]{2,1,0:T(8,128)S(1)}, u32[]{:S(2)}, u32[]{:S(2)}) collective-permute-start(f32[4,8,128]{2,1,0:T(8,128)S(1)} %get-tuple-element.78), channel_id=1, source_target_pairs={{1,2},{3,4},{5,6},{7,8},{9,10},{11,12},{13,14},{17,18},{19,20},{21... | collective-permute-start | bytes 49160 | tf_op jit(solution)/shard_map/ppermute | solution.py:527
  34.3 4.3 %collective-permute-start.8 = (f32[4,8,128]{2,1,0:T(8,128)S(1)}, f32[4,8,128]{2,1,0:T(8,128)S(1)}, u32[]{:S(2)}, u32[]{:S(2)}) collective-permute-start(f32[4,8,128]{2,1,0:T(8,128)S(1)} %get-tuple-element.82), channel_id=1, source_target_pairs={{0,1},{1,0},{2,3},{3,2},{4,5},{5,4},{6,7},{7,6},{8,9},{9,8},{10,11... | collective-permute-start | bytes 49160 | tf_op jit(solution)/shard_map/ppermute | solution.py:528
  34.5 4.1 %collective-permute-start.9 = (f32[4,8,128]{2,1,0:T(8,128)S(1)}, f32[4,8,128]{2,1,0:T(8,128)S(1)}, u32[]{:S(2)}, u32[]{:S(2)}) collective-permute-start(f32[4,8,128]{2,1,0:T(8,128)S(1)} %get-tuple-element.83), channel_id=1, source_target_pairs={{1,2},{3,4},{5,6},{7,8},{9,10},{11,12},{13,14},{17,18},{19,20},{21... | collective-permute-start | bytes 49160 | tf_op jit(solution)/shard_map/ppermute | solution.py:527
  39.3 4.4 %collective-permute-start.10 = (f32[4,8,128]{2,1,0:T(8,128)S(1)}, f32[4,8,128]{2,1,0:T(8,128)S(1)}, u32[]{:S(2)}, u32[]{:S(2)}) collective-permute-start(f32[4,8,128]{2,1,0:T(8,128)S(1)} %get-tuple-element.87), channel_id=1, source_target_pairs={{0,1},{1,0},{2,3},{3,2},{4,5},{5,4},{6,7},{7,6},{8,9},{9,8},{10,11... | collective-permute-start | bytes 49160 | tf_op jit(solution)/shard_map/ppermute | solution.py:528
  39.6 4.2 %collective-permute-start.11 = (f32[4,8,128]{2,1,0:T(8,128)S(1)}, f32[4,8,128]{2,1,0:T(8,128)S(1)}, u32[]{:S(2)}, u32[]{:S(2)}) collective-permute-start(f32[4,8,128]{2,1,0:T(8,128)S(1)} %get-tuple-element.88), channel_id=1, source_target_pairs={{1,2},{3,4},{5,6},{7,8},{9,10},{11,12},{13,14},{17,18},{19,20},{21... | collective-permute-start | bytes 49160 | tf_op jit(solution)/shard_map/ppermute | solution.py:527
  44.6 1.2 %collective-permute-start.12 = (f32[8,128]{1,0:T(8,128)S(1)}, f32[8,128]{1,0:T(8,128)S(1)}, u32[]{:S(2)}, u32[]{:S(2)}) collective-permute-start(f32[8,128]{1,0:T(8,128)S(1)} %get-tuple-element.97), channel_id=1, source_target_pairs={{0,1},{1,0},{2,3},{3,2},{4,5},{5,4},{6,7},{7,6},{8,9},{9,8},{10,11... | collective-permute-start | bytes 12296 | tf_op jit(solution)/shard_map/ppermute | solution.py:607
  45.9 3.6 %collective-permute-start.13 = (f32[8,128]{1,0:T(8,128)S(1)}, f32[8,128]{1,0:T(8,128)S(1)}, u32[]{:S(2)}, u32[]{:S(2)}) collective-permute-start(f32[8,128]{1,0:T(8,128)S(1)} %add.12), channel_id=1, source_target_pairs={{0,2},{1,3},{2,0},{3,1},{4,6},{5,7},{6,4},{7,5},{8,10},{9,11},{10,... | collective-permute-start | bytes 12296 | tf_op jit(solution)/shard_map/ppermute | solution.py:607
  49.5 3.6 %collective-permute-start.14 = (f32[8,128]{1,0:T(8,128)S(1)}, f32[8,128]{1,0:T(8,128)S(1)}, u32[]{:S(2)}, u32[]{:S(2)}) collective-permute-start(f32[8,128]{1,0:T(8,128)S(1)} %add.13), channel_id=1, source_target_pairs={{0,4},{1,5},{2,6},{3,7},{4,0},{5,1},{6,2},{7,3},{8,12},{9,13},{10,... | collective-permute-start | bytes 12296 | tf_op jit(solution)/shard_map/ppermute | solution.py:607
  53.1 4.5 %collective-permute-start.15 = (f32[8,128]{1,0:T(8,128)S(1)}, f32[8,128]{1,0:T(8,128)S(1)}, u32[]{:S(2)}, u32[]{:S(2)}) collective-permute-start(f32[8,128]{1,0:T(8,128)S(1)} %add.14), channel_id=1, source_target_pairs={{0,8},{1,9},{2,10},{3,11},{4,12},{5,13},{6,14},{7,15},{8,0},{9,1},... | collective-permute-start | bytes 12296 | tf_op jit(solution)/shard_map/ppermute | solution.py:607

commit v6 on v5

v6 whole, which is shorter than its diff:
```python
import functools
import math

import jax
import jax.numpy as jnp
import numpy as np
from jax import lax
from jax.experimental import pallas as pl
from jax.experimental.pallas import tpu as pltpu
from jax.sharding import PartitionSpec as P

W = 2
S = 6
CYCLES = 2
CHAIN = S * CYCLES
GROUPS = (3, 3, 3, 3)
SCALE = 0.125
GROW = 1.0 / SCALE
SHIFTS = [
    float(np.float32(1.6) + np.float32(0.8) * np.float32(math.cos(math.pi * (2 * j + 1) / (2 * S))))
    for j in range(S)
]
F32 = jnp.float32
BF16 = jnp.bfloat16
VM = pl.BlockSpec(memory_space=pltpu.VMEM)
HB = pl.BlockSpec(memory_space=pltpu.HBM)


def params(mib):
    return pltpu.CompilerParams(vmem_limit_bytes=mib << 20)


def halves():
    return lax.broadcasted_iota(jnp.int32, (8, 128), 0) < 4


def split(tile, mask):
    high = tile.astype(BF16).astype(F32)
    return jnp.where(mask, high, tile - high)


def store_pair(block, high_ref, low_ref, pair, half, k, factor=SCALE):
    block = block * factor
    high = block.astype(BF16)
    low = (block - high.astype(F32)).astype(BF16)
    rows, cols = slice(k * 128, (k + 1) * 128), slice(half * 128, (half + 1) * 128)
    high_ref[pair, rows, cols] = high.T
    low_ref[pair, rows, cols] = low.T


def neighbour_slots():
    return [(r, c) for r in range(2) for c in range(4) if (r, c) not in ((1, 0), (0, 3))] + [None]


def prep_kernel(blocks, diag, offs, even, odd, buf, diag_buf, offs_buf, sems):
    rows = diag.shape[0]
    parity = lax.axis_index("dom") % 2
    sides = ((even, 1 - parity), (odd, parity))
    small = [
        pltpu.make_async_copy(diag, diag_buf, sems.at[0]),
        pltpu.make_async_copy(offs, offs_buf, sems.at[1]),
    ]
    large = []
    for place, (ref, at) in enumerate(sides):
        first = pl.multiple_of(at * (rows - 2) * 512, 512)
        large.append(pltpu.make_async_copy(blocks.at[pl.ds(first, 1024)], buf.at[place], sems.at[2 + place]))
    for copy in large + small:
        copy.start()
    for copy in small:
        copy.wait()
    offsets = offs_buf[...].astype(F32)
    masks = []
    for ref, at in sides:
        last = at == 1
        places = jnp.where(last, offsets[:, rows - 2 :], offsets[:, :2])
        places = [
            [jnp.broadcast_to(places[k : k + 1, r : r + 1], (128, 128)) for k in range(4)] for r in range(2)
        ]
        own = jnp.where(last, diag_buf[rows - 2 :, :], diag_buf[:2, :])
        base = 128 * len(neighbour_slots())
        ref[base : base + 2, :] = own
        ref[base + 2 : base + 8, :] = jnp.zeros((6, 128), F32)
        masks.append((jnp.where(last, 0.0, -2.0), last, places))
    for number, (ref, at) in enumerate(sides):
        large[number].wait()
        shift, last, places = masks[number]
        parts = [[buf[number, (r * 4 + k) * 128 : (r * 4 + k + 1) * 128, :] for k in range(4)] for r in range(2)]

        def block(r, c):
            total = jnp.zeros((128, 128), F32)
            for k in range(4):
                total = jnp.where(places[r][k] == c - r + shift, parts[r][k], total)
            return total

        for at_slot, slot in enumerate(neighbour_slots()):
            here = jnp.where(last, block(1, 0), block(0, 3)) if slot is None else block(*slot)
            ref[at_slot * 128 : (at_slot + 1) * 128, :] = here


def at_inside():
    me = lax.axis_index("dom")
    return jnp.logical_and(me > 0, me < lax.axis_size("dom") - 1)


def take_vectors(parity, even, odd, halo):
    inside = at_inside()
    for i in range(even.shape[0]):
        halo[1 - parity, i] = even[i]
        tile = odd[i]
        halo[parity, i] = jnp.where(inside, tile, jnp.zeros_like(tile))


def take_message(parity, even, odd, high, low, scaled):
    factor = jnp.where(at_inside(), SCALE, 0.0)
    for ref, side, by in ((even, 1 - parity, SCALE), (odd, parity, factor)):
        left = side == 0
        for at_slot, slot in enumerate(neighbour_slots()):
            block = ref[at_slot * 128 : (at_slot + 1) * 128, :]
            if slot is None:
                none = jnp.zeros_like(block)
                store_pair(jnp.where(left, block, none), high, low, side, 1, 0, by)
                store_pair(jnp.where(left, none, block), high, low, side, 0, 3, by)
            else:
                store_pair(block, high, low, side, slot[0], slot[1], by)
        base = 128 * len(neighbour_slots())
        for r in range(2):
            scaled[side, r] = ref[base + r : base + r + 1, :] * SCALE


class Chain:
    def __init__(self, rows, shifts, places, high, low, scaled):
        self.rows, self.shifts = rows, shifts
        self.places, self.high, self.low, self.scaled = places, high, low, scaled
        self.mask = halves()

    def gather(self, source, row, k):
        if k == 0:
            return source[row + W]
        place = jnp.broadcast_to(self.places[k - 1, row], (8, 128))
        total = source[row + 2 * W]
        for c in (-W, 1 - W, W - 1):
            total = jnp.where(place == c, source[row + W + c], total)
        return total

    def fill(self, source, rows, value):
        for row in rows:
            source[row + W] = split(value(row), self.mask)

    def product(self, left, high, low):
        return jnp.dot(left, high, preferred_element_type=F32) + jnp.dot(left, low, preferred_element_type=F32)

    def part(self, total, h):
        part = total[8 * h : 8 * h + 8, 128 * h : 128 * h + 128]
        return part + pltpu.roll(part, 4, 0)

    def advance(self, step, pairs, source, value, emit, extra=()):
        streamed = []
        for row in pairs:
            parts = []
            for k in range(4):
                tiles = [self.gather(source, row + h, k) for h in range(2)]
                parts.append(jnp.concatenate(tiles, 0).astype(BF16))
            streamed.append(jnp.concatenate(parts, 1))
        more = [self.product(left, high, low) for left, high, low, _ in extra]
        sums = [self.product(left, self.high[row // 2], self.low[row // 2]) for row, left in zip(pairs, streamed)]
        for total, (_, _, _, use) in zip(more, extra):
            use(total)
        for row, total in zip(pairs, sums):
            for h in range(2):
                at = row + h
                emit(at, self.part(total, h) + (self.scaled[at] - SCALE * self.shifts[step]) * value(at))


def edge_pairs(rows, depth):
    return list(range(0, depth, 2)) + list(range(rows - depth, rows, 2))


def inner_rows(rows, step):
    return list(range(W * step, rows - W * step))


def around(pairs, rows):
    return sorted({p + c for p in pairs for c in range(-W, W + 2)} & set(range(rows)))


def send_edges(chain, steps, last, to_even, to_odd, sources):
    rows = chain.rows
    parity = lax.axis_index("dom") % 2
    values = {row: last[row] for row in around(edge_pairs(rows, W * steps), rows)}
    for step in range(steps):
        for h in range(2):
            low, top = values[h], values[rows - 2 + h]
            to_even[2 * step + h] = jnp.where(parity == 0, top, low)
            to_odd[2 * step + h] = jnp.where(parity == 0, low, top)
        if step == steps - 1:
            break
        source = sources[step]
        for row in (0, 1, rows + W, rows + W + 1):
            source[row] = jnp.zeros((8, 128), F32)
        pairs = edge_pairs(rows, W * (steps - 1 - step))
        chain.fill(source, around(pairs, rows), values.get)
        found = {}
        chain.advance(step, pairs, source, values.get, found.__setitem__)
        values = found


def convert_kernel(steps, shifts, *refs):
    blocks, rhs, diag, offs, start, scaled, places, high, low, to_even, to_odd = refs[:11]
    sources = refs[11 : 10 + steps]
    buf, sems = refs[10 + steps :]
    rows = buf.shape[0]

    def fetch(i):
        first = pl.multiple_of(i * 512, 512)
        return pltpu.make_async_copy(blocks.at[pl.ds(first, 512)], buf.at[i], sems.at[i])

    for i in range(rows):
        fetch(i).start()
    for i in range(rows):
        part = rhs[:, i * 128 : (i + 1) * 128]
        start[i] = jnp.concatenate([part, part], 0)
        scaled[i] = diag[i : i + 1, :] * SCALE
    turned = jnp.concatenate([offs[...].astype(F32), jnp.zeros((4, 128 - rows), F32)], 1)
    turned = jnp.concatenate([turned, jnp.zeros((4, 128), F32)], 0).T
    for k in range(1, 4):
        places[k - 1] = jnp.broadcast_to(turned[:rows, k : k + 1], (rows, 128)).reshape(rows, 1, 128)

    def body(p, carry):
        for half in range(2):
            i = 2 * p + half
            fetch(i).wait()
            for k in range(4):
                store_pair(buf[i, k * 128 : (k + 1) * 128, :], high, low, p, half, k)
        return carry

    lax.fori_loop(0, rows // 2, body, 0)
    chain = Chain(rows, shifts, places, high, low, scaled)
    send_edges(chain, steps, start, to_even, to_odd, sources)


def inner_kernel(steps, shifts, earlier, *refs):
    places, high, low, scaled, own = refs[:5]
    refs = list(refs[5:])
    before = refs[:earlier]
    del refs[:earlier]
    outs = refs[:steps]
    del refs[:steps]
    rows = own.shape[0]
    if earlier:
        products = refs.pop(0)
        vectors = before + [own]
        tile = jnp.zeros((8, 128), F32)
        products[...] = add_products(tile, vectors, pair_blocks((earlier + 1) // 2, earlier + 1))
    sources = refs
    chain = Chain(rows, shifts, places, high, low, scaled)
    chain.fill(sources[0], range(rows), lambda row: own[row])
    for step in range(steps):
        before = own if step == 0 else outs[step - 1]

        def emit(row, tile, step=step):
            outs[step][row] = tile
            if step < steps - 1:
                sources[step + 1][row + W] = split(tile, chain.mask)

        pairs = inner_rows(rows, step + 1)[::2]
        chain.advance(step, pairs, sources[step], lambda row, ref=before: ref[row], emit)


def rest_kernel(first, steps, shifts, next_steps, next_shifts, earlier, *refs):
    refs = list(refs)
    places, high, low, scaled, own, from_even, from_odd = refs[:7]
    del refs[:7]
    begun = refs[:steps]
    del refs[:steps]
    if first:
        bulk = refs[:2]
        del refs[:2]
    if earlier:
        products, before = refs[0], refs[1 : 1 + earlier]
        del refs[: 1 + earlier]
    side_high, side_low, side_scaled = refs[:3]
    del refs[:3]
    outs = refs[:steps]
    del refs[:steps]
    if earlier:
        gram = refs.pop(0)
    if next_steps:
        to_even, to_odd = refs[:2]
        del refs[:2]
    sources, halo = refs[:steps], refs[steps]
    more_sources = refs[steps + 1 :]
    rows = own.shape[0]
    parity = lax.axis_index("dom") % 2
    take_vectors(parity, from_even, from_odd, halo)
    if first:
        take_message(parity, *bulk, side_high, side_low, side_scaled)
    for j in range(steps):
        for row in inner_rows(rows, j + 1):
            outs[j][row] = begun[j][row]
    chain = Chain(rows, shifts, places, high, low, scaled)
    mask = chain.mask
    added = None
    for step in range(steps):
        source = sources[step]
        ref = own if step == 0 else outs[step - 1]
        pairs = edge_pairs(rows, W * (step + 1))
        known = around(pairs, rows)
        if step:
            known = [row for row in known if row in set(inner_rows(rows, step))]
        chain.fill(source, known, lambda row, ref=ref: ref[row])
        for side in range(2):
            for h in range(2):
                tile = halo[side, 2 * step + h]
                if added is not None:
                    tile = tile + added[side][h]
                source[h + side * (rows + W)] = split(tile, mask)
        extra, after = [], [[None] * 2 for _ in range(2)]
        if step < steps - 1:
            for side in range(2):
                near = [source[W + side * (rows - 2) + h] for h in range(2)]
                if added is None:
                    far = [jnp.zeros((8, 128), F32)] * 2
                else:
                    far = [split(tile, mask) for tile in added[side]]
                tiles = near + far if side else far + near
                left = jnp.concatenate([jnp.concatenate([t, t], 0).astype(BF16) for t in tiles], 1)

                def use(total, side=side, added=added, after=after, step=step):
                    for h in range(2):
                        tile = chain.part(total, h)
                        if added is not None:
                            tile = tile + (side_scaled[side, h] - SCALE * shifts[step]) * added[side][h]
                        after[side][h] = tile

                extra.append((left, side_high[side], side_low[side], use))

        def emit(row, tile, step=step):
            outs[step][row] = tile
            if step < steps - 1:
                sources[step + 1][row + W] = split(tile, mask)

        chain.advance(step, pairs, source, lambda row, ref=ref: ref[row], emit, extra)
        added = after
    if next_steps:
        chain = Chain(rows, next_shifts, places, high, low, scaled)
        send_edges(chain, next_steps, outs[-1], to_even, to_odd, more_sources)
    if earlier:
        vectors = list(before) + [own] + list(outs)
        new = [(i, j) for j in range(earlier + 1, earlier + 1 + steps) for i in range(j + 1)]
        tile = add_products(products[...], vectors, [new])
        gram[...] = tile + pltpu.roll(tile, 4, 0)


def pair_blocks(split, count):
    low, top = range(split), range(split, count)
    return (
        [(i, j) for i in low for j in low if i <= j],
        [(i, j) for i in low for j in top],
        [(i, j) for i in top for j in top if i <= j],
    )


PLACES = {pair: at for at, pair in enumerate((i, j) for j in range(CHAIN + 1) for i in range(j + 1))}


def dense(ref, p, mask):
    return jnp.where(mask, ref[2 * p], ref[2 * p + 1])


def add_products(tile, vectors, blocks):
    count = vectors[0].shape[0] // 2
    mask = halves()
    lane = lax.broadcasted_iota(jnp.int32, (8, 128), 1)
    for pairs in blocks:
        used = sorted({i for pair in pairs for i in pair})
        total = None
        for p in range(count):
            here = {i: dense(vectors[i], p, mask) for i in used}
            products = [here[i] * here[j] for i, j in pairs]
            total = products if total is None else [a + b for a, b in zip(total, products)]
        for pair, one in zip(pairs, total):
            tile = jnp.where(lane == PLACES[pair], jnp.sum(one, axis=1, keepdims=True), tile)
    return tile


def small_solve(gram):
    def g(i, j):
        return gram[(i, j) if i <= j else (j, i)]

    right = [[SHIFTS[b] * g(a, b) + GROW * g(a, b + 1) for b in range(S)] for a in range(S + 1)]
    normal = [
        [SHIFTS[a] * right[a][b] + GROW * right[a + 1][b] for b in range(a + 1)] for a in range(S)
    ]
    target = [SHIFTS[a] * g(a, 0) + GROW * g(a + 1, 0) for a in range(S)]
    lower = [[None] * S for _ in range(S)]
    scaled = [[None] * S for _ in range(S)]
    inverse = []
    for j in range(S):
        pivot = normal[j][j]
        for k in range(j):
            pivot = pivot - scaled[j][k] * lower[j][k]
        inverse.append(1.0 / pivot)
        for i in range(j + 1, S):
            entry = normal[i][j]
            for k in range(j):
                entry = entry - scaled[i][k] * lower[j][k]
            scaled[i][j] = entry
            lower[i][j] = entry * inverse[j]
    coeffs = list(target)
    for i in range(S):
        for k in range(i):
            coeffs[i] = coeffs[i] - lower[i][k] * coeffs[k]
    coeffs = [c * d for c, d in zip(coeffs, inverse)]
    for i in reversed(range(S)):
        for k in range(i + 1, S):
            coeffs[i] = coeffs[i] - lower[k][i] * coeffs[k]
    combine = []
    for m in range(S + 1):
        entry = jnp.ones_like(coeffs[0]) if m == 0 else -GROW * coeffs[m - 1]
        if m < S:
            entry = entry - SHIFTS[m] * coeffs[m]
        combine.append(entry)
    return coeffs, combine


def final_kernel(total_gram, *refs):
    vectors, solution_ref, residual_ref = refs[:-2], refs[-2], refs[-1]
    count = vectors[0].shape[0] // 2
    mask = halves()
    tile = total_gram[...]
    gram = {
        pair: jnp.broadcast_to(tile[:, at : at + 1], (8, 128)) for pair, at in PLACES.items()
    }

    def g(i, j):
        return gram[(i, j) if i <= j else (j, i)]

    coeffs, combine = small_solve(gram)
    columns = [combine]
    for k in range(S):
        last = columns[-1]
        column = []
        for m in range(len(last) + 1):
            entry = None
            if m < len(last):
                gap = SCALE * (SHIFTS[m % S] - SHIFTS[k])
                entry = gap * last[m] if m % S != k else None
            if m > 0:
                entry = last[m - 1] if entry is None else entry + last[m - 1]
            column.append(jnp.zeros_like(last[0]) if entry is None else entry)
        columns.append(column)
    second = {}
    for b in range(S + 1):
        image = []
        for m in range(len(columns[b])):
            total = None
            for i, c in enumerate(columns[b]):
                term = g(m, i) * c
                total = term if total is None else total + term
            image.append(total)
        for a in range(b + 1):
            total = None
            for m, c in enumerate(columns[a]):
                term = c * image[m]
                total = term if total is None else total + term
            second[(a, b)] = total
    more, ending = small_solve(second)
    to_solution, to_residual = [], []
    for m in range(CHAIN + 1):
        total = coeffs[m] if m < S else None
        for a in range(S):
            if m < len(columns[a]):
                term = more[a] * columns[a][m]
                total = term if total is None else total + term
        to_solution.append(total)
        total = None
        for a in range(S + 1):
            if m < len(columns[a]):
                term = ending[a] * columns[a][m]
                total = term if total is None else total + term
        to_residual.append(total)
    for p in range(count):
        here = [dense(ref, p, mask) for ref in vectors]
        for ref, weights in ((solution_ref, to_solution), (residual_ref, to_residual)):
            total = None
            for weight, one in zip(weights, here):
                if weight is not None:
                    total = weight * one if total is None else total + weight * one
            ref[:, (2 * p) * 128 : (2 * p + 1) * 128] = total[0:4]
            ref[:, (2 * p + 1) * 128 : (2 * p + 2) * 128] = total[4:8]


def shape(*dims, kind=F32):
    return jax.ShapeDtypeStruct(dims, kind)


def cost(block_rows):
    return pl.CostEstimate(flops=block_rows * 2**21, bytes_accessed=block_rows * 2**18, transcendentals=0)


def local(blocks, offsets, diag_shift, right_side):
    rhs_count = right_side.shape[0]
    rows, per_row, size = blocks.shape[0], blocks.shape[1], blocks.shape[2]
    count = lax.axis_size("dom")
    flat = pltpu.with_memory_space_constraint(blocks.reshape(rows * per_row * size, size), pltpu.HBM)
    offs = offsets.T
    diag = diag_shift.reshape(rows, size)
    message = shape(len(neighbour_slots()) * size + 8, size)
    even_blocks, odd_blocks = pl.pallas_call(
        prep_kernel,
        out_shape=[message, message],
        in_specs=[HB, HB, HB],
        out_specs=[VM] * 2,
        scratch_shapes=[
            pltpu.VMEM((2, 2 * per_row * size, size), F32),
            pltpu.VMEM(diag.shape, F32),
            pltpu.VMEM(offs.shape, jnp.int32),
            pltpu.SemaphoreType.DMA((4,)),
        ],
        compiler_params=params(16),
        name="prepare",
    )(flat, *[pltpu.with_memory_space_constraint(x, pltpu.HBM) for x in (diag, offs)])

    swap_even = [(i, i ^ 1) for i in range(count)]
    copies = lax.axis_size("groups")
    swap_odd = [(g * count + i, g * count + i + 1) for g in range(copies) for i in range(1, count - 1, 2)]
    for end in (0, count - 1):
        swap_odd += [(g * count + end, (g + 1) * count + end) for g in range(0, copies - 1, 2)]
    swap_odd += [(b, a) for a, b in swap_odd]

    def exchange(even, odd):
        odd = lax.ppermute(odd, ("groups", "dom"), swap_odd)
        return lax.ppermute(even, "dom", swap_even), odd

    bulk = exchange(even_blocks, odd_blocks)

    vector = shape(rows, 8, size)
    pair_shape = pltpu.VMEM((rows // 2, per_row * size, 2 * size), BF16)
    side_shape = pltpu.VMEM((2, per_row * size, 2 * size), BF16)
    source = pltpu.VMEM((rows + 2 * W, 8, size), F32)

    def shifts_from(at, steps):
        return [SHIFTS[(at + j) % S] for j in range(steps)]

    steps = GROUPS[0]
    edge = shape(2 * steps, 8, size)
    start, scaled, places, high, low, even, odd = pl.pallas_call(
        functools.partial(convert_kernel, steps, shifts_from(0, steps)),
        out_shape=[vector, shape(rows, 1, size), shape(per_row - 1, rows, 1, size)]
        + [pair_shape] * 2
        + [edge] * 2,
        in_specs=[HB, VM, VM, VM],
        out_specs=[VM] * 7,
        scratch_shapes=[source] * (steps - 1)
        + [pltpu.VMEM((rows, per_row * size, size), F32), pltpu.SemaphoreType.DMA((rows,))],
        compiler_params=params(24),
        cost_estimate=cost(2 * rows),
        name="convert",
    )(flat, right_side, diag, offs)

    vectors = [start]
    sides = None
    at = 0
    for number, steps in enumerate(GROUPS):
        even, odd = exchange(even, odd)
        shifts = shifts_from(at, steps)
        first, last = number == 0, number + 1 == len(GROUPS)
        before = vectors[:-1] if last else []
        begun = pl.pallas_call(
            functools.partial(inner_kernel, steps, shifts, len(before)),
            out_shape=[vector] * steps + [shape(8, size)] * last,
            in_specs=[VM] * (5 + len(before)),
            out_specs=[VM] * (steps + last),
            scratch_shapes=[source] * steps,
            compiler_params=params(16),
            cost_estimate=cost(sum(len(inner_rows(rows, j + 1)) for j in range(steps))),
            name="inner",
        )(places, high, low, scaled, vectors[-1], *before)
        begun, products = begun[:steps], begun[steps:]
        next_steps = 0 if last else GROUPS[number + 1]
        edge = shape(2 * next_steps, 8, size)
        outs = [vector] * steps + [shape(8, size)] * last + [edge] * (0 if last else 2)
        inputs = [places, high, low, scaled, vectors[-1], even, odd, *begun]
        if first:
            outs = [side_shape, side_shape, shape(2, 2, 1, size)] + outs
            inputs += bulk
        if last:
            inputs += [*products, *before]
        if not first:
            inputs += sides
        results = pl.pallas_call(
            functools.partial(
                rest_kernel,
                first,
                steps,
                shifts,
                next_steps,
                shifts_from(at + steps, next_steps),
                len(before),
            ),
            out_shape=outs,
            in_specs=[VM] * len(inputs),
            out_specs=[VM] * len(outs),
            scratch_shapes=[source] * steps
            + [pltpu.VMEM((2, 2 * steps, 8, size), F32)]
            + [source] * max(next_steps - 1, 0),
            compiler_params=params(16),
            cost_estimate=cost(16),
            name="rest",
        )(*inputs)
        results = list(results)
        if first:
            sides, results = results[:3], results[3:]
        vectors += results[:steps]
        at += steps
        if last:
            gram = results[steps]
        else:
            even, odd = results[steps:]

    if count & (count - 1):
        gram = lax.psum(gram, "dom")
    else:
        for stage in range(count.bit_length() - 1):
            gram = gram + lax.ppermute(gram, "dom", [(i, i ^ (1 << stage | 1)) for i in range(count)])
    return tuple(
        pl.pallas_call(
            final_kernel,
            out_shape=[shape(rhs_count, rows * size)] * 2,
            in_specs=[VM] * (1 + len(vectors)),
            out_specs=[VM] * 2,
            compiler_params=params(16),
            name="finish",
        )(gram, *vectors)
    )


def solution(mesh):
    in_specs = (
        P(("groups", "dom"), None, None, None),
        P(("groups", "dom"), None),
        P(("groups", "dom")),
        P(None, ("groups", "dom")),
    )
    out_specs = (P(None, ("groups", "dom")), P(None, ("groups", "dom")))
    return jax.shard_map(local, mesh=mesh, in_specs=in_specs, out_specs=out_specs, check_vma=False)
```

time: 59.1 us -> 53.2 us (0.900)
  starting transfers between devices: 19.9 us -> 14.4 us
  waiting for transfers between devices: 9.22 us -> 6.62 us
  Pallas kernels: 29 us -> 31.2 us
    ppermute x6 -> x5, starting transfers between devices: 4.51 us -> 1.23 us  [exchange(): return (lax.ppermute(even, 'dom', swap_even), odd)]
    pallas_call x13 -> x10, Pallas kernels: 27.7 us -> 29.9 us  [the longest x4 14 us: local(): pl.pallas_call(functools.partial(inner_kernel, steps, shifts, len(before)...]
    ppermute x6 -> x5, waiting for transfers between devices: 1.6 us -> 0.02 us  [exchange(): odd = lax.ppermute(odd, ('groups', 'dom'), swap_odd)]
    ppermute x6 -> x5, starting transfers between devices: 10 us -> 8.53 us  [exchange(): odd = lax.ppermute(odd, ('groups', 'dom'), swap_odd)]
    ppermute x4, waiting for transfers between devices: 7.6 us -> 6.59 us  [local(): lax.ppermute(gram, 'dom', [(i, i ^ (1 << stage | 1)) for i in range(count)])]
    ppermute x4, starting transfers between devices: 5.35 us -> 4.64 us  [local(): lax.ppermute(gram, 'dom', [(i, i ^ (1 << stage | 1)) for i in range(count)])]
  transfers between devices with their start and end apart: 16 -> 14, of which waited for: 5 -> 4; matrix products, arithmetic and copies ran while one was open for 0% -> 0% of each run, Pallas kernels for 37% -> 40%
where the time goes in v6:
time: 53.2 us; the launch traced here: 53 us
  Pallas kernels  31.2 us (59%)
  starting transfers between devices  14.4 us (27%)
  waiting for transfers between devices  6.62 us (12%)
  between operations  0.74 us (1%)
    pallas_call x4, Pallas kernels, local(): pl.pallas_call(functools.partial(inner_kernel, steps, shifts, len(before)...  14 us
    ppermute x5, starting transfers between devices, exchange(): odd = lax.ppermute(odd, ('groups', 'dom'), swap_odd)  8.53 us
    pallas_call x4, Pallas kernels, local(): pl.pallas_call(functools.partial(rest_kernel, first, steps, shifts, next_...  7.38 us
    pallas_call x1, Pallas kernels, local(): pl.pallas_call(functools.partial(convert_kernel, steps, shifts_from(0, st...  7.05 us
    ppermute x4, waiting for transfers between devices, local(): lax.ppermute(gram, 'dom', [(i, i ^ (1 << stage | 1)) for i in range(count)])  6.59 us
    ppermute x4, starting transfers between devices, local(): lax.ppermute(gram, 'dom', [(i, i ^ (1 << stage | 1)) for i in range(count)])  4.64 us
    pallas_call x1, Pallas kernels, local(): pl.pallas_call(prep_kernel, out_shape=[message, message], in_specs=[HB, H...  1.48 us
    pallas_call x1, Pallas kernels, local(): pl.pallas_call(final_kernel, out_shape=[shape(rhs_count, rows * size)] *...  1.29 us
  transfers between devices with their start and end apart: 14, of which 4 were waited for; matrix products, arithmetic and copies ran while one was open for 0% of the time, Pallas kernels for 40%

profile of v6, /device:TPU:0, one launch (start us, length us, event | category | flops | bytes accessed | tf_op | source)
XLA Modules:
  0.0 53.0 jit_solution(4058479627199268286)
XLA Ops:
  0.6 0.0 copy-start
  0.6 0.0 copy-start.1
  0.7 0.0 copy-start.2
  0.7 1.5 %prepare.1 = (f32[904,128]{1,0:T(8,128)S(1)}, f32[904,128]{1,0:T(8,128)S(1)}) custom-call(f32[20480,128]{1,0:T(8,128)} %bitcast.7, f32[40,128]{1,0:T(8,128)} %bitcast.3, s32[4,40]{1,0:T(4,128)} %bitcast.5), custom_call_target="tpu_custom_call" | custom-call | tf_op jit(solution)/shard_map/prepare/pallas_call | solution.py:509
  2.1 0.5 collective-permute-start.2
  2.7 2.6 %collective-permute-start.3 = (f32[904,128]{1,0:T(8,128)S(1)}, f32[904,128]{1,0:T(8,128)S(1)}, u32[]{:S(2)}, u32[]{:S(2)}) collective-permute-start(f32[904,128]{1,0:T(8,128)S(1)} %get-tuple-element.57), channel_id=1, source_target_pairs={{1,2},{3,4},{5,6},{7,8},{9,10},{11,12},{13,14},{17,18},{19,20},{21... | collective-permute-start | bytes 1388552 | tf_op jit(solution)/shard_map/ppermute | solution.py:532
  5.2 0.0 copy-done
  5.2 0.0 copy-done.1
  5.2 0.0 copy-done.2
  5.2 7.0 %convert.1 = (f32[40,8,128]{2,1,0:T(8,128)S(1)}, f32[40,1,128]{2,1,0:T(1,128)S(1)}, f32[3,40,1,128]{3,2,1,0:T(1,128)S(1)}, bf16[20,512,256]{2,1,0:T(8,128)(2,1)S...) custom-call(f32[20480,128]{1,0:T(8,128)} %bitcast.8, ...), custom_call_target="tpu_custom_call" | custom-call | flops 167772160 | bytes 20971520 | tf_op jit(solution)/shard_map/convert/pallas_call | solution.py:547
  12.3 0.2 collective-permute-start
  12.5 1.5 %collective-permute-start.1 = (f32[6,8,128]{2,1,0:T(8,128)S(1)}, f32[6,8,128]{2,1,0:T(8,128)S(1)}, u32[]{:S(2)}, u32[]{:S(2)}) collective-permute-start(f32[6,8,128]{2,1,0:T(8,128)S(1)} %get-tuple-element.52), channel_id=1, source_target_pairs={{1,2},{3,4},{5,6},{7,8},{9,10},{11,12},{13,14},{17,18},{19,20},{21... | collective-permute-start | bytes 73736 | tf_op jit(solution)/shard_map/ppermute | solution.py:532
  14.0 3.4 %inner.4 = (f32[40,8,128]{2,1,0:T(8,128)S(1)}, f32[40,8,128]{2,1,0:T(8,128)S(1)}, f32[40,8,128]{2,1,0:T(8,128)S(1)}) custom-call(f32[3,40,1,128]{3,2,1,0:T(1,128)S(1)} %get-tuple-element.46.refs_0_, bf16[20,512,256]{2,1,0:T(8,128)(2,1)S(1)} %get-tuple-element.47.refs_1_, bf16[20,512,256]{2,1,0:T(8,128)(2,1)S(1)} %get-tuple-element.48.refs_2_, ...), custom_call_target="tpu_custom_call" | custom-call | flops 201326592 | bytes 25165824 | tf_op jit(solution)/shard_map/inner/pallas_call | solution.py:569
  17.4 0.0 collective-permute-done.refs_5_
  17.4 0.0 collective-permute-done.1.refs_6_
  17.4 0.0 collective-permute-done.2.refs_10_
  17.4 0.0 collective-permute-done.3.refs_11_
  17.4 2.2 %rest.4 = (bf16[2,512,256]{2,1,0:T(8,128)(2,1)S(1)}, bf16[2,512,256]{2,1,0:T(8,128)(2,1)S(1)}, f32[2,2,1,128]{3,2,1,0:T(1,128)S(1)}, f32[40,8,128]{2,1,0:T(8,128...) custom-call(f32[3,40,1,128]{3,2,1,0:T(1,128)S(1)} %get-tuple-element, ...), custom_call_target="tpu_custom_call" | custom-call | flops 33554432 | bytes 4194304 | tf_op jit(solution)/shard_map/rest/pallas_call | solution.py:591
  19.7 0.2 collective-permute-start.4
  19.8 1.5 %collective-permute-start.5 = (f32[6,8,128]{2,1,0:T(8,128)S(1)}, f32[6,8,128]{2,1,0:T(8,128)S(1)}, u32[]{:S(2)}, u32[]{:S(2)}) collective-permute-start(f32[6,8,128]{2,1,0:T(8,128)S(1)} %get-tuple-element.60), channel_id=1, source_target_pairs={{1,2},{3,4},{5,6},{7,8},{9,10},{11,12},{13,14},{17,18},{19,20},{21... | collective-permute-start | bytes 73736 | tf_op jit(solution)/shard_map/ppermute | solution.py:532
  21.3 3.4 %inner.5 = (f32[40,8,128]{2,1,0:T(8,128)S(1)}, f32[40,8,128]{2,1,0:T(8,128)S(1)}, f32[40,8,128]{2,1,0:T(8,128)S(1)}) custom-call(f32[3,40,1,128]{3,2,1,0:T(1,128)S(1)} %get-tuple-element.46.refs_0_, bf16[20,512,256]{2,1,0:T(8,128)(2,1)S(1)} %get-tuple-element.47.refs_1_, bf16[20,512,256]{2,1,0:T(8,128)(2,1)S(1)} %get-tuple-element.48.refs_2_, ...), custom_call_target="tpu_custom_call" | custom-call | flops 201326592 | bytes 25165824 | tf_op jit(solution)/shard_map/inner/pallas_call | solution.py:569
  24.7 0.0 collective-permute-done.4.refs_5_
  24.7 0.0 collective-permute-done.5.refs_6_
  24.7 1.8 %rest.5 = (f32[40,8,128]{2,1,0:T(8,128)S(1)}, f32[40,8,128]{2,1,0:T(8,128)S(1)}, f32[40,8,128]{2,1,0:T(8,128)S(1)}, f32[6,8,128]{2,1,0:T(8,128)S(1)}, f32[6,8,128]{2,1,0:T(8,128)S(1)}) custom-call(f32[3,40,1,128]{3,2,1,0:T(1,128)S(1)} %get-tuple-element.46.refs_0_, bf16[20,512,256]{2,1,0:T(8,128)(2,1)S(1)} %get-tuple-element.47.refs_1_, ...), custom_call_target="tpu_custom_call" | custom-call | flops 33554432 | bytes 4194304 | tf_op jit(solution)/shard_map/rest/pallas_call | solution.py:591
  26.5 0.2 collective-permute-start.6
  26.7 1.5 %collective-permute-start.7 = (f32[6,8,128]{2,1,0:T(8,128)S(1)}, f32[6,8,128]{2,1,0:T(8,128)S(1)}, u32[]{:S(2)}, u32[]{:S(2)}) collective-permute-start(f32[6,8,128]{2,1,0:T(8,128)S(1)} %get-tuple-element.69), channel_id=1, source_target_pairs={{1,2},{3,4},{5,6},{7,8},{9,10},{11,12},{13,14},{17,18},{19,20},{21... | collective-permute-start | bytes 73736 | tf_op jit(solution)/shard_map/ppermute | solution.py:532
  28.2 3.6 %inner.6 = (f32[40,8,128]{2,1,0:T(8,128)S(1)}, f32[40,8,128]{2,1,0:T(8,128)S(1)}, f32[40,8,128]{2,1,0:T(8,128)S(1)}) custom-call(f32[3,40,1,128]{3,2,1,0:T(1,128)S(1)} %get-tuple-element.46.refs_0_, bf16[20,512,256]{2,1,0:T(8,128)(2,1)S(1)} %get-tuple-element.47.refs_1_, bf16[20,512,256]{2,1,0:T(8,128)(2,1)S(1)} %get-tuple-element.48.refs_2_, ...), custom_call_target="tpu_custom_call" | custom-call | flops 201326592 | bytes 25165824 | tf_op jit(solution)/shard_map/inner/pallas_call | solution.py:569
  31.8 0.0 collective-permute-done.6.refs_5_
  31.8 0.0 collective-permute-done.7.refs_6_
  31.8 1.8 %rest.6 = (f32[40,8,128]{2,1,0:T(8,128)S(1)}, f32[40,8,128]{2,1,0:T(8,128)S(1)}, f32[40,8,128]{2,1,0:T(8,128)S(1)}, f32[6,8,128]{2,1,0:T(8,128)S(1)}, f32[6,8,128]{2,1,0:T(8,128)S(1)}) custom-call(f32[3,40,1,128]{3,2,1,0:T(1,128)S(1)} %get-tuple-element.46.refs_0_, bf16[20,512,256]{2,1,0:T(8,128)(2,1)S(1)} %get-tuple-element.47.refs_1_, ...), custom_call_target="tpu_custom_call" | custom-call | flops 33554432 | bytes 4194304 | tf_op jit(solution)/shard_map/rest/pallas_call | solution.py:591
  33.6 0.2 collective-permute-start.8
  33.8 1.5 %collective-permute-start.9 = (f32[6,8,128]{2,1,0:T(8,128)S(1)}, f32[6,8,128]{2,1,0:T(8,128)S(1)}, u32[]{:S(2)}, u32[]{:S(2)}) collective-permute-start(f32[6,8,128]{2,1,0:T(8,128)S(1)} %get-tuple-element.75), channel_id=1, source_target_pairs={{1,2},{3,4},{5,6},{7,8},{9,10},{11,12},{13,14},{17,18},{19,20},{21... | collective-permute-start | bytes 73736 | tf_op jit(solution)/shard_map/ppermute | solution.py:532
  35.3 3.7 %inner.7 = (f32[40,8,128]{2,1,0:T(8,128)S(1)}, f32[40,8,128]{2,1,0:T(8,128)S(1)}, f32[40,8,128]{2,1,0:T(8,128)S(1)}, f32[8,128]{1,0:T(8,128)S(1)}) custom-call(f32[3,40,1,128]{3,2,1,0:T(1,128)S(1)} %get-tuple-element.46.refs_0_, bf16[20,512,256]{2,1,0:T(8,128)(2,1)S(1)} %get-tuple-element.47.refs_1_, bf16[20,512,256]{2,1,0:T(8,128)(2,1)S(1)} %get-tuple-element.48.refs_2_, ...), custom_call_target="tpu_custom_call" | custom-call | flops 201326592 | bytes 25165824 | tf_op jit(solution)/shard_map/inner/pallas_call | solution.py:569
  38.9 0.0 collective-permute-done.8.refs_5_
  38.9 0.0 collective-permute-done.9.refs_6_
  38.9 1.5 %rest.7 = (f32[40,8,128]{2,1,0:T(8,128)S(1)}, f32[40,8,128]{2,1,0:T(8,128)S(1)}, f32[40,8,128]{2,1,0:T(8,128)S(1)}, f32[8,128]{1,0:T(8,128)S(1)}) custom-call(f32[3,40,1,128]{3,2,1,0:T(1,128)S(1)} %get-tuple-element.46.refs_0_, bf16[20,512,256]{2,1,0:T(8,128)(2,1)S(1)} %get-tuple-element.47.refs_1_, bf16[20,512,256]{2,1,0:T(8,128)(2,1)S(1)} %get-tuple-element.48.refs_2_, ...), custom_call_target="tpu_custom_call" | custom-call | flops 33554432 | bytes 4194304 | tf_op jit(solution)/shard_map/rest/pallas_call | solution.py:591
  40.5 0.2 collective-permute-start.10
  40.6 1.1 %collective-permute-done.10 = f32[8,128]{1,0:T(8,128)S(1)} collective-permute-done((f32[8,128]{1,0:T(8,128)S(1)}, f32[8,128]{1,0:T(8,128)S(1)}, u32[]{:S(2)}, u32[]{:S(2)}) %collective-permute-start.10) | collective-permute-done | bytes 4128 | tf_op jit(solution)/shard_map/ppermute | solution.py:625
  41.7 1.3 %collective-permute-start.11 = (f32[8,128]{1,0:T(8,128)S(1)}, f32[8,128]{1,0:T(8,128)S(1)}, u32[]{:S(2)}, u32[]{:S(2)}) collective-permute-start(f32[8,128]{1,0:T(8,128)S(1)} %add.12), channel_id=1, source_target_pairs={{0,3},{1,2},{2,1},{3,0},{4,7},{5,6},{6,5},{7,4},{8,11},{9,10},{10,... | collective-permute-start | bytes 12296 | tf_op jit(solution)/shard_map/ppermute | solution.py:625
  43.0 1.8 %collective-permute-done.11 = f32[8,128]{1,0:T(8,128)S(1)} collective-permute-done((f32[8,128]{1,0:T(8,128)S(1)}, f32[8,128]{1,0:T(8,128)S(1)}, u32[]{:S(2)}, u32[]{:S(2)}) %collective-permute-start.11) | collective-permute-done | bytes 4128 | tf_op jit(solution)/shard_map/ppermute | solution.py:625
  44.7 1.3 %collective-permute-start.12 = (f32[8,128]{1,0:T(8,128)S(1)}, f32[8,128]{1,0:T(8,128)S(1)}, u32[]{:S(2)}, u32[]{:S(2)}) collective-permute-start(f32[8,128]{1,0:T(8,128)S(1)} %add.13), channel_id=1, source_target_pairs={{0,5},{1,4},{2,7},{3,6},{4,1},{5,0},{6,3},{7,2},{8,13},{9,12},{10,... | collective-permute-start | bytes 12296 | tf_op jit(solution)/shard_map/ppermute | solution.py:625
  46.0 1.7 %collective-permute-done.12 = f32[8,128]{1,0:T(8,128)S(1)} collective-permute-done((f32[8,128]{1,0:T(8,128)S(1)}, f32[8,128]{1,0:T(8,128)S(1)}, u32[]{:S(2)}, u32[]{:S(2)}) %collective-permute-start.12) | collective-permute-done | bytes 4128 | tf_op jit(solution)/shard_map/ppermute | solution.py:625
  47.8 1.9 %collective-permute-start.13 = (f32[8,128]{1,0:T(8,128)S(1)}, f32[8,128]{1,0:T(8,128)S(1)}, u32[]{:S(2)}, u32[]{:S(2)}) collective-permute-start(f32[8,128]{1,0:T(8,128)S(1)} %add.14), channel_id=1, source_target_pairs={{0,9},{1,8},{2,11},{3,10},{4,13},{5,12},{6,15},{7,14},{8,1},{9,0},... | collective-permute-start | bytes 12296 | tf_op jit(solution)/shard_map/ppermute | solution.py:625
  49.7 2.0 %collective-permute-done.13 = f32[8,128]{1,0:T(8,128)S(1)} collective-permute-done((f32[8,128]{1,0:T(8,128)S(1)}, f32[8,128]{1,0:T(8,128)S(1)}, u32[]{:S(2)}, u32[]{:S(2)}) %collective-permute-start.13) | collective-permute-done | bytes 4128 | tf_op jit(solution)/shard_map/ppermute | solution.py:625
  51.7 1.3 %finish.1 = (f32[4,5120]{1,0:T(4,128)}, f32[4,5120]{1,0:T(4,128)}) custom-call(f32[8,128]{1,0:T(8,128)S(1)} %add.15.total_gram, f32[40,8,128]{2,1,0:T(8,128)S(1)} %get-tuple-element.50.refs_4_.refs_5_.refs_11_.refs_0_, f32[40,8,128]{2,1,0:T(8,128)S(1)} %get-tuple-element.76.refs_6_.refs_12_.refs_1_, ...), custom_call_target="tpu_custom_call" | custom-call | tf_op jit(solution)/shard_map/finish/pallas_call | solution.py:627
  (4 shorter events, 0.0 us)
Async XLA Ops:
  0.6 4.6 %copy-start = (f32[4,5120]{1,0:T(4,128)S(1)}, f32[4,5120]{1,0:T(4,128)}, u32[]{:S(2)}) copy-start(f32[4,5120]{1,0:T(4,128)} %refs_1_.1) | copy-start | bytes 245764
  0.6 4.6 %copy-start.1 = (f32[5120]{0:T(1024)S(1)}, f32[5120]{0:T(1024)}, u32[]{:S(2)}) copy-start(f32[5120]{0:T(1024)} %param.6) | copy-start | bytes 61444
  0.7 4.6 %copy-start.2 = (s32[40,4]{0,1:T(4,128)S(1)}, s32[40,4]{0,1:T(4,128)}, u32[]{:S(2)}) copy-start(s32[40,4]{0,1:T(4,128)} %param.5) | copy-start | bytes 1924
  2.1 15.3 %collective-permute-start.2 = (f32[904,128]{1,0:T(8,128)S(1)}, f32[904,128]{1,0:T(8,128)S(1)}, u32[]{:S(2)}, u32[]{:S(2)}) collective-permute-start(f32[904,128]{1,0:T(8,128)S(1)} %get-tuple-element.56), channel_id=1, source_target_pairs={{0,1},{1,0},{2,3},{3,2},{4,5},{5,4},{6,7},{7,6},{8,9},{9,8},{10,11... | collective-permute-start | bytes 1388552 | tf_op jit(solution)/shard_map/ppermute | solution.py:533
  2.7 14.8 %collective-permute-start.3 = (f32[904,128]{1,0:T(8,128)S(1)}, f32[904,128]{1,0:T(8,128)S(1)}, u32[]{:S(2)}, u32[]{:S(2)}) collective-permute-start(f32[904,128]{1,0:T(8,128)S(1)} %get-tuple-element.57), channel_id=1, source_target_pairs={{1,2},{3,4},{5,6},{7,8},{9,10},{11,12},{13,14},{17,18},{19,20},{21... | collective-permute-start | bytes 1388552 | tf_op jit(solution)/shard_map/ppermute | solution.py:532
  12.3 5.1 %collective-permute-start = (f32[6,8,128]{2,1,0:T(8,128)S(1)}, f32[6,8,128]{2,1,0:T(8,128)S(1)}, u32[]{:S(2)}, u32[]{:S(2)}) collective-permute-start(f32[6,8,128]{2,1,0:T(8,128)S(1)} %get-tuple-element.51), channel_id=1, source_target_pairs={{0,1},{1,0},{2,3},{3,2},{4,5},{5,4},{6,7},{7,6},{8,9},{9,8},{10,11... | collective-permute-start | bytes 73736 | tf_op jit(solution)/shard_map/ppermute | solution.py:533
  12.5 4.9 %collective-permute-start.1 = (f32[6,8,128]{2,1,0:T(8,128)S(1)}, f32[6,8,128]{2,1,0:T(8,128)S(1)}, u32[]{:S(2)}, u32[]{:S(2)}) collective-permute-start(f32[6,8,128]{2,1,0:T(8,128)S(1)} %get-tuple-element.52), channel_id=1, source_target_pairs={{1,2},{3,4},{5,6},{7,8},{9,10},{11,12},{13,14},{17,18},{19,20},{21... | collective-permute-start | bytes 73736 | tf_op jit(solution)/shard_map/ppermute | solution.py:532
  19.7 5.1 %collective-permute-start.4 = (f32[6,8,128]{2,1,0:T(8,128)S(1)}, f32[6,8,128]{2,1,0:T(8,128)S(1)}, u32[]{:S(2)}, u32[]{:S(2)}) collective-permute-start(f32[6,8,128]{2,1,0:T(8,128)S(1)} %get-tuple-element.59), channel_id=1, source_target_pairs={{0,1},{1,0},{2,3},{3,2},{4,5},{5,4},{6,7},{7,6},{8,9},{9,8},{10,11... | collective-permute-start | bytes 73736 | tf_op jit(solution)/shard_map/ppermute | solution.py:533
  19.8 4.9 %collective-permute-start.5 = (f32[6,8,128]{2,1,0:T(8,128)S(1)}, f32[6,8,128]{2,1,0:T(8,128)S(1)}, u32[]{:S(2)}, u32[]{:S(2)}) collective-permute-start(f32[6,8,128]{2,1,0:T(8,128)S(1)} %get-tuple-element.60), channel_id=1, source_target_pairs={{1,2},{3,4},{5,6},{7,8},{9,10},{11,12},{13,14},{17,18},{19,20},{21... | collective-permute-start | bytes 73736 | tf_op jit(solution)/shard_map/ppermute | solution.py:532
  26.5 5.2 %collective-permute-start.6 = (f32[6,8,128]{2,1,0:T(8,128)S(1)}, f32[6,8,128]{2,1,0:T(8,128)S(1)}, u32[]{:S(2)}, u32[]{:S(2)}) collective-permute-start(f32[6,8,128]{2,1,0:T(8,128)S(1)} %get-tuple-element.68), channel_id=1, source_target_pairs={{0,1},{1,0},{2,3},{3,2},{4,5},{5,4},{6,7},{7,6},{8,9},{9,8},{10,11... | collective-permute-start | bytes 73736 | tf_op jit(solution)/shard_map/ppermute | solution.py:533
  26.7 5.1 %collective-permute-start.7 = (f32[6,8,128]{2,1,0:T(8,128)S(1)}, f32[6,8,128]{2,1,0:T(8,128)S(1)}, u32[]{:S(2)}, u32[]{:S(2)}) collective-permute-start(f32[6,8,128]{2,1,0:T(8,128)S(1)} %get-tuple-element.69), channel_id=1, source_target_pairs={{1,2},{3,4},{5,6},{7,8},{9,10},{11,12},{13,14},{17,18},{19,20},{21... | collective-permute-start | bytes 73736 | tf_op jit(solution)/shard_map/ppermute | solution.py:532
  33.6 5.3 %collective-permute-start.8 = (f32[6,8,128]{2,1,0:T(8,128)S(1)}, f32[6,8,128]{2,1,0:T(8,128)S(1)}, u32[]{:S(2)}, u32[]{:S(2)}) collective-permute-start(f32[6,8,128]{2,1,0:T(8,128)S(1)} %get-tuple-element.74), channel_id=1, source_target_pairs={{0,1},{1,0},{2,3},{3,2},{4,5},{5,4},{6,7},{7,6},{8,9},{9,8},{10,11... | collective-permute-start | bytes 73736 | tf_op jit(solution)/shard_map/ppermute | solution.py:533
  33.8 5.1 %collective-permute-start.9 = (f32[6,8,128]{2,1,0:T(8,128)S(1)}, f32[6,8,128]{2,1,0:T(8,128)S(1)}, u32[]{:S(2)}, u32[]{:S(2)}) collective-permute-start(f32[6,8,128]{2,1,0:T(8,128)S(1)} %get-tuple-element.75), channel_id=1, source_target_pairs={{1,2},{3,4},{5,6},{7,8},{9,10},{11,12},{13,14},{17,18},{19,20},{21... | collective-permute-start | bytes 73736 | tf_op jit(solution)/shard_map/ppermute | solution.py:532
  40.5 1.2 %collective-permute-start.10 = (f32[8,128]{1,0:T(8,128)S(1)}, f32[8,128]{1,0:T(8,128)S(1)}, u32[]{:S(2)}, u32[]{:S(2)}) collective-permute-start(f32[8,128]{1,0:T(8,128)S(1)} %get-tuple-element.86), channel_id=1, source_target_pairs={{0,1},{1,0},{2,3},{3,2},{4,5},{5,4},{6,7},{7,6},{8,9},{9,8},{10,11... | collective-permute-start | bytes 12296 | tf_op jit(solution)/shard_map/ppermute | solution.py:625
  41.7 3.0 %collective-permute-start.11 = (f32[8,128]{1,0:T(8,128)S(1)}, f32[8,128]{1,0:T(8,128)S(1)}, u32[]{:S(2)}, u32[]{:S(2)}) collective-permute-start(f32[8,128]{1,0:T(8,128)S(1)} %add.12), channel_id=1, source_target_pairs={{0,3},{1,2},{2,1},{3,0},{4,7},{5,6},{6,5},{7,4},{8,11},{9,10},{10,... | collective-permute-start | bytes 12296 | tf_op jit(solution)/shard_map/ppermute | solution.py:625
  44.7 3.0 %collective-permute-start.12 = (f32[8,128]{1,0:T(8,128)S(1)}, f32[8,128]{1,0:T(8,128)S(1)}, u32[]{:S(2)}, u32[]{:S(2)}) collective-permute-start(f32[8,128]{1,0:T(8,128)S(1)} %add.13), channel_id=1, source_target_pairs={{0,5},{1,4},{2,7},{3,6},{4,1},{5,0},{6,3},{7,2},{8,13},{9,12},{10,... | collective-permute-start | bytes 12296 | tf_op jit(solution)/shard_map/ppermute | solution.py:625
  47.8 3.9 %collective-permute-start.13 = (f32[8,128]{1,0:T(8,128)S(1)}, f32[8,128]{1,0:T(8,128)S(1)}, u32[]{:S(2)}, u32[]{:S(2)}) collective-permute-start(f32[8,128]{1,0:T(8,128)S(1)} %add.14), channel_id=1, source_target_pairs={{0,9},{1,8},{2,11},{3,10},{4,13},{5,12},{6,15},{7,14},{8,1},{9,0},... | collective-permute-start | bytes 12296 | tf_op jit(solution)/shard_map/ppermute | solution.py:625

commit v7 on v6

--- a/solution.py
+++ b/solution.py
@@ -14,6 +14,8 @@
 CYCLES = 2
 CHAIN = S * CYCLES
 GROUPS = (3, 3, 3, 3)
+AHEAD = (3, 1, 0, 0)
+PORTIONS = (3, 7, 11, 15, 18, 20)
 SCALE = 0.125
 GROW = 1.0 / SCALE
 SHIFTS = [
@@ -206,9 +208,10 @@
 
 def convert_kernel(steps, shifts, *refs):
     blocks, rhs, diag, offs, start, scaled, places, high, low, to_even, to_odd = refs[:11]
-    sources = refs[11 : 10 + steps]
-    buf, sems = refs[10 + steps :]
+    outs, sources = refs[11 : 11 + steps], refs[11 + steps : 11 + 2 * steps]
+    buf, sems = refs[11 + 2 * steps :]
     rows = buf.shape[0]
+    count = rows // 2
 
     def fetch(i):
         first = pl.multiple_of(i * 512, 512)
@@ -216,36 +219,70 @@
 
     for i in range(rows):
         fetch(i).start()
+    mask = halves()
+    zero = jnp.zeros((8, 128), F32)
+    for source in sources:
+        for row in (0, 1, rows + W, rows + W + 1):
+            source[row] = zero
     for i in range(rows):
         part = rhs[:, i * 128 : (i + 1) * 128]
-        start[i] = jnp.concatenate([part, part], 0)
+        tile = jnp.concatenate([part, part], 0)
+        start[i] = tile
+        sources[0][i + W] = split(tile, mask)
         scaled[i] = diag[i : i + 1, :] * SCALE
     turned = jnp.concatenate([offs[...].astype(F32), jnp.zeros((4, 128 - rows), F32)], 1)
     turned = jnp.concatenate([turned, jnp.zeros((4, 128), F32)], 0).T
     for k in range(1, 4):
         places[k - 1] = jnp.broadcast_to(turned[:rows, k : k + 1], (rows, 128)).reshape(rows, 1, 128)
-
-    def body(p, carry):
-        for half in range(2):
-            i = 2 * p + half
-            fetch(i).wait()
-            for k in range(4):
-                store_pair(buf[i, k * 128 : (k + 1) * 128, :], high, low, p, half, k)
-        return carry
-
-    lax.fori_loop(0, rows // 2, body, 0)
     chain = Chain(rows, shifts, places, high, low, scaled)
-    send_edges(chain, steps, start, to_even, to_odd, sources)
-
-
-def inner_kernel(steps, shifts, earlier, *refs):
+    values = [start] + list(outs)
+
+    def take(step, pairs):
+        def emit(row, tile):
+            outs[step][row] = tile
+            if step < steps - 1:
+                sources[step + 1][row + W] = split(tile, mask)
+
+        chain.advance(step, [2 * q for q in pairs], sources[step], lambda row: values[step][row], emit)
+
+    portions = [count * part // PORTIONS[-1] for part in PORTIONS]
+    taken = [0] * steps
+    before = 0
+    for until in portions + [count]:
+        for p in range(before, until):
+            for half in range(2):
+                fetch(2 * p + half).wait()
+        ready = before
+        for step in range(steps):
+            if step:
+                ready = count if taken[step - 1] == count else max(taken[step - 1] - 1, 0)
+            if step == steps - 1:
+                ready = min(ready, count - steps)
+            take(step, range(taken[step], max(ready, taken[step])))
+            taken[step] = max(ready, taken[step])
+        for p in range(before, until):
+            for half in range(2):
+                for k in range(4):
+                    store_pair(buf[2 * p + half, k * 128 : (k + 1) * 128, :], high, low, p, half, k)
+        before = until
+    parity = lax.axis_index("dom") % 2
+    for step in range(steps):
+        for h in range(2):
+            low_edge, top_edge = values[step][h], values[step][rows - 2 + h]
+            to_even[2 * step + h] = jnp.where(parity == 0, top_edge, low_edge)
+            to_odd[2 * step + h] = jnp.where(parity == 0, low_edge, top_edge)
+
+
+def inner_kernel(steps, shifts, base, done, earlier, *refs):
     places, high, low, scaled, own = refs[:5]
     refs = list(refs[5:])
+    begun = refs[: len(done)]
+    del refs[: len(done)]
     before = refs[:earlier]
     del refs[:earlier]
     outs = refs[:steps]
     del refs[:steps]
-    rows = own.shape[0]
+    rows = scaled.shape[0]
     if earlier:
         products = refs.pop(0)
         vectors = before + [own]
@@ -253,20 +290,25 @@
         products[...] = add_products(tile, vectors, pair_blocks((earlier + 1) // 2, earlier + 1))
     sources = refs
     chain = Chain(rows, shifts, places, high, low, scaled)
-    chain.fill(sources[0], range(rows), lambda row: own[row])
+    done = list(done) + [[]] * (steps - len(done))
+    for step, old in enumerate(begun):
+        for row in done[step]:
+            outs[step][row] = old[row]
     for step in range(steps):
-        before = own if step == 0 else outs[step - 1]
+        ref = own if step == 0 else outs[step - 1]
+        pairs = [row for row in range(base + W * (step + 1), rows - base - W * (step + 1)) if row not in done[step]][::2]
+        there = set(range(rows)) if step == 0 else set(done[step - 1])
+        chain.fill(sources[step], [row for row in around(pairs, rows) if row in there], lambda row, ref=ref: ref[row])
 
         def emit(row, tile, step=step):
             outs[step][row] = tile
             if step < steps - 1:
                 sources[step + 1][row + W] = split(tile, chain.mask)
 
-        pairs = inner_rows(rows, step + 1)[::2]
-        chain.advance(step, pairs, sources[step], lambda row, ref=before: ref[row], emit)
-
-
-def rest_kernel(first, steps, shifts, next_steps, next_shifts, earlier, *refs):
+        chain.advance(step, pairs, sources[step], lambda row, ref=ref: ref[row], emit)
+
+
+def rest_kernel(first, steps, shifts, next_steps, next_shifts, earlier, unused, *refs):
     refs = list(refs)
     places, high, low, scaled, own, from_even, from_odd = refs[:7]
     del refs[:7]
@@ -278,8 +320,12 @@
     if earlier:
         products, before = refs[0], refs[1 : 1 + earlier]
         del refs[: 1 + earlier]
+    if first:
+        del refs[:unused]
     side_high, side_low, side_scaled = refs[:3]
     del refs[:3]
+    if not first:
+        del refs[:unused]
     outs = refs[:steps]
     del refs[:steps]
     if earlier:
@@ -318,11 +364,11 @@
         if step < steps - 1:
             for side in range(2):
                 near = [source[W + side * (rows - 2) + h] for h in range(2)]
+                far = [] if added is None else [split(tile, mask) for tile in added[side]]
+                tiles = near + far if side else far + near
+                columns = slice(None)
                 if added is None:
-                    far = [jnp.zeros((8, 128), F32)] * 2
-                else:
-                    far = [split(tile, mask) for tile in added[side]]
-                tiles = near + far if side else far + near
+                    columns = slice(0, 256) if side else slice(256, 512)
                 left = jnp.concatenate([jnp.concatenate([t, t], 0).astype(BF16) for t in tiles], 1)
 
                 def use(total, side=side, added=added, after=after, step=step):
@@ -332,7 +378,7 @@
                             tile = tile + (side_scaled[side, h] - SCALE * shifts[step]) * added[side][h]
                         after[side][h] = tile
 
-                extra.append((left, side_high[side], side_low[side], use))
+                extra.append((left, side_high[side, columns], side_low[side, columns], use))
 
         def emit(row, tile, step=step):
             outs[step][row] = tile
@@ -544,39 +590,52 @@
 
     steps = GROUPS[0]
     edge = shape(2 * steps, 8, size)
-    start, scaled, places, high, low, even, odd = pl.pallas_call(
+    start, scaled, places, high, low, even, odd, *begun = pl.pallas_call(
         functools.partial(convert_kernel, steps, shifts_from(0, steps)),
         out_shape=[vector, shape(rows, 1, size), shape(per_row - 1, rows, 1, size)]
         + [pair_shape] * 2
-        + [edge] * 2,
+        + [edge] * 2
+        + [vector] * steps,
         in_specs=[HB, VM, VM, VM],
-        out_specs=[VM] * 7,
-        scratch_shapes=[source] * (steps - 1)
+        out_specs=[VM] * (7 + steps),
+        scratch_shapes=[source] * steps
         + [pltpu.VMEM((rows, per_row * size, size), F32), pltpu.SemaphoreType.DMA((rows,))],
         compiler_params=params(24),
         cost_estimate=cost(2 * rows),
         name="convert",
     )(flat, right_side, diag, offs)
 
+    def inner(steps, shifts, base, done, earlier, own, *more):
+        last = bool(earlier)
+        return pl.pallas_call(
+            functools.partial(inner_kernel, steps, shifts, base, done, earlier),
+            out_shape=[vector] * steps + [shape(8, size)] * last,
+            in_specs=[VM] * (5 + len(more)),
+            out_specs=[VM] * (steps + last),
+            scratch_shapes=[source] * steps,
+            compiler_params=params(16),
+            cost_estimate=cost(2 * rows),
+            name="inner",
+        )(places, high, low, scaled, own, *more)
+
     vectors = [start]
     sides = None
     at = 0
+    done, ahead = [], []
     for number, steps in enumerate(GROUPS):
         even, odd = exchange(even, odd)
         shifts = shifts_from(at, steps)
         first, last = number == 0, number + 1 == len(GROUPS)
         before = vectors[:-1] if last else []
-        begun = pl.pallas_call(
-            functools.partial(inner_kernel, steps, shifts, len(before)),
-            out_shape=[vector] * steps + [shape(8, size)] * last,
-            in_specs=[VM] * (5 + len(before)),
-            out_specs=[VM] * (steps + last),
-            scratch_shapes=[source] * steps,
-            compiler_params=params(16),
-            cost_estimate=cost(sum(len(inner_rows(rows, j + 1)) for j in range(steps))),
-            name="inner",
-        )(places, high, low, scaled, vectors[-1], *before)
-        begun, products = begun[:steps], begun[steps:]
+        products = []
+        if not first:
+            begun = inner(steps, shifts, 0, done, len(before), vectors[-1], *ahead, *before)
+            begun, products = begun[:steps], begun[steps:]
+        base, some = W * steps, AHEAD[number]
+        ahead = []
+        if some:
+            ahead = list(inner(some, shifts_from(at + steps, some), base, [], 0, begun[-1]))
+        done = [list(range(base + W * (j + 1), rows - base - W * (j + 1))) for j in range(some)]
         next_steps = 0 if last else GROUPS[number + 1]
         edge = shape(2 * next_steps, 8, size)
         outs = [vector] * steps + [shape(8, size)] * last + [edge] * (0 if last else 2)
@@ -588,6 +647,7 @@
             inputs += [*products, *before]
         if not first:
             inputs += sides
+        inputs += ahead[:1]
         results = pl.pallas_call(
             functools.partial(
                 rest_kernel,
@@ -597,6 +657,7 @@
                 next_steps,
                 shifts_from(at + steps, next_steps),
                 len(before),
+                len(ahead[:1]),
             ),
             out_shape=outs,
             in_specs=[VM] * len(inputs),

time: 53.2 us -> 51 us (0.959)
  Pallas kernels: 31.2 us -> 28.4 us
  starting transfers between devices: 14.4 us -> 16.1 us
  waiting for transfers between devices: 6.62 us -> 5.57 us
    pallas_call x4 -> x5, Pallas kernels: 14 us -> 10.7 us  [inner(): pl.pallas_call(functools.partial(inner_kernel, steps, shifts, base, done,...]
    ppermute x4, starting transfers between devices: 4.64 us -> 5.92 us  [local(): lax.ppermute(gram, 'dom', [(i, i ^ (1 << stage | 1)) for i in range(count)])]
    ppermute x4, waiting for transfers between devices: 6.59 us -> 5.32 us  [local(): lax.ppermute(gram, 'dom', [(i, i ^ (1 << stage | 1)) for i in range(count)])]
    pallas_call x1, Pallas kernels: 7.05 us -> 7.7 us  [local(): pl.pallas_call(functools.partial(convert_kernel, steps, shifts_from(0, st...]
  transfers between devices with their start and end apart: 14 -> 14, of which waited for: 4 -> 6; matrix products, arithmetic and copies ran while one was open for 0% -> 0% of each run, Pallas kernels for 40% -> 36%
where the time goes in v7:
time: 51 us; the launch traced here: 50.8 us
  Pallas kernels  28.4 us (56%)
  starting transfers between devices  16.1 us (32%)
  waiting for transfers between devices  5.57 us (11%)
  between operations  0.71 us (1%)
    pallas_call x5, Pallas kernels, inner(): pl.pallas_call(functools.partial(inner_kernel, steps, shifts, base, done,...  10.7 us
    ppermute x5, starting transfers between devices, exchange(): odd = lax.ppermute(odd, ('groups', 'dom'), swap_odd)  8.51 us
    pallas_call x1, Pallas kernels, local(): pl.pallas_call(functools.partial(convert_kernel, steps, shifts_from(0, st...  7.7 us
    pallas_call x4, Pallas kernels, local(): pl.pallas_call(functools.partial(rest_kernel, first, steps, shifts, next_...  7.25 us
    ppermute x4, starting transfers between devices, local(): lax.ppermute(gram, 'dom', [(i, i ^ (1 << stage | 1)) for i in range(count)])  5.92 us
    ppermute x4, waiting for transfers between devices, local(): lax.ppermute(gram, 'dom', [(i, i ^ (1 << stage | 1)) for i in range(count)])  5.32 us
    ppermute x5, starting transfers between devices, exchange(): return (lax.ppermute(even, 'dom', swap_even), odd)  1.69 us
    pallas_call x1, Pallas kernels, local(): pl.pallas_call(prep_kernel, out_shape=[message, message], in_specs=[HB, H...  1.48 us
  transfers between devices with their start and end apart: 14, of which 6 were waited for; matrix products, arithmetic and copies ran while one was open for 0% of the time, Pallas kernels for 36%

profile of v7, /device:TPU:0, one launch (start us, length us, event | category | flops | bytes accessed | tf_op | source)
XLA Modules:
  0.0 50.8 jit_solution(17278872274470789319)
XLA Ops:
  0.6 0.0 copy-start
  0.6 0.0 copy-start.1
  0.7 0.0 copy-start.2
  0.7 1.5 %prepare.1 = (f32[904,128]{1,0:T(8,128)S(1)}, f32[904,128]{1,0:T(8,128)S(1)}) custom-call(f32[20480,128]{1,0:T(8,128)} %bitcast.7, f32[40,128]{1,0:T(8,128)} %bitcast.3, s32[4,40]{1,0:T(4,128)} %bitcast.5), custom_call_target="tpu_custom_call" | custom-call | tf_op jit(solution)/shard_map/prepare/pallas_call | solution.py:555
  2.1 0.5 %collective-permute-start.2 = (f32[904,128]{1,0:T(8,128)S(1)}, f32[904,128]{1,0:T(8,128)S(1)}, u32[]{:S(2)}, u32[]{:S(2)}) collective-permute-start(f32[904,128]{1,0:T(8,128)S(1)} %get-tuple-element.59), channel_id=1, source_target_pairs={{0,1},{1,0},{2,3},{3,2},{4,5},{5,4},{6,7},{7,6},{8,9},{9,8},{10,11... | collective-permute-start | bytes 1388552 | tf_op jit(solution)/shard_map/ppermute | solution.py:579
  2.7 2.6 %collective-permute-start.3 = (f32[904,128]{1,0:T(8,128)S(1)}, f32[904,128]{1,0:T(8,128)S(1)}, u32[]{:S(2)}, u32[]{:S(2)}) collective-permute-start(f32[904,128]{1,0:T(8,128)S(1)} %get-tuple-element.60), channel_id=1, source_target_pairs={{1,2},{3,4},{5,6},{7,8},{9,10},{11,12},{13,14},{17,18},{19,20},{21... | collective-permute-start | bytes 1388552 | tf_op jit(solution)/shard_map/ppermute | solution.py:578
  5.2 0.0 copy-done
  5.2 0.0 copy-done.1
  5.2 0.0 copy-done.2
  5.2 7.7 %convert.1 = (f32[40,8,128]{2,1,0:T(8,128)S(1)}, f32[40,1,128]{2,1,0:T(1,128)S(1)}, f32[3,40,1,128]{3,2,1,0:T(1,128)S(1)}, bf16[20,512,256]{2,1,0:T(8,128)(2,1)S...) custom-call(f32[20480,128]{1,0:T(8,128)} %bitcast.8, ...), custom_call_target="tpu_custom_call" | custom-call | flops 167772160 | bytes 20971520 | tf_op jit(solution)/shard_map/convert/pallas_call | solution.py:593
  12.9 0.2 collective-permute-start
  13.2 1.5 %collective-permute-start.1 = (f32[6,8,128]{2,1,0:T(8,128)S(1)}, f32[6,8,128]{2,1,0:T(8,128)S(1)}, u32[]{:S(2)}, u32[]{:S(2)}) collective-permute-start(f32[6,8,128]{2,1,0:T(8,128)S(1)} %get-tuple-element.55), channel_id=1, source_target_pairs={{1,2},{3,4},{5,6},{7,8},{9,10},{11,12},{13,14},{17,18},{19,20},{21... | collective-permute-start | bytes 73736 | tf_op jit(solution)/shard_map/ppermute | solution.py:578
  14.6 2.2 %inner.5 = (f32[40,8,128]{2,1,0:T(8,128)S(1)}, f32[40,8,128]{2,1,0:T(8,128)S(1)}, f32[40,8,128]{2,1,0:T(8,128)S(1)}) custom-call(f32[3,40,1,128]{3,2,1,0:T(1,128)S(1)} %get-tuple-element.49.refs_0_, bf16[20,512,256]{2,1,0:T(8,128)(2,1)S(1)} %get-tuple-element.50.refs_1_, bf16[20,512,256]{2,1,0:T(8,128)(2,1)S(1)} %get-tuple-element.51.refs_2_, ...), custom_call_target="tpu_custom_call" | custom-call | flops 167772160 | bytes 20971520 | tf_op jit(solution)/shard_map/inner/pallas_call | solution.py:610
  16.8 0.0 collective-permute-done.refs_5_
  16.8 0.2 collective-permute-done.1.refs_6_
  17.0 0.0 collective-permute-done.2.refs_10_
  17.0 0.0 collective-permute-done.3.refs_11_
  17.0 2.2 %rest.4 = (bf16[2,512,256]{2,1,0:T(8,128)(2,1)S(1)}, bf16[2,512,256]{2,1,0:T(8,128)(2,1)S(1)}, f32[2,2,1,128]{3,2,1,0:T(1,128)S(1)}, f32[40,8,128]{2,1,0:T(8,128...) custom-call(f32[3,40,1,128]{3,2,1,0:T(1,128)S(1)} %get-tuple-element, ...), custom_call_target="tpu_custom_call" | custom-call | flops 33554432 | bytes 4194304 | tf_op jit(solution)/shard_map/rest/pallas_call | solution.py:651
  19.2 0.1 collective-permute-start.4
  19.3 1.5 %collective-permute-start.5 = (f32[6,8,128]{2,1,0:T(8,128)S(1)}, f32[6,8,128]{2,1,0:T(8,128)S(1)}, u32[]{:S(2)}, u32[]{:S(2)}) collective-permute-start(f32[6,8,128]{2,1,0:T(8,128)S(1)} %get-tuple-element.64), channel_id=1, source_target_pairs={{1,2},{3,4},{5,6},{7,8},{9,10},{11,12},{13,14},{17,18},{19,20},{21... | collective-permute-start | bytes 73736 | tf_op jit(solution)/shard_map/ppermute | solution.py:578
  20.7 1.3 %inner.6 = (f32[40,8,128]{2,1,0:T(8,128)S(1)}, f32[40,8,128]{2,1,0:T(8,128)S(1)}, f32[40,8,128]{2,1,0:T(8,128)S(1)}) custom-call(f32[3,40,1,128]{3,2,1,0:T(1,128)S(1)} %get-tuple-element.49.refs_0_, bf16[20,512,256]{2,1,0:T(8,128)(2,1)S(1)} %get-tuple-element.50.refs_1_, bf16[20,512,256]{2,1,0:T(8,128)(2,1)S(1)} %get-tuple-element.51.refs_2_, ...), custom_call_target="tpu_custom_call" | custom-call | flops 167772160 | bytes 20971520 | tf_op jit(solution)/shard_map/inner/pallas_call | solution.py:610
  22.1 0.9 %inner.7.refs_13_.refs_5_ = f32[40,8,128]{2,1,0:T(8,128)S(1)} custom-call(f32[3,40,1,128]{3,2,1,0:T(1,128)S(1)} %get-tuple-element.49.refs_0_, bf16[20,512,256]{2,1,0:T(8,128)(2,1)S(1)} %get-tuple-element.50.refs_1_, bf16[20,512,256]{2,1,0:T(8,128)(2,1)S(1)} %get-tuple-element.51.refs_2_, f32[40,1,128]{2,1,0:T(1,128)S(1)} %get-tuple-element.52.refs_3_, ...), custom_call_target="tpu_custom_call" | custom-call | flops 167772160 | bytes 20971520 | tf_op jit(solution)/shard_map/inner/pallas_call | solution.py:610
  23.0 0.0 collective-permute-done.4.refs_5_
  23.0 0.1 collective-permute-done.5.refs_6_
  23.1 1.9 %rest.5 = (f32[40,8,128]{2,1,0:T(8,128)S(1)}, f32[40,8,128]{2,1,0:T(8,128)S(1)}, f32[40,8,128]{2,1,0:T(8,128)S(1)}, f32[6,8,128]{2,1,0:T(8,128)S(1)}, f32[6,8,128]{2,1,0:T(8,128)S(1)}) custom-call(f32[3,40,1,128]{3,2,1,0:T(1,128)S(1)} %get-tuple-element.49.refs_0_, bf16[20,512,256]{2,1,0:T(8,128)(2,1)S(1)} %get-tuple-element.50.refs_1_, ...), custom_call_target="tpu_custom_call" | custom-call | flops 33554432 | bytes 4194304 | tf_op jit(solution)/shard_map/rest/pallas_call | solution.py:651
  25.0 0.4 collective-permute-start.6
  25.4 1.5 %collective-permute-start.7 = (f32[6,8,128]{2,1,0:T(8,128)S(1)}, f32[6,8,128]{2,1,0:T(8,128)S(1)}, u32[]{:S(2)}, u32[]{:S(2)}) collective-permute-start(f32[6,8,128]{2,1,0:T(8,128)S(1)} %get-tuple-element.75), channel_id=1, source_target_pairs={{1,2},{3,4},{5,6},{7,8},{9,10},{11,12},{13,14},{17,18},{19,20},{21... | collective-permute-start | bytes 73736 | tf_op jit(solution)/shard_map/ppermute | solution.py:578
  26.9 2.6 %inner.8 = (f32[40,8,128]{2,1,0:T(8,128)S(1)}, f32[40,8,128]{2,1,0:T(8,128)S(1)}, f32[40,8,128]{2,1,0:T(8,128)S(1)}) custom-call(f32[3,40,1,128]{3,2,1,0:T(1,128)S(1)} %get-tuple-element.49.refs_0_, bf16[20,512,256]{2,1,0:T(8,128)(2,1)S(1)} %get-tuple-element.50.refs_1_, bf16[20,512,256]{2,1,0:T(8,128)(2,1)S(1)} %get-tuple-element.51.refs_2_, ...), custom_call_target="tpu_custom_call" | custom-call | flops 167772160 | bytes 20971520 | tf_op jit(solution)/shard_map/inner/pallas_call | solution.py:610
  29.5 0.0 collective-permute-done.6.refs_5_
  29.5 0.0 collective-permute-done.7.refs_6_
  29.5 1.7 %rest.6 = (f32[40,8,128]{2,1,0:T(8,128)S(1)}, f32[40,8,128]{2,1,0:T(8,128)S(1)}, f32[40,8,128]{2,1,0:T(8,128)S(1)}, f32[6,8,128]{2,1,0:T(8,128)S(1)}, f32[6,8,128]{2,1,0:T(8,128)S(1)}) custom-call(f32[3,40,1,128]{3,2,1,0:T(1,128)S(1)} %get-tuple-element.49.refs_0_, bf16[20,512,256]{2,1,0:T(8,128)(2,1)S(1)} %get-tuple-element.50.refs_1_, ...), custom_call_target="tpu_custom_call" | custom-call | flops 33554432 | bytes 4194304 | tf_op jit(solution)/shard_map/rest/pallas_call | solution.py:651
  31.2 0.4 collective-permute-start.8
  31.7 1.5 %collective-permute-start.9 = (f32[6,8,128]{2,1,0:T(8,128)S(1)}, f32[6,8,128]{2,1,0:T(8,128)S(1)}, u32[]{:S(2)}, u32[]{:S(2)}) collective-permute-start(f32[6,8,128]{2,1,0:T(8,128)S(1)} %get-tuple-element.81), channel_id=1, source_target_pairs={{1,2},{3,4},{5,6},{7,8},{9,10},{11,12},{13,14},{17,18},{19,20},{21... | collective-permute-start | bytes 73736 | tf_op jit(solution)/shard_map/ppermute | solution.py:578
  33.2 3.7 %inner.9 = (f32[40,8,128]{2,1,0:T(8,128)S(1)}, f32[40,8,128]{2,1,0:T(8,128)S(1)}, f32[40,8,128]{2,1,0:T(8,128)S(1)}, f32[8,128]{1,0:T(8,128)S(1)}) custom-call(f32[3,40,1,128]{3,2,1,0:T(1,128)S(1)} %get-tuple-element.49.refs_0_, bf16[20,512,256]{2,1,0:T(8,128)(2,1)S(1)} %get-tuple-element.50.refs_1_, bf16[20,512,256]{2,1,0:T(8,128)(2,1)S(1)} %get-tuple-element.51.refs_2_, ...), custom_call_target="tpu_custom_call" | custom-call | flops 167772160 | bytes 20971520 | tf_op jit(solution)/shard_map/inner/pallas_call | solution.py:610
  36.8 0.0 collective-permute-done.8.refs_5_
  36.8 0.0 collective-permute-done.9.refs_6_
  36.8 1.4 %rest.7 = (f32[40,8,128]{2,1,0:T(8,128)S(1)}, f32[40,8,128]{2,1,0:T(8,128)S(1)}, f32[40,8,128]{2,1,0:T(8,128)S(1)}, f32[8,128]{1,0:T(8,128)S(1)}) custom-call(f32[3,40,1,128]{3,2,1,0:T(1,128)S(1)} %get-tuple-element.49.refs_0_, bf16[20,512,256]{2,1,0:T(8,128)(2,1)S(1)} %get-tuple-element.50.refs_1_, bf16[20,512,256]{2,1,0:T(8,128)(2,1)S(1)} %get-tuple-element.51.refs_2_, ...), custom_call_target="tpu_custom_call" | custom-call | flops 33554432 | bytes 4194304 | tf_op jit(solution)/shard_map/rest/pallas_call | solution.py:651
  38.3 0.4 collective-permute-start.10
  38.7 0.8 %collective-permute-done.10 = f32[8,128]{1,0:T(8,128)S(1)} collective-permute-done((f32[8,128]{1,0:T(8,128)S(1)}, f32[8,128]{1,0:T(8,128)S(1)}, u32[]{:S(2)}, u32[]{:S(2)}) %collective-permute-start.10) | collective-permute-done | bytes 4128 | tf_op jit(solution)/shard_map/ppermute | solution.py:686
  39.5 1.4 %collective-permute-start.11 = (f32[8,128]{1,0:T(8,128)S(1)}, f32[8,128]{1,0:T(8,128)S(1)}, u32[]{:S(2)}, u32[]{:S(2)}) collective-permute-start(f32[8,128]{1,0:T(8,128)S(1)} %add.12), channel_id=1, source_target_pairs={{0,3},{1,2},{2,1},{3,0},{4,7},{5,6},{6,5},{7,4},{8,11},{9,10},{10,... | collective-permute-start | bytes 12296 | tf_op jit(solution)/shard_map/ppermute | solution.py:686
  41.0 1.6 %collective-permute-done.11 = f32[8,128]{1,0:T(8,128)S(1)} collective-permute-done((f32[8,128]{1,0:T(8,128)S(1)}, f32[8,128]{1,0:T(8,128)S(1)}, u32[]{:S(2)}, u32[]{:S(2)}) %collective-permute-start.11) | collective-permute-done | bytes 4128 | tf_op jit(solution)/shard_map/ppermute | solution.py:686
  42.6 1.5 %collective-permute-start.12 = (f32[8,128]{1,0:T(8,128)S(1)}, f32[8,128]{1,0:T(8,128)S(1)}, u32[]{:S(2)}, u32[]{:S(2)}) collective-permute-start(f32[8,128]{1,0:T(8,128)S(1)} %add.13), channel_id=1, source_target_pairs={{0,5},{1,4},{2,7},{3,6},{4,1},{5,0},{6,3},{7,2},{8,13},{9,12},{10,... | collective-permute-start | bytes 12296 | tf_op jit(solution)/shard_map/ppermute | solution.py:686
  44.1 1.5 %collective-permute-done.12 = f32[8,128]{1,0:T(8,128)S(1)} collective-permute-done((f32[8,128]{1,0:T(8,128)S(1)}, f32[8,128]{1,0:T(8,128)S(1)}, u32[]{:S(2)}, u32[]{:S(2)}) %collective-permute-start.12) | collective-permute-done | bytes 4128 | tf_op jit(solution)/shard_map/ppermute | solution.py:686
  45.6 2.5 %collective-permute-start.13 = (f32[8,128]{1,0:T(8,128)S(1)}, f32[8,128]{1,0:T(8,128)S(1)}, u32[]{:S(2)}, u32[]{:S(2)}) collective-permute-start(f32[8,128]{1,0:T(8,128)S(1)} %add.14), channel_id=1, source_target_pairs={{0,9},{1,8},{2,11},{3,10},{4,13},{5,12},{6,15},{7,14},{8,1},{9,0},... | collective-permute-start | bytes 12296 | tf_op jit(solution)/shard_map/ppermute | solution.py:686
  48.1 1.4 %collective-permute-done.13 = f32[8,128]{1,0:T(8,128)S(1)} collective-permute-done((f32[8,128]{1,0:T(8,128)S(1)}, f32[8,128]{1,0:T(8,128)S(1)}, u32[]{:S(2)}, u32[]{:S(2)}) %collective-permute-start.13) | collective-permute-done | bytes 4128 | tf_op jit(solution)/shard_map/ppermute | solution.py:686
  49.5 1.3 %finish.1 = (f32[4,5120]{1,0:T(4,128)}, f32[4,5120]{1,0:T(4,128)}) custom-call(f32[8,128]{1,0:T(8,128)S(1)} %add.15.total_gram, f32[40,8,128]{2,1,0:T(8,128)S(1)} %get-tuple-element.53.refs_4_.refs_5_.refs_11_.refs_0_, f32[40,8,128]{2,1,0:T(8,128)S(1)} %get-tuple-element.82.refs_6_.refs_12_.refs_1_, ...), custom_call_target="tpu_custom_call" | custom-call | tf_op jit(solution)/shard_map/finish/pallas_call | solution.py:688
  (4 shorter events, 0.0 us)
Async XLA Ops:
  0.6 4.6 %copy-start = (f32[4,5120]{1,0:T(4,128)S(1)}, f32[4,5120]{1,0:T(4,128)}, u32[]{:S(2)}) copy-start(f32[4,5120]{1,0:T(4,128)} %refs_1_.1) | copy-start | bytes 245764
  0.6 4.6 %copy-start.1 = (f32[5120]{0:T(1024)S(1)}, f32[5120]{0:T(1024)}, u32[]{:S(2)}) copy-start(f32[5120]{0:T(1024)} %param.6) | copy-start | bytes 61444
  0.7 4.6 %copy-start.2 = (s32[40,4]{0,1:T(4,128)S(1)}, s32[40,4]{0,1:T(4,128)}, u32[]{:S(2)}) copy-start(s32[40,4]{0,1:T(4,128)} %param.5) | copy-start | bytes 1924
  2.1 14.8 %collective-permute-start.2 = (f32[904,128]{1,0:T(8,128)S(1)}, f32[904,128]{1,0:T(8,128)S(1)}, u32[]{:S(2)}, u32[]{:S(2)}) collective-permute-start(f32[904,128]{1,0:T(8,128)S(1)} %get-tuple-element.59), channel_id=1, source_target_pairs={{0,1},{1,0},{2,3},{3,2},{4,5},{5,4},{6,7},{7,6},{8,9},{9,8},{10,11... | collective-permute-start | bytes 1388552 | tf_op jit(solution)/shard_map/ppermute | solution.py:579
  2.7 14.3 %collective-permute-start.3 = (f32[904,128]{1,0:T(8,128)S(1)}, f32[904,128]{1,0:T(8,128)S(1)}, u32[]{:S(2)}, u32[]{:S(2)}) collective-permute-start(f32[904,128]{1,0:T(8,128)S(1)} %get-tuple-element.60), channel_id=1, source_target_pairs={{1,2},{3,4},{5,6},{7,8},{9,10},{11,12},{13,14},{17,18},{19,20},{21... | collective-permute-start | bytes 1388552 | tf_op jit(solution)/shard_map/ppermute | solution.py:578
  12.9 3.9 %collective-permute-start = (f32[6,8,128]{2,1,0:T(8,128)S(1)}, f32[6,8,128]{2,1,0:T(8,128)S(1)}, u32[]{:S(2)}, u32[]{:S(2)}) collective-permute-start(f32[6,8,128]{2,1,0:T(8,128)S(1)} %get-tuple-element.54), channel_id=1, source_target_pairs={{0,1},{1,0},{2,3},{3,2},{4,5},{5,4},{6,7},{7,6},{8,9},{9,8},{10,11... | collective-permute-start | bytes 73736 | tf_op jit(solution)/shard_map/ppermute | solution.py:579
  13.2 3.8 %collective-permute-start.1 = (f32[6,8,128]{2,1,0:T(8,128)S(1)}, f32[6,8,128]{2,1,0:T(8,128)S(1)}, u32[]{:S(2)}, u32[]{:S(2)}) collective-permute-start(f32[6,8,128]{2,1,0:T(8,128)S(1)} %get-tuple-element.55), channel_id=1, source_target_pairs={{1,2},{3,4},{5,6},{7,8},{9,10},{11,12},{13,14},{17,18},{19,20},{21... | collective-permute-start | bytes 73736 | tf_op jit(solution)/shard_map/ppermute | solution.py:578
  19.2 3.9 %collective-permute-start.4 = (f32[6,8,128]{2,1,0:T(8,128)S(1)}, f32[6,8,128]{2,1,0:T(8,128)S(1)}, u32[]{:S(2)}, u32[]{:S(2)}) collective-permute-start(f32[6,8,128]{2,1,0:T(8,128)S(1)} %get-tuple-element.63), channel_id=1, source_target_pairs={{0,1},{1,0},{2,3},{3,2},{4,5},{5,4},{6,7},{7,6},{8,9},{9,8},{10,11... | collective-permute-start | bytes 73736 | tf_op jit(solution)/shard_map/ppermute | solution.py:579
  19.3 3.8 %collective-permute-start.5 = (f32[6,8,128]{2,1,0:T(8,128)S(1)}, f32[6,8,128]{2,1,0:T(8,128)S(1)}, u32[]{:S(2)}, u32[]{:S(2)}) collective-permute-start(f32[6,8,128]{2,1,0:T(8,128)S(1)} %get-tuple-element.64), channel_id=1, source_target_pairs={{1,2},{3,4},{5,6},{7,8},{9,10},{11,12},{13,14},{17,18},{19,20},{21... | collective-permute-start | bytes 73736 | tf_op jit(solution)/shard_map/ppermute | solution.py:578
  25.0 4.5 %collective-permute-start.6 = (f32[6,8,128]{2,1,0:T(8,128)S(1)}, f32[6,8,128]{2,1,0:T(8,128)S(1)}, u32[]{:S(2)}, u32[]{:S(2)}) collective-permute-start(f32[6,8,128]{2,1,0:T(8,128)S(1)} %get-tuple-element.74), channel_id=1, source_target_pairs={{0,1},{1,0},{2,3},{3,2},{4,5},{5,4},{6,7},{7,6},{8,9},{9,8},{10,11... | collective-permute-start | bytes 73736 | tf_op jit(solution)/shard_map/ppermute | solution.py:579
  25.4 4.1 %collective-permute-start.7 = (f32[6,8,128]{2,1,0:T(8,128)S(1)}, f32[6,8,128]{2,1,0:T(8,128)S(1)}, u32[]{:S(2)}, u32[]{:S(2)}) collective-permute-start(f32[6,8,128]{2,1,0:T(8,128)S(1)} %get-tuple-element.75), channel_id=1, source_target_pairs={{1,2},{3,4},{5,6},{7,8},{9,10},{11,12},{13,14},{17,18},{19,20},{21... | collective-permute-start | bytes 73736 | tf_op jit(solution)/shard_map/ppermute | solution.py:578
  31.2 5.6 %collective-permute-start.8 = (f32[6,8,128]{2,1,0:T(8,128)S(1)}, f32[6,8,128]{2,1,0:T(8,128)S(1)}, u32[]{:S(2)}, u32[]{:S(2)}) collective-permute-start(f32[6,8,128]{2,1,0:T(8,128)S(1)} %get-tuple-element.80), channel_id=1, source_target_pairs={{0,1},{1,0},{2,3},{3,2},{4,5},{5,4},{6,7},{7,6},{8,9},{9,8},{10,11... | collective-permute-start | bytes 73736 | tf_op jit(solution)/shard_map/ppermute | solution.py:579
  31.7 5.2 %collective-permute-start.9 = (f32[6,8,128]{2,1,0:T(8,128)S(1)}, f32[6,8,128]{2,1,0:T(8,128)S(1)}, u32[]{:S(2)}, u32[]{:S(2)}) collective-permute-start(f32[6,8,128]{2,1,0:T(8,128)S(1)} %get-tuple-element.81), channel_id=1, source_target_pairs={{1,2},{3,4},{5,6},{7,8},{9,10},{11,12},{13,14},{17,18},{19,20},{21... | collective-permute-start | bytes 73736 | tf_op jit(solution)/shard_map/ppermute | solution.py:578
  38.3 1.2 %collective-permute-start.10 = (f32[8,128]{1,0:T(8,128)S(1)}, f32[8,128]{1,0:T(8,128)S(1)}, u32[]{:S(2)}, u32[]{:S(2)}) collective-permute-start(f32[8,128]{1,0:T(8,128)S(1)} %get-tuple-element.92), channel_id=1, source_target_pairs={{0,1},{1,0},{2,3},{3,2},{4,5},{5,4},{6,7},{7,6},{8,9},{9,8},{10,11... | collective-permute-start | bytes 12296 | tf_op jit(solution)/shard_map/ppermute | solution.py:686
  39.5 3.0 %collective-permute-start.11 = (f32[8,128]{1,0:T(8,128)S(1)}, f32[8,128]{1,0:T(8,128)S(1)}, u32[]{:S(2)}, u32[]{:S(2)}) collective-permute-start(f32[8,128]{1,0:T(8,128)S(1)} %add.12), channel_id=1, source_target_pairs={{0,3},{1,2},{2,1},{3,0},{4,7},{5,6},{6,5},{7,4},{8,11},{9,10},{10,... | collective-permute-start | bytes 12296 | tf_op jit(solution)/shard_map/ppermute | solution.py:686
  42.6 3.0 %collective-permute-start.12 = (f32[8,128]{1,0:T(8,128)S(1)}, f32[8,128]{1,0:T(8,128)S(1)}, u32[]{:S(2)}, u32[]{:S(2)}) collective-permute-start(f32[8,128]{1,0:T(8,128)S(1)} %add.13), channel_id=1, source_target_pairs={{0,5},{1,4},{2,7},{3,6},{4,1},{5,0},{6,3},{7,2},{8,13},{9,12},{10,... | collective-permute-start | bytes 12296 | tf_op jit(solution)/shard_map/ppermute | solution.py:686
  45.6 3.9 %collective-permute-start.13 = (f32[8,128]{1,0:T(8,128)S(1)}, f32[8,128]{1,0:T(8,128)S(1)}, u32[]{:S(2)}, u32[]{:S(2)}) collective-permute-start(f32[8,128]{1,0:T(8,128)S(1)} %add.14), channel_id=1, source_target_pairs={{0,9},{1,8},{2,11},{3,10},{4,13},{5,12},{6,15},{7,14},{8,1},{9,0},... | collective-permute-start | bytes 12296 | tf_op jit(solution)/shard_map/ppermute | solution.py:686
